TPU v7x, 32 devices: a whole 2x2x4 slice. The times are simulated.
32 devices in a mesh: view: 4 (over y, x), band: 8 (over z, core).
Axes of the slice: x: 2, y: 2, z: 4, core: 2. Of those that a mesh axis runs over, the one named last changes fastest.
Arguments:
- features: float32 [4, 64, 512, 128], P('view', 'band'), may hold values from -6 to 6
- tempers: float32 [4, 64, 512], P('view', 'band'), may hold values from 0.5 to 80
- partners: int32 [4, 2], replicated, may hold values from 0 to 3, as said below
- conv_one: bfloat16 [3, 3, 128, 128], replicated, may hold values from -0.1875 to 0.1875
- conv_two: bfloat16 [3, 3, 128, 128], replicated, may hold values from -0.1875 to 0.1875
- query_weight: bfloat16 [128, 128], replicated, may hold values from -0.5 to 0.5
- key_weight: bfloat16 [128, 128], replicated, may hold values from -0.5 to 0.5
- value_weight: bfloat16 [128, 128], replicated, may hold values from -0.5 to 0.5
- out_weight: bfloat16 [128, 128], replicated, may hold values from -0.5 to 0.5
- norm_gain: float32 [128], replicated, may hold values from 0.25 to 1.75
- message_gain: float32 [128], replicated, may hold values from 0.25 to 1.75
Outputs:
- refined: float32 [4, 64, 512, 128], P('view', 'band')
Inputs may be any that keep to these rules, and one draw needn't show every extreme that they name: Column 0 and column 1 are each a permutation of the 4 views; a view is never its own partner, and its two partners differ. At least one view has as its first partner the view 4 positions away from it (modulo 4).
All inputs are finite; a program needn't handle non-finite values.
Results may differ from a plain program's by a relative error of at most 0.0065.
Values may be sent and summed in bfloat16 or wider, within the bound.
No kernel may reach another device: no remote copies, remote signals or barrier semaphores. Data moves between devices by JAX's collectives and lax.ppermute only.
A program may use at most 64 MiB of HBM per device.

v0:
```python
import math

import jax
import jax.numpy as jnp
from jax import lax
from jax.sharding import PartitionSpec as P

epsilon = 1e-06


def extended(cells, sides, width):
    for axis, dim in sides:
        count = lax.axis_size(axis)
        ends = count - 1
        head = lax.slice_in_dim(cells, 0, width, axis=dim)
        tail = lax.slice_in_dim(cells, cells.shape[dim] - width, cells.shape[dim], axis=dim)
        cells = jnp.concatenate(
            [
                lax.ppermute(tail, axis, [(i, (i + 1) % count) for i in range(ends)]),
                cells,
                lax.ppermute(head, axis, [((i + 1) % count, i) for i in range(ends)]),
            ],
            axis=dim,
        )
    return cells


def root_norm(values, gain):
    mean_square = jnp.mean(values * values, axis=-1, keepdims=True)
    return values * lax.rsqrt(mean_square + epsilon) * gain


def convolve(padded, kernel):
    leading = padded.shape[:-3]
    out_rows = padded.shape[-3] - 2
    columns = padded.shape[-2]
    channels = padded.shape[-1]
    widened = jnp.pad(padded, [(0, 0)] * len(leading) + [(0, 0), (1, 1), (0, 0)])
    summed = jnp.zeros(leading + (out_rows, columns, kernel.shape[-1]), jnp.float32)
    for row_tap in range(3):
        for col_tap in range(3):
            window = widened[..., row_tap : row_tap + out_rows, col_tap : col_tap + columns, :]
            product = jnp.dot(
                window.reshape(-1, channels),
                kernel[row_tap, col_tap],
                preferred_element_type=jnp.float32,
            )
            summed = summed + product.reshape(summed.shape)
    return summed


def route_pair(normed_rows, partners):
    held = lax.all_to_all(normed_rows[None], "view", split_axis=2, concat_axis=0, tiled=True)
    outgoing = jnp.take(held, partners, axis=0)
    returned = lax.all_to_all(outgoing, "view", split_axis=0, concat_axis=3, tiled=True)
    return returned[0]


def per_device(
    features,
    tempers,
    partners,
    conv_one,
    conv_two,
    query_weight,
    key_weight,
    value_weight,
    out_weight,
    norm_gain,
    message_gain,
):
    current = features[0]
    temper = tempers[0]
    row_count, columns, channels = current.shape
    first_input = jax.nn.silu(current).astype(jnp.bfloat16)
    first_rows = extended(first_input, (("band", 0),), 1)
    state_one = current + convolve(first_rows, conv_one)
    second_input = jax.nn.silu(state_one).astype(jnp.bfloat16)
    second_rows = extended(second_input, (("band", 0),), 1)
    state_two = state_one + convolve(second_rows, conv_two)
    normed = root_norm(state_two, norm_gain).astype(jnp.bfloat16)
    flat_normed = normed.reshape(-1, channels)
    queries = (
        jnp.dot(flat_normed, query_weight, preferred_element_type=jnp.float32)
        .astype(jnp.bfloat16)
        .reshape(normed.shape)
    )
    paired = route_pair(normed, partners)
    paired_rows = extended(paired, (("band", 1),), 1)
    pair_flat = paired_rows.reshape(-1, channels)
    key_rows = (
        jnp.dot(pair_flat, key_weight, preferred_element_type=jnp.float32)
        .astype(jnp.bfloat16)
        .reshape(paired_rows.shape)
    )
    value_rows = (
        jnp.dot(pair_flat, value_weight, preferred_element_type=jnp.float32)
        .astype(jnp.bfloat16)
        .reshape(paired_rows.shape)
    )
    block_size = min(columns, 512)
    factor = 1.0 / math.sqrt(channels)

    def attend_row(row_index):
        query_row = lax.dynamic_index_in_dim(queries, row_index, 0, keepdims=False)
        temper_row = lax.dynamic_index_in_dim(temper, row_index, 0, keepdims=False) * factor
        key_window = lax.dynamic_slice_in_dim(key_rows, row_index, 3, 1).reshape(
            2, 3 * columns, channels
        )
        value_window = lax.dynamic_slice_in_dim(value_rows, row_index, 3, 1).reshape(
            2, 3 * columns, channels
        )
        summed = jnp.zeros((columns, channels), jnp.float32)
        for partner in range(2):
            scores = lax.dot_general(
                query_row,
                key_window[partner],
                (((1,), (1,)), ((), ())),
                preferred_element_type=jnp.float32,
            )
            scores = scores * temper_row[0:block_size, None]
            row_peak = jnp.max(scores, axis=-1, keepdims=True)
            lifted = jnp.exp(scores - row_peak)
            shares = (lifted / jnp.sum(lifted, axis=-1, keepdims=True)).astype(jnp.bfloat16)
            pieces = [
                jnp.dot(shares, value_window[partner], preferred_element_type=jnp.float32).astype(
                    jnp.bfloat16
                )
            ]
            blended = jnp.concatenate(pieces, axis=0)
            summed = summed + jnp.dot(blended, out_weight, preferred_element_type=jnp.float32)
        return summed

    messages = lax.map(attend_row, jnp.arange(row_count, dtype=jnp.int32))
    refined = state_two + root_norm(messages, message_gain)
    return refined[None]


def solution(mesh):
    in_specs = (
        P("view", "band", None, None),
        P("view", "band", None),
        P(),
        P(),
        P(),
        P(),
        P(),
        P(),
        P(),
        P(),
        P(),
    )
    out_specs = P("view", "band", None, None)
    return jax.shard_map(
        per_device, mesh=mesh, in_specs=in_specs, out_specs=out_specs, check_vma=False
    )
```

profile of v0, /device:TPU:1, one launch (start us, length us, event | category | flops | bytes accessed | tf_op | source)
XLA Modules:
  0.0 244.1 jit_solution(6281866245228158784)
XLA Ops:
  0.0 2.3 fusion.19
  2.3 4.6 %collective-permute-start = (bf16[1,512,128]{2,1,0:T(8,128)(2,1)S(1)}, bf16[1,512,128]{2,1,0:T(8,128)(2,1)S(1)}, u32[]{:S(2)}, u32[]{:S(2)}) collective-permute-start(bf16[1,512,128]{2,1,0:T(8,128)(2,1)S(1)} %get-tuple-element.78), channel_id=1, source_target_pairs={{0,1},{1,2},{2,3},{3,4},{4,5},{5,6},{6,7},{8,9},{9,10},{10,11},{11... | collective-permute-start | bytes 393224 | tf_op jit(solution)/shard_map/ppermute | solution.py:19
  6.9 1.9 collective-permute-start.1
  9.6 3.6 %collective-permute-done.1 = bf16[1,512,128]{2,1,0:T(8,128)(2,1)S(1)} collective-permute-done((bf16[1,512,128]{2,1,0:T(8,128)(2,1)S(1)}, bf16[1,512,128]{2,1,0:T(8,128)(2,1)S(1)}, u32[]{:S(2)}, u32[]{:S(2)}) %collective-permute-start.1) | collective-permute-done | bytes 131104 | tf_op jit(solution)/shard_map/ppermute | solution.py:21
  18.0 1.9 collective-permute-start.2
  19.9 2.4 collective-permute-start.3
  22.7 3.4 %collective-permute-done.3 = bf16[1,512,128]{2,1,0:T(8,128)(2,1)S(1)} collective-permute-done((bf16[1,512,128]{2,1,0:T(8,128)(2,1)S(1)}, bf16[1,512,128]{2,1,0:T(8,128)(2,1)S(1)}, u32[]{:S(2)}, u32[]{:S(2)}) %collective-permute-start.3) | collective-permute-done | bytes 131104 | tf_op jit(solution)/shard_map/ppermute | solution.py:21
  31.6 1.7 copy.27
  33.3 3.5 %all-to-all-start = ((bf16[1,8,512,128]{3,1,0,2:T(8,128)(2,1)}), bf16[1,8,512,128]{3,1,0,2:T(8,128)(2,1)S(1)}, u32[]{:S(2)}, u32[]{:S(2)}) async-start(bf16[1,8,512,128]{3,1,0,2:T(8,128)(2,1)} %copy.27), calls=%async_computation | async-start | bytes 2097152 | tf_op jit(solution)/shard_map/all_to_all | solution.py:53
  37.1 11.7 %all-to-all-done = bf16[1,8,512,128]{3,1,0,2:T(8,128)(2,1)S(1)} async-done(((bf16[1,8,512,128]{3,1,0,2:T(8,128)(2,1)}), bf16[1,8,512,128]{3,1,0,2:T(8,128)(2,1)S(1)}, u32[]{:S(2)}, u32[]{:S(2)}) %all-to-all-start) | async-done | bytes 1048608 | tf_op jit(solution)/shard_map/all_to_all | solution.py:53
  51.2 2.1 gather_fusion
  53.4 3.2 %broadcast_select_fusion = bf16[4,2,8,128,128]{4,3,2,1,0:T(8,128)(2,1)} fusion(bf16[4,2,8,128,128]{4,3,2,1,0:T(8,128)(2,1)} %bitcast.203, pred[4,2]{1,0:T(4,128)(4,1)S(1)} %copy.26), kind=kLoop, calls=%fused_computation.49 | loop fusion | flops 1048576 | bytes 4194312 | tf_op jit(solution)/shard_map/jit(_take)/select_n | solution.py:54
  56.6 4.6 %all-to-all-start.1 = ((bf16[4,2,8,128,128]{4,3,2,1,0:T(8,128)(2,1)}), bf16[4,2,8,128,128]{4,3,2,1,0:T(8,128)(2,1)}, u32[]{:S(2)}, u32[]{:S(2)}) async-start(bf16[4,2,8,128,128]{4,3,2,1,0:T(8,128)(2,1)} %broadcast_select_fusion), calls=%async_computation.1 | async-start | bytes 4194304 | tf_op jit(solution)/shard_map/all_to_all | solution.py:55
  62.0 24.5 %all-to-all-done.1 = bf16[4,2,8,128,128]{4,3,2,1,0:T(8,128)(2,1)} async-done(((bf16[4,2,8,128,128]{4,3,2,1,0:T(8,128)(2,1)}), bf16[4,2,8,128,128]{4,3,2,1,0:T(8,128)(2,1)}, u32[]{:S(2)}, u32[]{:S(2)}) %all-to-all-start.1) | async-done | bytes 2097184 | tf_op jit(solution)/shard_map/all_to_all | solution.py:55
  86.5 1.7 copy.31
  88.3 4.8 %collective-permute-start.4 = (bf16[2,1,512,128]{3,2,1,0:T(8,128)(2,1)S(1)}, bf16[2,1,512,128]{3,2,1,0:T(8,128)(2,1)S(1)}, u32[]{:S(2)}, u32[]{:S(2)}) collective-permute-start(bf16[2,1,512,128]{3,2,1,0:T(8,128)(2,1)S(1)} %get-tuple-element.74), channel_id=1, source_target_pairs={{0,1},{1,2},{2,3},{3,4},{4,5},{5,6},{6,7},{8,9},{9,10},{10,11},{11... | collective-permute-start | bytes 786440 | tf_op jit(solution)/shard_map/ppermute | solution.py:19
  93.0 1.9 collective-permute-start.5
  96.4 4.3 %collective-permute-done.5 = bf16[2,1,512,128]{3,2,1,0:T(8,128)(2,1)S(1)} collective-permute-done((bf16[2,1,512,128]{3,2,1,0:T(8,128)(2,1)S(1)}, bf16[2,1,512,128]{3,2,1,0:T(8,128)(2,1)S(1)}, u32[]{:S(2)}, u32[]{:S(2)}) %collective-permute-start.5) | collective-permute-done | bytes 262176 | tf_op jit(solution)/shard_map/ppermute | solution.py:21
  101.1 2.3 convolution_convert_fusion
  103.4 2.3 convolution_convert_fusion.1
  105.8 133.0 %while.10 = (s32[]{:T(128)}, f32[8,512,128]{2,1,0:T(8,128)}, s32[8]{0:T(128)S(1)}, bf16[8,512,128]{2,1,0:T(8,128)(2,1)}, bf16[2,10,512,128]{3,2,1,0:T(8,128)(2,1...) while((s32[]{:T(128)}, f32[8,512,128]{2,1,0:T(8,128)}, ...), condition=%wide.region_6.7_spmd, body=%wide.region_1.6_spmd.sunk | while | flops 850065920 | bytes 26308876 | solution.py:134
  110.2 2.4 constant_dynamic-slice_fusion.5
  114.8 2.5 %fusion.148 = f32[512,128]{1,0:T(8,128)} fusion(bf16[128,128]{1,0:T(8,128)(2,1)} %get-tuple-element.182, bf16[1536,128]{1,0:T(8,128)(2,1)} %bitcast.201, f32[512,1536]{1,0:T(8,128)S(1)} %get-tuple-element.143, f32[512]{0:T(512)S(1)} %fusion.147, f32[512]{0:T(512)S(1)} %get-tuple-element.144), kind=kOutput, calls=%fused_computation.16.clone.1 | convolution fusion | flops 220528640 | bytes 3837952 | tf_op jit(solution)/shard_map/while/body/eval_jaxpr/dot_general | solution.py:131
  119.9 2.5 %fusion.151 = f32[8,512,128]{2,1,0:T(8,128)} fusion(f32[8,512,128]{2,1,0:T(8,128)} %get-tuple-element.163, s32[]{:T(128)S(6)} %copy.39, f32[512,128]{1,0:T(8,128)} %fusion.148, bf16[128,128]{1,0:T(8,128)(2,1)} %get-tuple-element.182, bf16[1536,128]{1,0:T(8,128)(2,1)S(1)} %bitcast.200, f32[512,1536]{1,0:T(8,128)S(1)} %get-tuple-element.147, ...), kind=kOutput, calls=%fused_computation.13.clone.1 | convolution fusion | flops 220594176 | bytes 4100100 | tf_op jit(solution)/shard_map/while/body/eval_jaxpr/dot_general | solution.py:131
  126.8 2.4 constant_dynamic-slice_fusion.5
  131.4 2.5 %fusion.148 = f32[512,128]{1,0:T(8,128)} fusion(bf16[128,128]{1,0:T(8,128)(2,1)} %get-tuple-element.182, bf16[1536,128]{1,0:T(8,128)(2,1)} %bitcast.201, f32[512,1536]{1,0:T(8,128)S(1)} %get-tuple-element.143, f32[512]{0:T(512)S(1)} %fusion.147, f32[512]{0:T(512)S(1)} %get-tuple-element.144), kind=kOutput, calls=%fused_computation.16.clone.1 | convolution fusion | flops 220528640 | bytes 3837952 | tf_op jit(solution)/shard_map/while/body/eval_jaxpr/dot_general | solution.py:131
  136.5 2.5 %fusion.151 = f32[8,512,128]{2,1,0:T(8,128)} fusion(f32[8,512,128]{2,1,0:T(8,128)} %get-tuple-element.163, s32[]{:T(128)S(6)} %copy.39, f32[512,128]{1,0:T(8,128)} %fusion.148, bf16[128,128]{1,0:T(8,128)(2,1)} %get-tuple-element.182, bf16[1536,128]{1,0:T(8,128)(2,1)S(1)} %bitcast.200, f32[512,1536]{1,0:T(8,128)S(1)} %get-tuple-element.147, ...), kind=kOutput, calls=%fused_computation.13.clone.1 | convolution fusion | flops 220594176 | bytes 4100100 | tf_op jit(solution)/shard_map/while/body/eval_jaxpr/dot_general | solution.py:131
  143.5 2.4 constant_dynamic-slice_fusion.5
  145.9 1.6 fusion.146
  148.0 2.5 %fusion.148 = f32[512,128]{1,0:T(8,128)} fusion(bf16[128,128]{1,0:T(8,128)(2,1)} %get-tuple-element.182, bf16[1536,128]{1,0:T(8,128)(2,1)} %bitcast.201, f32[512,1536]{1,0:T(8,128)S(1)} %get-tuple-element.143, f32[512]{0:T(512)S(1)} %fusion.147, f32[512]{0:T(512)S(1)} %get-tuple-element.144), kind=kOutput, calls=%fused_computation.16.clone.1 | convolution fusion | flops 220528640 | bytes 3837952 | tf_op jit(solution)/shard_map/while/body/eval_jaxpr/dot_general | solution.py:131
  153.1 2.5 %fusion.151 = f32[8,512,128]{2,1,0:T(8,128)} fusion(f32[8,512,128]{2,1,0:T(8,128)} %get-tuple-element.163, s32[]{:T(128)S(6)} %copy.39, f32[512,128]{1,0:T(8,128)} %fusion.148, bf16[128,128]{1,0:T(8,128)(2,1)} %get-tuple-element.182, bf16[1536,128]{1,0:T(8,128)(2,1)S(1)} %bitcast.200, f32[512,1536]{1,0:T(8,128)S(1)} %get-tuple-element.147, ...), kind=kOutput, calls=%fused_computation.13.clone.1 | convolution fusion | flops 220594176 | bytes 4100100 | tf_op jit(solution)/shard_map/while/body/eval_jaxpr/dot_general | solution.py:131
  160.1 2.4 constant_dynamic-slice_fusion.5
  164.6 2.5 %fusion.148 = f32[512,128]{1,0:T(8,128)} fusion(bf16[128,128]{1,0:T(8,128)(2,1)} %get-tuple-element.182, bf16[1536,128]{1,0:T(8,128)(2,1)} %bitcast.201, f32[512,1536]{1,0:T(8,128)S(1)} %get-tuple-element.143, f32[512]{0:T(512)S(1)} %fusion.147, f32[512]{0:T(512)S(1)} %get-tuple-element.144), kind=kOutput, calls=%fused_computation.16.clone.1 | convolution fusion | flops 220528640 | bytes 3837952 | tf_op jit(solution)/shard_map/while/body/eval_jaxpr/dot_general | solution.py:131
  169.8 2.5 %fusion.151 = f32[8,512,128]{2,1,0:T(8,128)} fusion(f32[8,512,128]{2,1,0:T(8,128)} %get-tuple-element.163, s32[]{:T(128)S(6)} %copy.39, f32[512,128]{1,0:T(8,128)} %fusion.148, bf16[128,128]{1,0:T(8,128)(2,1)} %get-tuple-element.182, bf16[1536,128]{1,0:T(8,128)(2,1)S(1)} %bitcast.200, f32[512,1536]{1,0:T(8,128)S(1)} %get-tuple-element.147, ...), kind=kOutput, calls=%fused_computation.13.clone.1 | convolution fusion | flops 220594176 | bytes 4100100 | tf_op jit(solution)/shard_map/while/body/eval_jaxpr/dot_general | solution.py:131
  176.7 2.4 constant_dynamic-slice_fusion.5
  181.3 2.5 %fusion.148 = f32[512,128]{1,0:T(8,128)} fusion(bf16[128,128]{1,0:T(8,128)(2,1)} %get-tuple-element.182, bf16[1536,128]{1,0:T(8,128)(2,1)} %bitcast.201, f32[512,1536]{1,0:T(8,128)S(1)} %get-tuple-element.143, f32[512]{0:T(512)S(1)} %fusion.147, f32[512]{0:T(512)S(1)} %get-tuple-element.144), kind=kOutput, calls=%fused_computation.16.clone.1 | convolution fusion | flops 220528640 | bytes 3837952 | tf_op jit(solution)/shard_map/while/body/eval_jaxpr/dot_general | solution.py:131
  186.4 2.5 %fusion.151 = f32[8,512,128]{2,1,0:T(8,128)} fusion(f32[8,512,128]{2,1,0:T(8,128)} %get-tuple-element.163, s32[]{:T(128)S(6)} %copy.39, f32[512,128]{1,0:T(8,128)} %fusion.148, bf16[128,128]{1,0:T(8,128)(2,1)} %get-tuple-element.182, bf16[1536,128]{1,0:T(8,128)(2,1)S(1)} %bitcast.200, f32[512,1536]{1,0:T(8,128)S(1)} %get-tuple-element.147, ...), kind=kOutput, calls=%fused_computation.13.clone.1 | convolution fusion | flops 220594176 | bytes 4100100 | tf_op jit(solution)/shard_map/while/body/eval_jaxpr/dot_general | solution.py:131
  193.3 2.4 constant_dynamic-slice_fusion.5
  197.9 2.5 %fusion.148 = f32[512,128]{1,0:T(8,128)} fusion(bf16[128,128]{1,0:T(8,128)(2,1)} %get-tuple-element.182, bf16[1536,128]{1,0:T(8,128)(2,1)} %bitcast.201, f32[512,1536]{1,0:T(8,128)S(1)} %get-tuple-element.143, f32[512]{0:T(512)S(1)} %fusion.147, f32[512]{0:T(512)S(1)} %get-tuple-element.144), kind=kOutput, calls=%fused_computation.16.clone.1 | convolution fusion | flops 220528640 | bytes 3837952 | tf_op jit(solution)/shard_map/while/body/eval_jaxpr/dot_general | solution.py:131
  203.0 2.5 %fusion.151 = f32[8,512,128]{2,1,0:T(8,128)} fusion(f32[8,512,128]{2,1,0:T(8,128)} %get-tuple-element.163, s32[]{:T(128)S(6)} %copy.39, f32[512,128]{1,0:T(8,128)} %fusion.148, bf16[128,128]{1,0:T(8,128)(2,1)} %get-tuple-element.182, bf16[1536,128]{1,0:T(8,128)(2,1)S(1)} %bitcast.200, f32[512,1536]{1,0:T(8,128)S(1)} %get-tuple-element.147, ...), kind=kOutput, calls=%fused_computation.13.clone.1 | convolution fusion | flops 220594176 | bytes 4100100 | tf_op jit(solution)/shard_map/while/body/eval_jaxpr/dot_general | solution.py:131
  210.0 2.4 constant_dynamic-slice_fusion.5
  214.5 2.5 %fusion.148 = f32[512,128]{1,0:T(8,128)} fusion(bf16[128,128]{1,0:T(8,128)(2,1)} %get-tuple-element.182, bf16[1536,128]{1,0:T(8,128)(2,1)} %bitcast.201, f32[512,1536]{1,0:T(8,128)S(1)} %get-tuple-element.143, f32[512]{0:T(512)S(1)} %fusion.147, f32[512]{0:T(512)S(1)} %get-tuple-element.144), kind=kOutput, calls=%fused_computation.16.clone.1 | convolution fusion | flops 220528640 | bytes 3837952 | tf_op jit(solution)/shard_map/while/body/eval_jaxpr/dot_general | solution.py:131
  219.6 2.5 %fusion.151 = f32[8,512,128]{2,1,0:T(8,128)} fusion(f32[8,512,128]{2,1,0:T(8,128)} %get-tuple-element.163, s32[]{:T(128)S(6)} %copy.39, f32[512,128]{1,0:T(8,128)} %fusion.148, bf16[128,128]{1,0:T(8,128)(2,1)} %get-tuple-element.182, bf16[1536,128]{1,0:T(8,128)(2,1)S(1)} %bitcast.200, f32[512,1536]{1,0:T(8,128)S(1)} %get-tuple-element.147, ...), kind=kOutput, calls=%fused_computation.13.clone.1 | convolution fusion | flops 220594176 | bytes 4100100 | tf_op jit(solution)/shard_map/while/body/eval_jaxpr/dot_general | solution.py:131
  226.6 2.4 constant_dynamic-slice_fusion.5
  231.1 2.5 %fusion.148 = f32[512,128]{1,0:T(8,128)} fusion(bf16[128,128]{1,0:T(8,128)(2,1)} %get-tuple-element.182, bf16[1536,128]{1,0:T(8,128)(2,1)} %bitcast.201, f32[512,1536]{1,0:T(8,128)S(1)} %get-tuple-element.143, f32[512]{0:T(512)S(1)} %fusion.147, f32[512]{0:T(512)S(1)} %get-tuple-element.144), kind=kOutput, calls=%fused_computation.16.clone.1 | convolution fusion | flops 220528640 | bytes 3837952 | tf_op jit(solution)/shard_map/while/body/eval_jaxpr/dot_general | solution.py:131
  236.3 2.5 %fusion.151 = f32[8,512,128]{2,1,0:T(8,128)} fusion(f32[8,512,128]{2,1,0:T(8,128)} %get-tuple-element.163, s32[]{:T(128)S(6)} %copy.39, f32[512,128]{1,0:T(8,128)} %fusion.148, bf16[128,128]{1,0:T(8,128)(2,1)} %get-tuple-element.182, bf16[1536,128]{1,0:T(8,128)(2,1)S(1)} %bitcast.200, f32[512,1536]{1,0:T(8,128)S(1)} %get-tuple-element.147, ...), kind=kOutput, calls=%fused_computation.13.clone.1 | convolution fusion | flops 220594176 | bytes 4100100 | tf_op jit(solution)/shard_map/while/body/eval_jaxpr/dot_general | solution.py:131
  238.8 2.4 multiply_reduce_fusion
  241.2 2.9 %add_bitcast_fusion = f32[1,8,512,128]{3,2,1,0:T(8,128)} fusion(f32[8,512,128]{2,1,0:T(8,128)S(1)} %copy-done.3, f32[8,512,128]{2,1,0:T(8,128)} %get-tuple-element.47, f32[128]{0:T(128)S(1)} %copy-done.13, f32[8,512]{1,0:T(8,128)S(1)} %add_rsqrt_fusion), kind=kLoop, calls=%fused_computation.41 | loop fusion | flops 1572864 | bytes 6308352 | tf_op jit(solution)/shard_map/broadcast_in_dim | solution.py:136
  (130 shorter events, 63.2 us)
Async XLA Ops:
  0.0 101.1 %copy-start = (bf16[128,128]{1,0:T(8,128)(2,1)S(1)}, bf16[128,128]{1,0:T(8,128)(2,1)}, u32[]{:S(2)}) copy-start(bf16[128,128]{1,0:T(8,128)(2,1)} %param.20) | copy-start | bytes 98308
  0.0 8.9 %copy-start.5 = (f32[1,8,512,128]{3,2,1,0:T(8,128)S(1)}, f32[1,8,512,128]{3,2,1,0:T(8,128)}, u32[]{:S(2)}) copy-start(f32[1,8,512,128]{3,2,1,0:T(8,128)} %param.13) | copy-start | bytes 6291460
  0.0 8.9 %copy-start.8 = (bf16[3,3,128,128]{3,2,1,0:T(8,128)(2,1)S(1)}, bf16[3,3,128,128]{3,2,1,0:T(8,128)(2,1)}, u32[]{:S(2)}) copy-start(bf16[3,3,128,128]{3,2,1,0:T(8,128)(2,1)} %param.16) | copy-start | bytes 884740
  2.3 7.2 %collective-permute-start = (bf16[1,512,128]{2,1,0:T(8,128)(2,1)S(1)}, bf16[1,512,128]{2,1,0:T(8,128)(2,1)S(1)}, u32[]{:S(2)}, u32[]{:S(2)}) collective-permute-start(bf16[1,512,128]{2,1,0:T(8,128)(2,1)S(1)} %get-tuple-element.78), channel_id=1, source_target_pairs={{0,1},{1,2},{2,3},{3,4},{4,5},{5,6},{6,7},{8,9},{9,10},{10,11},{11... | collective-permute-start | bytes 393224 | tf_op jit(solution)/shard_map/ppermute | solution.py:19
  6.9 6.3 %collective-permute-start.1 = (bf16[1,512,128]{2,1,0:T(8,128)(2,1)S(1)}, bf16[1,512,128]{2,1,0:T(8,128)(2,1)S(1)}, u32[]{:S(2)}, u32[]{:S(2)}) collective-permute-start(bf16[1,512,128]{2,1,0:T(8,128)(2,1)S(1)} %get-tuple-element.79), channel_id=1, source_target_pairs={{1,0},{2,1},{3,2},{4,3},{5,4},{6,5},{7,6},{9,8},{10,9},{11,10},{12... | collective-permute-start | bytes 393224 | tf_op jit(solution)/shard_map/ppermute | solution.py:21
  16.5 5.8 %copy-start.7 = (bf16[3,3,128,128]{3,2,1,0:T(8,128)(2,1)S(1)}, bf16[3,3,128,128]{3,2,1,0:T(8,128)(2,1)}, u32[]{:S(2)}) copy-start(bf16[3,3,128,128]{3,2,1,0:T(8,128)(2,1)} %param.17) | copy-start | bytes 884740
  18.0 4.8 %collective-permute-start.2 = (bf16[1,512,128]{2,1,0:T(8,128)(2,1)S(1)}, bf16[1,512,128]{2,1,0:T(8,128)(2,1)S(1)}, u32[]{:S(2)}, u32[]{:S(2)}) collective-permute-start(bf16[1,512,128]{2,1,0:T(8,128)(2,1)S(1)} %get-tuple-element.76), channel_id=1, source_target_pairs={{0,1},{1,2},{2,3},{3,4},{4,5},{5,6},{6,7},{8,9},{9,10},{10,11},{11... | collective-permute-start | bytes 393224 | tf_op jit(solution)/shard_map/ppermute | solution.py:19
  19.9 6.3 %collective-permute-start.3 = (bf16[1,512,128]{2,1,0:T(8,128)(2,1)S(1)}, bf16[1,512,128]{2,1,0:T(8,128)(2,1)S(1)}, u32[]{:S(2)}, u32[]{:S(2)}) collective-permute-start(bf16[1,512,128]{2,1,0:T(8,128)(2,1)S(1)} %get-tuple-element.77), channel_id=1, source_target_pairs={{1,0},{2,1},{3,2},{4,3},{5,4},{6,5},{7,6},{9,8},{10,9},{11,10},{12... | collective-permute-start | bytes 393224 | tf_op jit(solution)/shard_map/ppermute | solution.py:21
  29.5 1.4 copy-start.11
  30.8 30.4 %copy-start.2 = (f32[8,512,128]{2,1,0:T(8,128)}, f32[8,512,128]{2,1,0:T(8,128)S(1)}, u32[]{:S(2)}) copy-start(f32[8,512,128]{2,1,0:T(8,128)S(1)} %get-tuple-element.83) | copy-start | bytes 6291460
  31.6 5.2 %copy-start.12 = (s32[4,2]{0,1:T(2,128)S(1)}, s32[4,2]{0,1:T(2,128)}, u32[]{:S(2)}) copy-start(s32[4,2]{0,1:T(2,128)} %param.15) | copy-start | bytes 100
  33.3 15.5 %all-to-all-start = ((bf16[1,8,512,128]{3,1,0,2:T(8,128)(2,1)}), bf16[1,8,512,128]{3,1,0,2:T(8,128)(2,1)S(1)}, u32[]{:S(2)}, u32[]{:S(2)}) async-start(bf16[1,8,512,128]{3,1,0,2:T(8,128)(2,1)} %copy.27), calls=%async_computation | async-start | bytes 2097152 | tf_op jit(solution)/shard_map/all_to_all | solution.py:53
  48.8 1.0 copy-start.6
  56.6 29.9 %all-to-all-start.1 = ((bf16[4,2,8,128,128]{4,3,2,1,0:T(8,128)(2,1)}), bf16[4,2,8,128,128]{4,3,2,1,0:T(8,128)(2,1)}, u32[]{:S(2)}, u32[]{:S(2)}) async-start(bf16[4,2,8,128,128]{4,3,2,1,0:T(8,128)(2,1)} %broadcast_select_fusion), calls=%async_computation.1 | async-start | bytes 4194304 | tf_op jit(solution)/shard_map/all_to_all | solution.py:55
  86.5 8.5 %copy-start.9 = (bf16[128,128]{1,0:T(8,128)(2,1)S(1)}, bf16[128,128]{1,0:T(8,128)(2,1)}, u32[]{:S(2)}) copy-start(bf16[128,128]{1,0:T(8,128)(2,1)} %param.18) | copy-start | bytes 98308
  88.3 8.2 %collective-permute-start.4 = (bf16[2,1,512,128]{3,2,1,0:T(8,128)(2,1)S(1)}, bf16[2,1,512,128]{3,2,1,0:T(8,128)(2,1)S(1)}, u32[]{:S(2)}, u32[]{:S(2)}) collective-permute-start(bf16[2,1,512,128]{3,2,1,0:T(8,128)(2,1)S(1)} %get-tuple-element.74), channel_id=1, source_target_pairs={{0,1},{1,2},{2,3},{3,4},{4,5},{5,6},{6,7},{8,9},{9,10},{10,11},{11... | collective-permute-start | bytes 786440 | tf_op jit(solution)/shard_map/ppermute | solution.py:19
  93.0 7.7 %collective-permute-start.5 = (bf16[2,1,512,128]{3,2,1,0:T(8,128)(2,1)S(1)}, bf16[2,1,512,128]{3,2,1,0:T(8,128)(2,1)S(1)}, u32[]{:S(2)}, u32[]{:S(2)}) collective-permute-start(bf16[2,1,512,128]{3,2,1,0:T(8,128)(2,1)S(1)} %get-tuple-element.75), channel_id=1, source_target_pairs={{1,0},{2,1},{3,2},{4,3},{5,4},{6,5},{7,6},{9,8},{10,9},{11,10},{12... | collective-permute-start | bytes 786440 | tf_op jit(solution)/shard_map/ppermute | solution.py:21
  101.1 2.4 copy-start.10
  118.9 1.0 copy-start.4
  135.5 1.0 copy-start.4
  152.1 1.0 copy-start.4
  168.8 1.0 copy-start.4
  185.4 1.0 copy-start.4
  202.0 1.0 copy-start.4
  218.6 1.0 copy-start.4
  235.3 1.0 copy-start.4
  238.8 2.4 copy-start.3
  238.8 2.4 copy-start.13
  241.1 3.0 %copy-start.1 = (bf16[128,128]{1,0:T(8,128)(2,1)S(1)}, bf16[128,128]{1,0:T(8,128)(2,1)}, u32[]{:S(2)}) copy-start(bf16[128,128]{1,0:T(8,128)(2,1)} %param.20) | copy-start | bytes 98308
where the time goes:
time: 247 us; the launch traced here: 244 us
  matrix products  81.3 us (33%)
  waiting for transfers between devices  47.6 us (19%)
  local copies, waits for them, and re-layouts  36 us (15%)
  other arithmetic  28.2 us (11%)
  starting transfers between devices  25.7 us (10%)
  loops' own time  24.9 us (10%)
    dot_general x16, matrix products, attend_row(): jnp.dot(blended, out_weight, preferred_element_type=jnp.float32)  40.4 us
    dot_general x16, matrix products, attend_row(): lax.dot_general(query_row, key_window[partner], (((1,), (1,)), ((), ())),...  25.1 us
    another operation x1, loops' own time, per_device(): messages = lax.map(attend_row, jnp.arange(row_count, dtype=jnp.int32))  24.9 us
    all_to_all x1, waiting for transfers between devices, route_pair(): lax.all_to_all(outgoing, 'view', split_axis=0, concat_axis=3, tiled=True)  24.5 us
    slice x8, local copies, waits for them, and re-layouts, attend_row(): value_window[partner]  19.4 us
    all_to_all x1, waiting for transfers between devices, route_pair(): lax.all_to_all(normed_rows[None], 'view', split_axis=2, concat_axis=0, ti...  11.7 us
    ppermute x3, waiting for transfers between devices, extended(): lax.ppermute(head, axis, [((i + 1) % count, i) for i in range(ends)])  11.4 us
    ppermute x3, starting transfers between devices, extended(): lax.ppermute(tail, axis, [(i, (i + 1) % count) for i in range(ends)])  11.3 us
  transfers between devices with their start and end apart: 8, of which 5 were waited for; matrix products, arithmetic and copies ran while one was open for 1% of the time, Pallas kernels for 0%

commit v1 on v0

v1 whole, which is shorter than its diff:
```python
import functools
import math

import jax
import jax.numpy as jnp
from jax import lax
from jax.experimental import pallas as pl
from jax.experimental.pallas import tpu as pltpu
from jax.sharding import PartitionSpec as P

epsilon = 1e-06
vmem_bytes = 56 * 1024 * 1024


def pair_weights(kernel):
    taps, _, channels, out_channels = kernel.shape
    zero = jnp.zeros_like(kernel[:1])
    first = jnp.concatenate([kernel, zero], axis=0)
    second = jnp.concatenate([zero, kernel], axis=0)
    both = jnp.stack([first, second], axis=3)
    return both.reshape((taps + 1) * taps * channels, 2 * out_channels)


def silu(v):
    return v / (1.0 + jnp.exp(-v))


def spread(value, pad, out):
    columns = value.shape[0]
    pad[8 : 8 + columns] = value
    left = pad[7 : 7 + columns]
    right = pad[9 : 9 + columns]
    out[...] = jnp.concatenate([left, value, right], axis=-1).astype(jnp.bfloat16)


def row_pair(x_ref, first, weights):
    lhs = jnp.concatenate([x_ref[first + j] for j in range(4)], axis=-1)
    return jnp.dot(lhs, weights[...], preferred_element_type=jnp.float32)


def residual_body(
    flags, cells, above, below, weights_one, weights_two, gain, tempers, mixing,
    state_out, edge_out, middle_out, query_out, pad, x_one, x_two, state_one,
):
    rows, columns, channels = cells.shape
    zeros = jnp.zeros((8, channels), jnp.float32)
    for slot in range(2):
        pad[slot, 0:8] = zeros
        pad[slot, 8 + columns : 16 + columns] = zeros
    for r in range(rows + 4):
        if r < 2:
            value = above[r].astype(jnp.float32)
        elif r < rows + 2:
            value = cells[r - 2]
        else:
            value = below[r - rows - 2].astype(jnp.float32)
        spread(silu(value), pad.at[r % 2], x_one.at[r])
    for first in range(0, rows + 2, 2):
        out = row_pair(x_one, first, weights_one)
        for o in range(2):
            r = first + o
            if r == 0:
                state = above[1].astype(jnp.float32) + out[:, :channels]
            elif r == rows + 1:
                state = below[0].astype(jnp.float32) + out[:, channels:]
            else:
                state = cells[r - 1] + out[:, o * channels : (o + 1) * channels]
                state_one[r - 1] = state
            lifted = silu(state)
            if r == 0:
                lifted = jnp.where(flags[0] > 0, lifted, 0.0)
            elif r == rows + 1:
                lifted = jnp.where(flags[1] > 0, lifted, 0.0)
            spread(lifted, pad.at[o], x_two.at[r])
    quarter = rows // 4
    for first in range(0, rows, 2):
        out = row_pair(x_two, first, weights_two)
        for o in range(2):
            r = first + o
            state = state_one[r] + out[:, o * channels : (o + 1) * channels]
            state_out[r] = state
            scale = lax.rsqrt(jnp.mean(state * state, axis=-1, keepdims=True) + epsilon)
            normed = (state * scale * gain[...]).astype(jnp.bfloat16)
            if r < quarter:
                edge_out[r] = normed
            elif r >= rows - quarter:
                edge_out[r - rows + 2 * quarter] = normed
            else:
                middle_out[r - quarter] = normed
            query = jnp.dot(normed, mixing[...], preferred_element_type=jnp.float32)
            query_out[r] = (query * tempers[:, r : r + 1]).astype(jnp.bfloat16)


def residual_step(flags, cells, above, below, weights_one, weights_two, gain, tempers, mixing):
    rows, columns, channels = cells.shape
    whole = pl.BlockSpec(memory_space=pltpu.VMEM)
    half = rows // 4 * 2
    return pl.pallas_call(
        residual_body,
        in_specs=[pl.BlockSpec(memory_space=pltpu.SMEM)] + [whole] * 8,
        out_specs=[whole] * 4,
        out_shape=[
            jax.ShapeDtypeStruct(cells.shape, jnp.float32),
            jax.ShapeDtypeStruct((half, columns, channels), jnp.bfloat16),
            jax.ShapeDtypeStruct((rows - half, columns, channels), jnp.bfloat16),
            jax.ShapeDtypeStruct(cells.shape, jnp.bfloat16),
        ],
        scratch_shapes=[
            pltpu.VMEM((2, columns + 16, channels), jnp.float32),
            pltpu.VMEM((rows + 4, columns, 3 * channels), jnp.bfloat16),
            pltpu.VMEM((rows + 2, columns, 3 * channels), jnp.bfloat16),
            pltpu.VMEM(cells.shape, jnp.float32),
        ],
        compiler_params=pltpu.CompilerParams(vmem_limit_bytes=vmem_bytes),
        name="residual_convolutions",
    )(flags, cells, above, below, weights_one, weights_two, gain, tempers, mixing)


def blend(query, window, store):
    keys, channels = window.shape
    extended = jnp.concatenate([window, jnp.ones((keys, channels), jnp.bfloat16)], axis=1)
    columns = query.shape[0]
    block = 128 if columns % 128 == 0 else columns
    for start in range(0, columns, block):
        scores = lax.dot_general(
            query[start : start + block],
            window,
            (((1,), (1,)), ((), ())),
            preferred_element_type=jnp.float32,
        )
        peak = jnp.max(scores, axis=-1, keepdims=True)
        lifted = jnp.exp2(scores - peak).astype(jnp.bfloat16)
        total = jnp.dot(lifted, extended, preferred_element_type=jnp.float32)
        store(start, block, total[:, :channels] / total[:, channels:])


def attend_near_body(query, keys, out):
    row = pl.program_id(0)
    columns, channels = query.shape[1:]
    window = keys[pl.ds(row, 3)].reshape(3 * columns, channels)

    def store(start, block, value):
        out[0, start : start + block] = value

    blend(query[0], window, store)


def attend_far_body(query, keys, near, state, value_out, gain, out):
    row = pl.program_id(0)
    columns, channels = query.shape[1:]
    window = keys[pl.ds(row, 3)].reshape(3 * columns, channels)

    def store(start, block, value):
        both = (value + near[0, start : start + block]).astype(jnp.bfloat16)
        message = jnp.dot(both, value_out[...], preferred_element_type=jnp.float32)
        scale = lax.rsqrt(jnp.mean(message * message, axis=-1, keepdims=True) + epsilon)
        out[0, start : start + block] = state[0, start : start + block] + message * scale * gain[...]

    blend(query[0], window, store)


def attend(body, name, query, keys, *rest):
    rows, columns, channels = query.shape
    row_spec = pl.BlockSpec((1, columns, channels), lambda i: (i, 0, 0))
    whole = pl.BlockSpec(memory_space=pltpu.VMEM)
    rest_specs = [row_spec if a.ndim == 3 else whole for a in rest]
    return pl.pallas_call(
        body,
        grid=(rows,),
        in_specs=[row_spec, whole] + rest_specs,
        out_specs=row_spec,
        out_shape=jax.ShapeDtypeStruct(query.shape, jnp.float32),
        compiler_params=pltpu.CompilerParams(vmem_limit_bytes=vmem_bytes),
        name=name,
    )(query, keys, *rest)


def swap(cells, views, offset):
    return lax.ppermute(cells, "view", [(i, i ^ offset) for i in range(views)])


def gather_views(cells, views):
    half = cells.shape[0] // 2
    held = {}
    for offset in range(1, views):
        low = offset & -offset
        high = 1 << (offset.bit_length() - 1)
        if low == high:
            held[offset] = swap(cells, views, offset)
        else:
            first = swap(held[offset ^ low][:half], views, low)
            second = swap(held[offset ^ high][half:], views, high)
            held[offset] = jnp.concatenate([first, second], axis=0)
    return held


def choose(held, offset, low, high):
    picked = held[low]
    for candidate in range(low + 1, high + 1):
        picked = jnp.where(offset == candidate, held[candidate], picked)
    return picked


def per_device(
    features, tempers, partners, conv_one, conv_two, query_weight, key_weight,
    value_weight, out_weight, norm_gain, message_gain,
):
    views = lax.axis_size("view")
    bands = lax.axis_size("band")
    band = lax.axis_index("band")
    view = lax.axis_index("view")
    cells = features[0]
    rows, columns, channels = cells.shape
    upward = [(i + 1, i) for i in range(bands - 1)]
    downward = [(i, i + 1) for i in range(bands - 1)]

    above = lax.ppermute(cells[rows - 2 :].astype(jnp.bfloat16), "band", downward)
    below = lax.ppermute(cells[:2].astype(jnp.bfloat16), "band", upward)
    flags = jnp.stack([band > 0, band < bands - 1]).astype(jnp.int32)
    factor = math.log2(math.e) / math.sqrt(channels)
    columns_tempers = tempers[0].T * factor
    mixing = lax.dot_general(
        query_weight, key_weight, (((1,), (1,)), ((), ())), preferred_element_type=jnp.float32
    ).astype(jnp.bfloat16)
    value_out = jnp.dot(value_weight, out_weight, preferred_element_type=jnp.float32).astype(
        jnp.bfloat16
    )
    state_two, edge, middle, queries = residual_step(
        flags, cells, above, below, pair_weights(conv_one), pair_weights(conv_two),
        norm_gain[None], columns_tempers, mixing,
    )
    edges = gather_views(edge, views)
    middles = gather_views(middle, views)

    offsets = jnp.bitwise_xor(lax.dynamic_index_in_dim(partners, view, 0, keepdims=False), view)
    near, far = jnp.min(offsets), jnp.max(offsets)
    bounds = ((near, 1, max(1, views - 2)), (far, min(2, views - 1), views - 1))
    half = edge.shape[0] // 2
    picked_edges = [choose(edges, *bound) for bound in bounds]
    picked_middles = [choose(middles, *bound) for bound in bounds]
    heads = jnp.stack([e[:1] for e in picked_edges])
    tails = jnp.stack([e[-1:] for e in picked_edges])
    from_above = lax.ppermute(tails, "band", downward)
    from_below = lax.ppermute(heads, "band", upward)
    keys = [
        jnp.concatenate(
            [from_above[i], picked_edges[i][:half], picked_middles[i], picked_edges[i][half:],
             from_below[i]], axis=0,
        )
        for i in range(2)
    ]
    near_blend = attend(attend_near_body, "attend_near", queries, keys[0])
    refined = attend(
        attend_far_body, "attend_far", queries, keys[1], near_blend, state_two, value_out,
        message_gain[None],
    )
    return refined[None]


def solution(mesh):
    whole = P()
    in_specs = (P("view", "band", None, None), P("view", "band", None)) + (whole,) * 9
    return jax.shard_map(
        per_device, mesh=mesh, in_specs=in_specs,
        out_specs=P("view", "band", None, None), check_vma=False,
    )
```

time: 247 us -> 112 us (0.45)
  matrix products: 81.3 us -> 1.52 us
  Pallas kernels: 0 us -> 51.6 us
  local copies, waits for them, and re-layouts: 36 us -> 5.68 us
  waiting for transfers between devices: 47.6 us -> 21.3 us
  loops' own time: 24.9 us -> 0 us
  other arithmetic: 28.2 us -> 4.6 us
    dot_general x53 -> x2, matrix products: 81.3 us -> 1.52 us  [the longest x1 0.77 us: per_device(): lax.dot_general(query_weight, key_weight, (((1,), (1,)), ((), ())), prefe...]
    pallas_call x0 -> x3, Pallas kernels: none -> 51.6 us  [the longest x2 39.7 us: attend(): pl.pallas_call(body, grid=(rows,), in_specs=[row_spec, whole] + rest_spec...]
    all_to_all x2 -> x0, waiting for transfers between devices: 36.2 us -> none  [the longest x1 24.5 us: route_pair(): lax.all_to_all(outgoing, 'view', split_axis=0, concat_axis=3, tiled=True)]
    another operation x1 -> x0, loops' own time: 24.9 us -> none  [per_device(): messages = lax.map(attend_row, jnp.arange(row_count, dtype=jnp.int32))]
    slice x11 -> x4, local copies, waits for them, and re-layouts: 19.4 us -> 0.07 us  [the longest x2 0.04 us: gather_views(): first = swap(held[offset ^ low][:half], views, low)]
    reduce_sum x17 -> x0, other arithmetic: 11.4 us -> none  [the longest x16 9.08 us: attend_row(): jnp.sum(lifted, axis=-1, keepdims=True)]
    ppermute x6 -> x12, waiting for transfers between devices: 11.4 us -> 21.3 us  [the longest x8 19 us: swap(): return lax.ppermute(cells, 'view', [(i, i ^ offset) for i in range(views)])]
    all_to_all x2 -> x0, starting transfers between devices: 8.15 us -> none  [the longest x1 4.64 us: route_pair(): lax.all_to_all(outgoing, 'view', split_axis=0, concat_axis=3, tiled=True)]
  transfers between devices with their start and end apart: 8 -> 12, of which waited for: 5 -> 8; matrix products, arithmetic and copies ran while one was open for 1% -> 7% of each run, Pallas kernels for 0% -> 0%
where the time goes in v1:
time: 112 us; the launch traced here: 111 us
  Pallas kernels  51.6 us (46%)
  starting transfers between devices  24.9 us (22%)
  waiting for transfers between devices  21.3 us (19%)
  local copies, waits for them, and re-layouts  5.68 us (5%)
  other arithmetic  4.6 us (4%)
  between operations  1.67 us (1%)
  matrix products  1.52 us (1%)
    pallas_call x2, Pallas kernels, attend(): pl.pallas_call(body, grid=(rows,), in_specs=[row_spec, whole] + rest_spec...  39.7 us
    ppermute x8, waiting for transfers between devices, swap(): return lax.ppermute(cells, 'view', [(i, i ^ offset) for i in range(views)])  19 us
    pallas_call x1, Pallas kernels, residual_step(): pl.pallas_call(residual_body, in_specs=[pl.BlockSpec(memory_space=pltpu.S...  11.9 us
    ppermute x8, starting transfers between devices, swap(): return lax.ppermute(cells, 'view', [(i, i ^ offset) for i in range(views)])  10 us
    ppermute x1, starting transfers between devices, per_device(): from_above = lax.ppermute(tails, 'band', downward)  5.63 us
    ppermute x1, starting transfers between devices, per_device(): lax.ppermute(cells[rows - 2:].astype(jnp.bfloat16), 'band', downward)  4.59 us
    ppermute x1, starting transfers between devices, per_device(): from_below = lax.ppermute(heads, 'band', upward)  2.76 us
    ppermute x1, waiting for transfers between devices, per_device(): from_below = lax.ppermute(heads, 'band', upward)  2.31 us
  transfers between devices with their start and end apart: 12, of which 8 were waited for; matrix products, arithmetic and copies ran while one was open for 7% of the time, Pallas kernels for 0%

profile of v1, /device:TPU:1, one launch (start us, length us, event | category | flops | bytes accessed | tf_op | source)
XLA Modules:
  0.0 111.4 jit_solution(375154907985607281)
XLA Ops:
  0.0 1.8 %convert.4 = bf16[1,8,512,128]{3,2,1,0:T(8,128)(2,1)S(1)} convert(f32[1,8,512,128]{3,2,1,0:T(8,128)} %param.11) | non-fusion elementwise | flops 524288 | bytes 3145728 | tf_op jit(solution)/shard_map/convert.1
  1.9 4.6 %collective-permute-start = (bf16[2,512,128]{2,1,0:T(8,128)(2,1)S(1)}, bf16[2,512,128]{2,1,0:T(8,128)(2,1)S(1)}, u32[]{:S(2)}, u32[]{:S(2)}) collective-permute-start(bf16[2,512,128]{2,1,0:T(8,128)(2,1)S(1)} %get-tuple-element.16), channel_id=1, source_target_pairs={{0,1},{1,2},{2,3},{3,4},{4,5},{5,6},{6,7},{8,9},{9,10},{10,11},{11... | collective-permute-start | bytes 786440 | tf_op jit(solution)/shard_map/ppermute | solution.py:217
  6.5 1.9 %collective-permute-start.1 = (bf16[2,512,128]{2,1,0:T(8,128)(2,1)S(1)}, bf16[2,512,128]{2,1,0:T(8,128)(2,1)S(1)}, u32[]{:S(2)}, u32[]{:S(2)}) collective-permute-start(bf16[2,512,128]{2,1,0:T(8,128)(2,1)S(1)} %get-tuple-element.15), channel_id=1, source_target_pairs={{1,0},{2,1},{3,2},{4,3},{5,4},{6,5},{7,6},{9,8},{10,9},{11,10},{12... | collective-permute-start | bytes 786440 | tf_op jit(solution)/shard_map/ppermute | solution.py:218
  8.4 0.1 pad_bitcast_fusion.3
  8.5 0.0 copy-start.4
  8.6 0.1 pad_maximum_fusion
  8.6 0.8 copy.12
  9.5 0.1 copy-done.4
  9.5 0.1 pad_bitcast_fusion.1
  9.7 0.1 pad_maximum_fusion.1
  9.7 0.8 copy.13
  10.6 0.0 copy-start.7
  10.6 0.0 copy-start.10
  10.6 1.4 %copy_bitcast_fusion = (bf16[1536,256]{1,0:T(8,128)(2,1)}, bf16[1536,256]{1,0:T(8,128)(2,1)}) fusion(bf16[192,8,2,128]{3,2,1,0:T(2,128)(2,1)S(1)} %bitcast.60, bf16[192,8,2,128]{3,2,1,0:T(2,128)(2,1)S(1)} %bitcast.59), kind=kLoop, calls=%fused_computation.2 | loop fusion | bytes 3145728 | tf_op jit(solution)/shard_map/reshape | solution.py:21
  12.0 0.8 convolution_convert_fusion.1.mixing
  12.8 0.7 add_convert_fusion.flags
  13.4 0.1 copy.14
  13.5 0.8 multiply_bitcast_fusion.tempers
  14.3 0.7 copy-done.5
  15.0 0.1 copy-done.6
  15.1 11.9 %residual_convolutions.1 = (f32[8,512,128]{2,1,0:T(8,128)}, bf16[4,512,128]{2,1,0:T(8,128)(2,1)}, bf16[4,512,128]{2,1,0:T(8,128)(2,1)}, bf16[8,512,128]{2,1,0:T(8,128)(2,1)}) custom-call(s32[2]{0:T(128)} %add_convert_fusion.flags, f32[8,512,128]{2,1,0:T(8,128)} %bitcast.58, bf16[2,512,128]{2,1,0:T(8,128)(2,1)} %copy-done.5, bf16[2,512,128]{2,1,0:T(8,128)(2,1)} %copy-done.6, ...), custom_call_target="tpu_custom_call" | custom-call | tf_op jit(solution)/shard_map/residual_convolutions/pallas_call | solution.py:98
  27.0 1.2 %collective-permute-start.2 = (bf16[4,512,128]{2,1,0:T(8,128)(2,1)}, bf16[4,512,128]{2,1,0:T(8,128)(2,1)S(1)}, u32[]{:S(2)}, u32[]{:S(2)}) collective-permute-start(bf16[4,512,128]{2,1,0:T(8,128)(2,1)} %get-tuple-element.10), channel_id=1, source_target_pairs={{0,16},{8,24},{16,0},{24,8},{1,17},{9,25},{17,1},{25,9},{2,18},{10... | collective-permute-start | bytes 1572872 | tf_op jit(solution)/shard_map/ppermute | solution.py:179
  28.2 1.2 %collective-permute-start.3 = (bf16[4,512,128]{2,1,0:T(8,128)(2,1)}, bf16[4,512,128]{2,1,0:T(8,128)(2,1)S(1)}, u32[]{:S(2)}, u32[]{:S(2)}) collective-permute-start(bf16[4,512,128]{2,1,0:T(8,128)(2,1)} %get-tuple-element.10), channel_id=1, source_target_pairs={{0,8},{8,0},{16,24},{24,16},{1,9},{9,1},{17,25},{25,17},{2,10},{10... | collective-permute-start | bytes 1572872 | tf_op jit(solution)/shard_map/ppermute | solution.py:179
  29.4 9.7 %collective-permute-done.2 = bf16[4,512,128]{2,1,0:T(8,128)(2,1)S(1)} collective-permute-done((bf16[4,512,128]{2,1,0:T(8,128)(2,1)}, bf16[4,512,128]{2,1,0:T(8,128)(2,1)S(1)}, u32[]{:S(2)}, u32[]{:S(2)}) %collective-permute-start.2) | collective-permute-done | bytes 524320 | tf_op jit(solution)/shard_map/ppermute | solution.py:179
  39.2 1.8 %collective-permute-start.4 = (bf16[2,512,128]{2,1,0:T(8,128)(2,1)S(1)}, bf16[2,512,128]{2,1,0:T(8,128)(2,1)S(1)}, u32[]{:S(2)}, u32[]{:S(2)}) collective-permute-start(bf16[2,512,128]{2,1,0:T(8,128)(2,1)S(1)} %slice.79), channel_id=1, source_target_pairs={{0,8},{8,0},{16,24},{24,16},{1,9},{9,1},{17,25},{25,17},{2,10},{10... | collective-permute-start | bytes 786440 | tf_op jit(solution)/shard_map/ppermute | solution.py:179
  41.0 1.0 collective-permute-start.5
  42.0 0.8 fusion.6
  44.1 0.5 collective-permute-start.9
  44.6 1.2 %collective-permute-start.7 = (bf16[4,512,128]{2,1,0:T(8,128)(2,1)}, bf16[4,512,128]{2,1,0:T(8,128)(2,1)S(1)}, u32[]{:S(2)}, u32[]{:S(2)}) collective-permute-start(bf16[4,512,128]{2,1,0:T(8,128)(2,1)} %get-tuple-element.11), channel_id=1, source_target_pairs={{0,16},{8,24},{16,0},{24,8},{1,17},{9,25},{17,1},{25,9},{2,18},{10... | collective-permute-start | bytes 1572872 | tf_op jit(solution)/shard_map/ppermute | solution.py:179
  45.8 1.2 %collective-permute-done.4 = bf16[2,512,128]{2,1,0:T(8,128)(2,1)S(1)} collective-permute-done((bf16[2,512,128]{2,1,0:T(8,128)(2,1)S(1)}, bf16[2,512,128]{2,1,0:T(8,128)(2,1)S(1)}, u32[]{:S(2)}, u32[]{:S(2)}) %collective-permute-start.4) | collective-permute-done | bytes 262176 | tf_op jit(solution)/shard_map/ppermute | solution.py:179
  47.0 2.3 %collective-permute-done.5 = bf16[2,512,128]{2,1,0:T(8,128)(2,1)S(1)} collective-permute-done((bf16[2,512,128]{2,1,0:T(8,128)(2,1)S(1)}, bf16[2,512,128]{2,1,0:T(8,128)(2,1)S(1)}, u32[]{:S(2)}, u32[]{:S(2)}) %collective-permute-start.5) | collective-permute-done | bytes 262176 | tf_op jit(solution)/shard_map/ppermute | solution.py:179
  49.4 0.1 broadcast_select_fusion
  49.5 0.0 copy-start.8
  49.6 5.6 %collective-permute-start.6 = (bf16[2,1,512,128]{3,2,1,0:T(8,128)(2,1)S(1)}, bf16[2,1,512,128]{3,2,1,0:T(8,128)(2,1)S(1)}, u32[]{:S(2)}, u32[]{:S(2)}) collective-permute-start(bf16[2,1,512,128]{3,2,1,0:T(8,128)(2,1)S(1)} %pad_maximum_fusion.2), channel_id=1, source_target_pairs={{0,1},{1,2},{2,3},{3,4},{4,5},{5,6},{6,7},{8,9},{9,10},{10,11},{11... | collective-permute-start | bytes 786440 | tf_op jit(solution)/shard_map/ppermute | solution.py:243
  55.2 0.8 convolution_convert_fusion.value_out
  56.0 2.2 %collective-permute-done.9 = bf16[4,512,128]{2,1,0:T(8,128)(2,1)S(1)} collective-permute-done((bf16[4,512,128]{2,1,0:T(8,128)(2,1)}, bf16[4,512,128]{2,1,0:T(8,128)(2,1)S(1)}, u32[]{:S(2)}, u32[]{:S(2)}) %collective-permute-start.9) | collective-permute-done | bytes 524320 | tf_op jit(solution)/shard_map/ppermute | solution.py:179
  58.2 1.7 %collective-permute-start.10 = (bf16[2,512,128]{2,1,0:T(8,128)(2,1)S(1)}, bf16[2,512,128]{2,1,0:T(8,128)(2,1)S(1)}, u32[]{:S(2)}, u32[]{:S(2)}) collective-permute-start(bf16[2,512,128]{2,1,0:T(8,128)(2,1)S(1)} %slice.85), channel_id=1, source_target_pairs={{0,16},{8,24},{16,0},{24,8},{1,17},{9,25},{17,1},{25,9},{2,18},{10... | collective-permute-start | bytes 786440 | tf_op jit(solution)/shard_map/ppermute | solution.py:179
  59.9 0.3 collective-permute-done.7
  60.3 1.4 %collective-permute-start.8 = (bf16[2,512,128]{2,1,0:T(8,128)(2,1)S(1)}, bf16[2,512,128]{2,1,0:T(8,128)(2,1)S(1)}, u32[]{:S(2)}, u32[]{:S(2)}) collective-permute-start(bf16[2,512,128]{2,1,0:T(8,128)(2,1)S(1)} %slice.84), channel_id=1, source_target_pairs={{0,8},{8,0},{16,24},{24,16},{1,9},{9,1},{17,25},{25,17},{2,10},{10... | collective-permute-start | bytes 786440 | tf_op jit(solution)/shard_map/ppermute | solution.py:179
  61.6 2.8 %collective-permute-start.11 = (bf16[2,1,512,128]{3,2,1,0:T(8,128)(2,1)S(1)}, bf16[2,1,512,128]{3,2,1,0:T(8,128)(2,1)S(1)}, u32[]{:S(2)}, u32[]{:S(2)}) collective-permute-start(bf16[2,1,512,128]{3,2,1,0:T(8,128)(2,1)S(1)} %pad_maximum_fusion.3), channel_id=1, source_target_pairs={{1,0},{2,1},{3,2},{4,3},{5,4},{6,5},{7,6},{9,8},{10,9},{11,10},{12... | collective-permute-start | bytes 786440 | tf_op jit(solution)/shard_map/ppermute | solution.py:244
  64.5 1.4 %collective-permute-done.10 = bf16[2,512,128]{2,1,0:T(8,128)(2,1)S(1)} collective-permute-done((bf16[2,512,128]{2,1,0:T(8,128)(2,1)S(1)}, bf16[2,512,128]{2,1,0:T(8,128)(2,1)S(1)}, u32[]{:S(2)}, u32[]{:S(2)}) %collective-permute-start.10) | collective-permute-done | bytes 262176 | tf_op jit(solution)/shard_map/ppermute | solution.py:179
  66.0 1.8 %collective-permute-done.8 = bf16[2,512,128]{2,1,0:T(8,128)(2,1)S(1)} collective-permute-done((bf16[2,512,128]{2,1,0:T(8,128)(2,1)S(1)}, bf16[2,512,128]{2,1,0:T(8,128)(2,1)S(1)}, u32[]{:S(2)}, u32[]{:S(2)}) %collective-permute-start.8) | collective-permute-done | bytes 262176 | tf_op jit(solution)/shard_map/ppermute | solution.py:179
  67.8 0.3 select_dynamic-update-slice_fusion
  68.2 2.3 %collective-permute-done.11 = bf16[2,1,512,128]{3,2,1,0:T(8,128)(2,1)S(1)} collective-permute-done((bf16[2,1,512,128]{3,2,1,0:T(8,128)(2,1)S(1)}, bf16[2,1,512,128]{3,2,1,0:T(8,128)(2,1)S(1)}, u32[]{:S(2)}, u32[]{:S(2)}) %collective-permute-start.11) | collective-permute-done | bytes 262176 | tf_op jit(solution)/shard_map/ppermute | solution.py:244
  70.6 0.0 copy-start.2
  70.6 1.0 copy-done.2
  71.6 13.4 %attend_near.1.near = f32[8,512,128]{2,1,0:T(8,128)} custom-call(bf16[8,512,128]{2,1,0:T(8,128)(2,1)} %get-tuple-element.9.query, bf16[10,512,128]{2,1,0:T(8,128)(2,1)} %copy-done.2), custom_call_target="tpu_custom_call" | custom-call | tf_op jit(solution)/shard_map/attend_near/pallas_call | solution.py:167
  85.0 26.4 %attend_far.1 = f32[8,512,128]{2,1,0:T(8,128)} custom-call(bf16[8,512,128]{2,1,0:T(8,128)(2,1)} %get-tuple-element.9.query, bf16[10,512,128]{2,1,0:T(8,128)(2,1)} %copy-done.1, f32[8,512,128]{2,1,0:T(8,128)} %attend_near.1.near, f32[8,512,128]{2,1,0:T(8,128)} %get-tuple-element.12.state, bf16[128,128]{1,0:T(8,128)(2,1)} %convolution_convert_fusion.value_out, ...), custom_call_target="tpu_custom_call" | custom-call | tf_op jit(solution)/shard_map/attend_far/pallas_call | solution.py:167
  (34 shorter events, 0.4 us)
Async XLA Ops:
  0.0 12.0 %copy-start = (bf16[128,128]{1,0:T(8,128)(2,1)S(1)}, bf16[128,128]{1,0:T(8,128)(2,1)}, u32[]{:S(2)}) copy-start(bf16[128,128]{1,0:T(8,128)(2,1)} %param.16) | copy-start | bytes 98308
  0.0 8.4 %copy-start.3 = (bf16[3,3,128,128]{3,2,1,0:T(8,128)(2,1)S(1)}, bf16[3,3,128,128]{3,2,1,0:T(8,128)(2,1)}, u32[]{:S(2)}) copy-start(bf16[3,3,128,128]{3,2,1,0:T(8,128)(2,1)} %param.14) | copy-start | bytes 884740
  1.9 12.4 %collective-permute-start = (bf16[2,512,128]{2,1,0:T(8,128)(2,1)S(1)}, bf16[2,512,128]{2,1,0:T(8,128)(2,1)S(1)}, u32[]{:S(2)}, u32[]{:S(2)}) collective-permute-start(bf16[2,512,128]{2,1,0:T(8,128)(2,1)S(1)} %get-tuple-element.16), channel_id=1, source_target_pairs={{0,1},{1,2},{2,3},{3,4},{4,5},{5,6},{6,7},{8,9},{9,10},{10,11},{11... | collective-permute-start | bytes 786440 | tf_op jit(solution)/shard_map/ppermute | solution.py:217
  6.5 7.8 %collective-permute-start.1 = (bf16[2,512,128]{2,1,0:T(8,128)(2,1)S(1)}, bf16[2,512,128]{2,1,0:T(8,128)(2,1)S(1)}, u32[]{:S(2)}, u32[]{:S(2)}) collective-permute-start(bf16[2,512,128]{2,1,0:T(8,128)(2,1)S(1)} %get-tuple-element.15), channel_id=1, source_target_pairs={{1,0},{2,1},{3,2},{4,3},{5,4},{6,5},{7,6},{9,8},{10,9},{11,10},{12... | collective-permute-start | bytes 786440 | tf_op jit(solution)/shard_map/ppermute | solution.py:218
  8.5 1.0 copy-start.4
  10.6 1.4 %copy-start.7 = (bf16[128,128]{1,0:T(8,128)(2,1)S(1)}, bf16[128,128]{1,0:T(8,128)(2,1)}, u32[]{:S(2)}) copy-start(bf16[128,128]{1,0:T(8,128)(2,1)} %param.17) | copy-start | bytes 98308
  10.6 2.8 %copy-start.10 = (f32[1,8,512]{2,1,0:T(8,128)S(1)}, f32[1,8,512]{2,1,0:T(8,128)}, u32[]{:S(2)}) copy-start(f32[1,8,512]{2,1,0:T(8,128)} %param.12) | copy-start | bytes 49156
  14.3 0.7 copy-start.5
  14.3 0.8 copy-start.6
  15.1 26.9 %copy-start.11 = (s32[4,2]{0,1:T(2,128)S(1)}, s32[4,2]{0,1:T(2,128)}, u32[]{:S(2)}) copy-start(s32[4,2]{0,1:T(2,128)} %param.13) | copy-start | bytes 100
  27.0 12.1 %collective-permute-start.2 = (bf16[4,512,128]{2,1,0:T(8,128)(2,1)}, bf16[4,512,128]{2,1,0:T(8,128)(2,1)S(1)}, u32[]{:S(2)}, u32[]{:S(2)}) collective-permute-start(bf16[4,512,128]{2,1,0:T(8,128)(2,1)} %get-tuple-element.10), channel_id=1, source_target_pairs={{0,16},{8,24},{16,0},{24,8},{1,17},{9,25},{17,1},{25,9},{2,18},{10... | collective-permute-start | bytes 1572872 | tf_op jit(solution)/shard_map/ppermute | solution.py:179
  28.2 12.7 %collective-permute-start.3 = (bf16[4,512,128]{2,1,0:T(8,128)(2,1)}, bf16[4,512,128]{2,1,0:T(8,128)(2,1)S(1)}, u32[]{:S(2)}, u32[]{:S(2)}) collective-permute-start(bf16[4,512,128]{2,1,0:T(8,128)(2,1)} %get-tuple-element.10), channel_id=1, source_target_pairs={{0,8},{8,0},{16,24},{24,16},{1,9},{9,1},{17,25},{25,17},{2,10},{10... | collective-permute-start | bytes 1572872 | tf_op jit(solution)/shard_map/ppermute | solution.py:179
  39.2 7.9 %collective-permute-start.4 = (bf16[2,512,128]{2,1,0:T(8,128)(2,1)S(1)}, bf16[2,512,128]{2,1,0:T(8,128)(2,1)S(1)}, u32[]{:S(2)}, u32[]{:S(2)}) collective-permute-start(bf16[2,512,128]{2,1,0:T(8,128)(2,1)S(1)} %slice.79), channel_id=1, source_target_pairs={{0,8},{8,0},{16,24},{24,16},{1,9},{9,1},{17,25},{25,17},{2,10},{10... | collective-permute-start | bytes 786440 | tf_op jit(solution)/shard_map/ppermute | solution.py:179
  41.0 8.4 %collective-permute-start.5 = (bf16[2,512,128]{2,1,0:T(8,128)(2,1)S(1)}, bf16[2,512,128]{2,1,0:T(8,128)(2,1)S(1)}, u32[]{:S(2)}, u32[]{:S(2)}) collective-permute-start(bf16[2,512,128]{2,1,0:T(8,128)(2,1)S(1)} %slice.80), channel_id=1, source_target_pairs={{0,16},{8,24},{16,0},{24,8},{1,17},{9,25},{17,1},{25,9},{2,18},{10... | collective-permute-start | bytes 786440 | tf_op jit(solution)/shard_map/ppermute | solution.py:179
  44.1 14.1 %collective-permute-start.9 = (bf16[4,512,128]{2,1,0:T(8,128)(2,1)}, bf16[4,512,128]{2,1,0:T(8,128)(2,1)S(1)}, u32[]{:S(2)}, u32[]{:S(2)}) collective-permute-start(bf16[4,512,128]{2,1,0:T(8,128)(2,1)} %get-tuple-element.11), channel_id=1, source_target_pairs={{0,8},{8,0},{16,24},{24,16},{1,9},{9,1},{17,25},{25,17},{2,10},{10... | collective-permute-start | bytes 1572872 | tf_op jit(solution)/shard_map/ppermute | solution.py:179
  44.6 15.6 %collective-permute-start.7 = (bf16[4,512,128]{2,1,0:T(8,128)(2,1)}, bf16[4,512,128]{2,1,0:T(8,128)(2,1)S(1)}, u32[]{:S(2)}, u32[]{:S(2)}) collective-permute-start(bf16[4,512,128]{2,1,0:T(8,128)(2,1)} %get-tuple-element.11), channel_id=1, source_target_pairs={{0,16},{8,24},{16,0},{24,8},{1,17},{9,25},{17,1},{25,9},{2,18},{10... | collective-permute-start | bytes 1572872 | tf_op jit(solution)/shard_map/ppermute | solution.py:179
  49.5 5.8 %copy-start.8 = (bf16[128,128]{1,0:T(8,128)(2,1)S(1)}, bf16[128,128]{1,0:T(8,128)(2,1)}, u32[]{:S(2)}) copy-start(bf16[128,128]{1,0:T(8,128)(2,1)} %param.18) | copy-start | bytes 98308
  49.5 5.8 %copy-start.9 = (bf16[128,128]{1,0:T(8,128)(2,1)S(1)}, bf16[128,128]{1,0:T(8,128)(2,1)}, u32[]{:S(2)}) copy-start(bf16[128,128]{1,0:T(8,128)(2,1)} %param.19) | copy-start | bytes 98308
  49.6 14.8 %collective-permute-start.6 = (bf16[2,1,512,128]{3,2,1,0:T(8,128)(2,1)S(1)}, bf16[2,1,512,128]{3,2,1,0:T(8,128)(2,1)S(1)}, u32[]{:S(2)}, u32[]{:S(2)}) collective-permute-start(bf16[2,1,512,128]{3,2,1,0:T(8,128)(2,1)S(1)} %pad_maximum_fusion.2), channel_id=1, source_target_pairs={{0,1},{1,2},{2,3},{3,4},{4,5},{5,6},{6,7},{8,9},{9,10},{10,11},{11... | collective-permute-start | bytes 786440 | tf_op jit(solution)/shard_map/ppermute | solution.py:243
  58.2 7.8 %collective-permute-start.10 = (bf16[2,512,128]{2,1,0:T(8,128)(2,1)S(1)}, bf16[2,512,128]{2,1,0:T(8,128)(2,1)S(1)}, u32[]{:S(2)}, u32[]{:S(2)}) collective-permute-start(bf16[2,512,128]{2,1,0:T(8,128)(2,1)S(1)} %slice.85), channel_id=1, source_target_pairs={{0,16},{8,24},{16,0},{24,8},{1,17},{9,25},{17,1},{25,9},{2,18},{10... | collective-permute-start | bytes 786440 | tf_op jit(solution)/shard_map/ppermute | solution.py:179
  60.3 7.6 %collective-permute-start.8 = (bf16[2,512,128]{2,1,0:T(8,128)(2,1)S(1)}, bf16[2,512,128]{2,1,0:T(8,128)(2,1)S(1)}, u32[]{:S(2)}, u32[]{:S(2)}) collective-permute-start(bf16[2,512,128]{2,1,0:T(8,128)(2,1)S(1)} %slice.84), channel_id=1, source_target_pairs={{0,8},{8,0},{16,24},{24,16},{1,9},{9,1},{17,25},{25,17},{2,10},{10... | collective-permute-start | bytes 786440 | tf_op jit(solution)/shard_map/ppermute | solution.py:179
  61.6 8.9 %collective-permute-start.11 = (bf16[2,1,512,128]{3,2,1,0:T(8,128)(2,1)S(1)}, bf16[2,1,512,128]{3,2,1,0:T(8,128)(2,1)S(1)}, u32[]{:S(2)}, u32[]{:S(2)}) collective-permute-start(bf16[2,1,512,128]{3,2,1,0:T(8,128)(2,1)S(1)} %pad_maximum_fusion.3), channel_id=1, source_target_pairs={{1,0},{2,1},{3,2},{4,3},{5,4},{6,5},{7,6},{9,8},{10,9},{11,10},{12... | collective-permute-start | bytes 786440 | tf_op jit(solution)/shard_map/ppermute | solution.py:244
  70.6 1.1 copy-start.2
  70.6 14.4 %copy-start.1 = (bf16[10,512,128]{2,1,0:T(8,128)(2,1)}, bf16[10,512,128]{2,1,0:T(8,128)(2,1)S(1)}, u32[]{:S(2)}) copy-start(bf16[10,512,128]{2,1,0:T(8,128)(2,1)S(1)} %get-tuple-element.30.keys) | copy-start | bytes 3932164

commit v2 on v1

v2 whole, which is shorter than its diff:
```python
import functools
import math

import jax
import jax.numpy as jnp
from jax import lax
from jax.experimental import pallas as pl
from jax.experimental.pallas import tpu as pltpu
from jax.sharding import PartitionSpec as P

epsilon = 1e-06
vmem_bytes = 28 * 1024 * 1024
whole_vmem_bytes = 56 * 1024 * 1024
in_vmem = pl.BlockSpec(memory_space=pltpu.VMEM)
in_smem = pl.BlockSpec(memory_space=pltpu.SMEM)
anywhere = pl.BlockSpec(memory_space=pl.ANY)


def silu(v):
    half = 0.5 * v
    return half * jnp.tanh(half) + half


def scaled(values, gain):
    channels = values.shape[-1]
    squares = (values * values).astype(jnp.bfloat16)
    ones = jnp.ones((channels, channels), jnp.bfloat16)
    mean_square = jnp.dot(squares, ones, preferred_element_type=jnp.float32) * (1.0 / channels)
    return values * lax.rsqrt(mean_square + epsilon) * gain


class Copies:
    def __init__(self, semaphores):
        self.semaphores = semaphores
        self.count = 0

    def start(self, source, target):
        copy = pltpu.make_async_copy(source, target, self.semaphores.at[self.count])
        self.count += 1
        copy.start()
        return copy

    def start_one(self, sources, chosen, target):
        slot = self.semaphores.at[self.count]
        self.count += 1
        for i, source in enumerate(sources):

            @pl.when(chosen == i)
            def _(source=source):
                pltpu.make_async_copy(source, target, slot).start()

        return pltpu.make_async_copy(sources[0], target, slot)


def clear(pad):
    slots, length, channels = pad.shape
    zeros = jnp.zeros((8, channels), jnp.float32)
    for slot in range(slots):
        pad[slot, 0:8] = zeros
        pad[slot, length - 8 : length] = zeros


def place(value, pad, slot):
    pad[slot, 8 : 8 + value.shape[0]] = value


def pack(kernel, out):
    channels = kernel.shape[2]
    zero = jnp.zeros((channels, channels), jnp.bfloat16)
    for j in range(4):
        for b in range(3):
            rows = pl.ds((3 * j + b) * channels, channels)
            out[rows, :channels] = kernel[j, b] if j < 3 else zero
            out[rows, channels:] = kernel[j - 1, b] if j > 0 else zero


def row_pair(pad, first, weights):
    columns = pad.shape[1] - 16
    lhs = [pad[first + j, 7 + b : 7 + b + columns] for j in range(4) for b in range(3)]
    lhs = jnp.concatenate(lhs, axis=-1).astype(jnp.bfloat16)
    return jnp.dot(lhs, weights[...], preferred_element_type=jnp.float32)


def ask(norm, slots, query_weight, key_weight, tempers, rows_of, query):
    channels = norm.shape[-1]
    mixing = lax.dot_general(
        query_weight[...],
        key_weight[...],
        (((1,), (1,)), ((), ())),
        preferred_element_type=jnp.float32,
    ).astype(jnp.bfloat16)
    scales = tempers[...].T * (math.log2(math.e) / math.sqrt(channels))
    for slot in range(slots):
        mixed = jnp.dot(norm[slot], mixing, preferred_element_type=jnp.float32)
        r = rows_of(slot)
        query[slot] = (mixed * scales[:, r : r + 1]).astype(jnp.bfloat16)


def middle_body(
    cells, one, two, query_weight, key_weight, tempers, gain,
    state_one_out, state_out, norm_out, query_out,
    held, one_held, two_held, query_held, key_held, tempers_held, gain_held,
    w1, w2, state_one, state_two, norm, query, x1, x2, sems,
):
    rows = cells.shape[0]
    channels = cells.shape[2]
    copies = Copies(sems)
    loads = [copies.start(cells.at[r], held.at[r]) for r in range(4)]
    later = [copies.start(one, one_held)]
    later += [copies.start(cells.at[r], held.at[r]) for r in range(4, rows)]
    later += [
        copies.start(two, two_held),
        copies.start(gain, gain_held),
        copies.start(query_weight, query_held),
        copies.start(key_weight, key_held),
        copies.start(tempers, tempers_held),
    ]
    clear(x1)
    clear(x2)

    def convolve_one(first):
        out = row_pair(x1, first, w1)
        for o in range(2):
            r = first + 1 + o
            state = held[r] + out[:, o * channels : (o + 1) * channels]
            state_one[r - 1] = state
            place(silu(state), x2, r - 1)

    def convolve_two(first):
        out = row_pair(x2, first, w2)
        for o in range(2):
            slot = first + o
            state = state_one[slot + 1] + out[:, o * channels : (o + 1) * channels]
            state_two[slot] = state
            norm[slot] = scaled(state, gain_held[...]).astype(jnp.bfloat16)

    for load in loads:
        load.wait()
    for r in range(4):
        place(silu(held[r]), x1, r)
    for load in later:
        load.wait()
    pack(one_held, w1)
    pack(two_held, w2)
    for first in range(0, rows - 2, 2):
        convolve_one(first)
        for r in range(first + 4, min(first + 6, rows)):
            place(silu(held[r]), x1, r)
        if first >= 2:
            convolve_two(first - 2)
    stores = [
        copies.start(norm, norm_out),
        copies.start(state_one.at[pl.ds(0, 2)], state_one_out.at[pl.ds(0, 2)]),
        copies.start(state_one.at[pl.ds(rows - 4, 2)], state_one_out.at[pl.ds(2, 2)]),
        copies.start(state_two, state_out),
    ]
    ask(norm, rows - 4, query_held, key_held, tempers_held, lambda slot: slot + 2, query)
    stores.append(copies.start(query, query_out))
    for store in stores:
        store.wait()


def scratch(*arrays):
    return [pltpu.VMEM(shape, kind) for shape, kind in arrays]


def middle_rows(cells, one, two, query_weight, key_weight, tempers, gain):
    rows, columns, channels = cells.shape
    row = (columns, channels)
    padded = (columns + 16, channels)
    packed = ((12 * channels, 2 * channels), jnp.bfloat16)
    operands = (cells, one, two, query_weight, key_weight, tempers, gain)
    return pl.pallas_call(
        middle_body,
        in_specs=[anywhere] * 7,
        out_specs=[anywhere] * 4,
        out_shape=[
            jax.ShapeDtypeStruct((4, *row), jnp.float32),
            jax.ShapeDtypeStruct((rows - 4, *row), jnp.float32),
            jax.ShapeDtypeStruct((rows - 4, *row), jnp.bfloat16),
            jax.ShapeDtypeStruct((rows - 4, *row), jnp.bfloat16),
        ],
        scratch_shapes=[
            *scratch(*[(a.shape, a.dtype) for a in operands]),
            *scratch(
                packed,
                packed,
                ((rows - 2, *row), jnp.float32),
                ((rows - 4, *row), jnp.float32),
                ((rows - 4, *row), jnp.bfloat16),
                ((rows - 4, *row), jnp.bfloat16),
                ((rows, *padded), jnp.float32),
                ((rows - 2, *padded), jnp.float32),
            ),
            pltpu.SemaphoreType.DMA((rows + 11,)),
        ],
        compiler_params=pltpu.CompilerParams(vmem_limit_bytes=whole_vmem_bytes),
        name="residual_middle",
    )(*operands)


def edge_body(
    cells, mate, cross, one, two, state_one, query_weight, key_weight, tempers, gain,
    state_out, norm_out, query_out,
    held, mate_held, cross_held, one_held, two_held, state_held, query_held, key_held,
    tempers_held, gain_held, w1, w2, state_two, norm, query, x1, x2, sems,
):
    rows = cells.shape[0]
    channels = cells.shape[2]
    first_band, last_band, odd = band_place()
    copies = Copies(sems)
    loads = [
        copies.start(cells.at[pl.ds(0, 2)], held.at[pl.ds(0, 2)]),
        copies.start(cells.at[pl.ds(rows - 2, 2)], held.at[pl.ds(2, 2)]),
        copies.start(mate, mate_held),
        copies.start(cross, cross_held),
    ]
    later = [
        copies.start(one, one_held),
        copies.start(two, two_held),
        copies.start(state_one, state_held),
        copies.start(query_weight, query_held),
        copies.start(key_weight, key_held),
        copies.start(tempers, tempers_held),
        copies.start(gain, gain_held),
    ]
    clear(x1)
    clear(x2)
    for load in loads:
        load.wait()
    for r in range(2):
        place(silu(held[r]), x1, 2 + r)
        place(silu(held[2 + r]), x1, 4 + r)
    outside = []
    for r in range(2):
        mate_row = mate_held[r].astype(jnp.float32)
        cross_row = cross_held[r].astype(jnp.float32)
        over = jnp.where(first_band, 0.0, jnp.where(odd, mate_row, cross_row))
        under = jnp.where(last_band, 0.0, jnp.where(odd, cross_row, mate_row))
        place(silu(over), x1, r)
        place(silu(under), x1, 6 + r)
        outside.append((over, under))
    over, under = outside[1][0], outside[0][1]
    for load in later:
        load.wait()
    pack(one_held, w1)
    pack(two_held, w2)
    out = row_pair(x1, 0, w1)
    over = over + out[:, :channels]
    top = held[0] + out[:, channels:]
    out = row_pair(x1, 4, w1)
    bottom = held[3] + out[:, :channels]
    under = under + out[:, channels:]
    for r in range(2):
        place(silu(state_held[r]), x2, 2 + r)
        place(silu(state_held[2 + r]), x2, 4 + r)
    place(jnp.where(first_band, 0.0, silu(over)), x2, 0)
    place(silu(top), x2, 1)
    place(silu(bottom), x2, 6)
    place(jnp.where(last_band, 0.0, silu(under)), x2, 7)
    for slot, states in ((0, (top, state_held[0])), (2, (state_held[3], bottom))):
        out = row_pair(x2, 2 * slot, w2)
        for o in range(2):
            state = states[o] + out[:, o * channels : (o + 1) * channels]
            state_two[slot + o] = state
            norm[slot + o] = scaled(state, gain_held[...]).astype(jnp.bfloat16)
    stores = [copies.start(norm, norm_out), copies.start(state_two, state_out)]
    ask(
        norm, 4, query_held, key_held, tempers_held,
        lambda slot: slot if slot < 2 else rows - 4 + slot, query,
    )
    stores.append(copies.start(query, query_out))
    for store in stores:
        store.wait()


def edge_rows(cells, mate, cross, one, two, state_one, query_weight, key_weight, tempers, gain):
    columns, channels = cells.shape[1:]
    row = (columns, channels)
    padded = (columns + 16, channels)
    packed = ((12 * channels, 2 * channels), jnp.bfloat16)
    operands = (
        cells, mate, cross, one, two, state_one, query_weight, key_weight, tempers, gain
    )
    return pl.pallas_call(
        edge_body,
        in_specs=[anywhere] * 10,
        out_specs=[anywhere] * 3,
        out_shape=[
            jax.ShapeDtypeStruct((4, *row), jnp.float32),
            jax.ShapeDtypeStruct((4, *row), jnp.bfloat16),
            jax.ShapeDtypeStruct((4, *row), jnp.bfloat16),
        ],
        scratch_shapes=[
            *scratch(((4, *row), jnp.float32), *[(a.shape, a.dtype) for a in operands[1:]]),
            *scratch(
                packed,
                packed,
                ((4, *row), jnp.float32),
                ((4, *row), jnp.bfloat16),
                ((4, *row), jnp.bfloat16),
                ((8, *padded), jnp.float32),
                ((8, *padded), jnp.float32),
            ),
            pltpu.SemaphoreType.DMA((14,)),
        ],
        compiler_params=pltpu.CompilerParams(vmem_limit_bytes=whole_vmem_bytes),
        name="residual_edge",
    )(*operands)


def band_place():
    band = lax.axis_index("band")
    return band == 0, band == lax.axis_size("band") - 1, lax.rem(band, 2) == 1


def blend(query, window, store):
    keys, channels = window.shape
    extended = jnp.concatenate([window, jnp.ones((keys, channels), jnp.bfloat16)], axis=1)
    columns = query.shape[0]
    block = 128 if columns % 128 == 0 else columns
    for start in range(0, columns, block):
        scores = lax.dot_general(
            query[pl.ds(start, block)],
            window,
            (((1,), (1,)), ((), ())),
            preferred_element_type=jnp.float32,
        )
        peak = jnp.max(scores, axis=-1, keepdims=True)
        lifted = jnp.exp2(scores - peak).astype(jnp.bfloat16)
        total = jnp.dot(lifted, extended, preferred_element_type=jnp.float32)
        store(pl.ds(start, block), total[:, :channels] / total[:, channels:])


def pick(chosen, candidates):
    picked = candidates[0]
    for i, candidate in enumerate(candidates[1:], 1):
        picked = jnp.where(chosen == i, candidate, picked)
    return picked


def gather_keys(chosen, edges, middles, mate, cross, keys):
    rows = keys.shape[0] - 2
    first_band, last_band, odd = band_place()
    above = jnp.where(odd, mate[0], cross[0])
    below = jnp.where(odd, cross[0], mate[0])
    keys[0] = jnp.where(first_band, jnp.zeros_like(above), above)
    keys[rows + 1] = jnp.where(last_band, jnp.zeros_like(below), below)
    for r in range(2):
        keys[1 + r] = pick(chosen, [edge[r] for edge in edges])
        keys[rows - 1 + r] = pick(chosen, [edge[2 + r] for edge in edges])
    for r in range(rows - 4):
        keys[3 + r] = pick(chosen, [middle[r] for middle in middles])


def band_row(edge, middle, r):
    inner = middle.shape[0]
    if r < 2:
        return edge.at[r]
    if r < inner + 2:
        return middle.at[r - 2]
    return edge.at[r - inner]


def attend_near_body(count, chosen, *refs):
    edges, middles = refs[:count], refs[count : 2 * count]
    mate, cross, query_edge, query_middle, out, keys = refs[2 * count :]
    rows, columns, channels = out.shape
    gather_keys(chosen[0], edges, middles, mate, cross, keys)
    for r in range(rows):
        window = keys[r : r + 3].reshape(3 * columns, channels)

        def store(place, value, r=r):
            out[r, place] = value.astype(jnp.bfloat16)

        blend(band_row(query_edge, query_middle, r), window, store)


def attend_far_body(count, chosen, *refs):
    edges, middles = refs[:count], refs[count : 2 * count]
    (
        mate, cross, query_edge, query_middle, near, state_edge, state_middle, value_out, gain,
        out, keys, both,
    ) = refs[2 * count :]
    rows, columns, channels = out.shape
    gather_keys(chosen[0], edges, middles, mate, cross, keys)
    for r in range(rows):
        window = keys[r : r + 3].reshape(3 * columns, channels)

        def store(place, value, r=r):
            both[r, place] = (value + near[r, place].astype(jnp.float32)).astype(jnp.bfloat16)

        blend(band_row(query_edge, query_middle, r), window, store)
    for r in range(rows):
        message = jnp.dot(both[r], value_out[...], preferred_element_type=jnp.float32)
        state = band_row(state_edge, state_middle, r)[...]
        out[r] = state + scaled(message, gain[...])


def attend(body, name, chosen, edges, middles, mate, cross, queries, rest, out_type, extra):
    query_edge, query_middle = queries
    rows = query_edge.shape[0] + query_middle.shape[0]
    columns, channels = query_edge.shape[1:]
    operands = [*edges, *middles, mate, cross, *queries, *rest]
    return pl.pallas_call(
        functools.partial(body, len(edges)),
        in_specs=[in_smem] + [in_vmem] * len(operands),
        out_specs=in_vmem,
        out_shape=jax.ShapeDtypeStruct((rows, columns, channels), out_type),
        scratch_shapes=[
            pltpu.VMEM((rows + 2, columns, channels), jnp.bfloat16),
            *[pltpu.VMEM((rows, columns, channels), kind) for kind in extra],
        ],
        compiler_params=pltpu.CompilerParams(vmem_limit_bytes=vmem_bytes),
        name=name,
    )(chosen, *operands)


def swap(cells, views, offset):
    return lax.ppermute(cells, "view", [(i, i ^ offset) for i in range(views)])


def gather_direct(cells, views):
    return {1 << i: swap(cells, views, 1 << i) for i in range((views - 1).bit_length())}


def gather_relayed(edges, middles, views):
    for offset in range(1, views):
        low = offset & -offset
        high = 1 << (offset.bit_length() - 1)
        if low != high:
            edges[offset] = swap(edges[offset ^ high], views, high)
            middles[offset] = swap(middles[offset ^ low], views, low)


def swap_bands(head, tail, odd, bands):
    mates = [(i, i ^ 1) for i in range(bands)]
    crosses = [(i, i + 1) for i in range(1, bands - 1, 2)]
    crosses = crosses + [(j, i) for i, j in crosses]
    mate = lax.ppermute(jnp.where(odd, head, tail), "band", mates)
    cross = lax.ppermute(jnp.where(odd, tail, head), "band", crosses)
    return mate, cross


def per_device(
    features, tempers, partners, conv_one, conv_two, query_weight, key_weight,
    value_weight, out_weight, norm_gain, message_gain,
):
    views = lax.axis_size("view")
    bands = lax.axis_size("band")
    odd = lax.axis_index("band") % 2 > 0
    view = lax.axis_index("view")
    cells, temper, gain = features[0], tempers[0], norm_gain[None]
    rows = cells.shape[0]

    state_one, state_middle, middle, query_middle = middle_rows(
        cells, conv_one, conv_two, query_weight, key_weight, temper, gain
    )
    middles = gather_direct(middle, views)
    head, tail = cells[:2].astype(jnp.bfloat16), cells[rows - 2 :].astype(jnp.bfloat16)
    mate, cross = swap_bands(head, tail, odd, bands)
    state_edge, edge, query_edge = edge_rows(
        cells, mate, cross, conv_one, conv_two, state_one, query_weight, key_weight, temper, gain
    )
    queries = (query_edge, query_middle)
    edges = gather_direct(edge, views)
    edges, middles = lax.optimization_barrier((edges, middles))
    gather_relayed(edges, middles, views)
    value_out = jnp.dot(value_weight, out_weight, preferred_element_type=jnp.float32).astype(
        jnp.bfloat16
    )

    offsets = jnp.bitwise_xor(lax.dynamic_index_in_dim(partners, view, 0, keepdims=False), view)

    def keys_of(offset, low, high, after=None):
        chosen = offset - low
        some_edges = [edges[i] for i in range(low, high + 1)]
        some_middles = [middles[i] for i in range(low, high + 1)]
        if after is not None:
            some_edges, some_middles, after = lax.optimization_barrier(
                (some_edges, some_middles, after)
            )
        tail = pick(chosen, [e[-1:] for e in some_edges])
        head = pick(chosen, [e[:1] for e in some_edges])
        halos = swap_bands(head, tail, odd, bands)
        return chosen[None], some_edges, some_middles, *halos

    near_keys = keys_of(jnp.min(offsets), 1, max(1, views - 2))
    near_blend = attend(
        attend_near_body, "attend_near", *near_keys, queries, (), jnp.bfloat16, []
    )
    far_keys = keys_of(jnp.max(offsets), min(2, views - 1), views - 1, near_blend)
    refined = attend(
        attend_far_body, "attend_far", *far_keys, queries,
        (near_blend, state_edge, state_middle, value_out, message_gain[None]), jnp.float32,
        [jnp.bfloat16],
    )
    return refined[None]


def solution(mesh):
    whole = P()
    in_specs = (P("view", "band", None, None), P("view", "band", None)) + (whole,) * 9
    return jax.shard_map(
        per_device, mesh=mesh, in_specs=in_specs,
        out_specs=P("view", "band", None, None), check_vma=False,
    )
```

time: 112 us -> 76.7 us (0.68)
  Pallas kernels: 51.6 us -> 31.4 us
  starting transfers between devices: 24.9 us -> 18.2 us
  local copies, waits for them, and re-layouts: 5.68 us -> 1.85 us
  waiting for transfers between devices: 21.3 us -> 19.9 us
  matrix products: 1.52 us -> 0.13 us
  other arithmetic: 4.6 us -> 3.35 us
    pallas_call x3 -> x4, Pallas kernels: 51.6 us -> 31.4 us  [the longest x2 17.6 us: attend(): pl.pallas_call(functools.partial(body, len(edges)), in_specs=[in_smem] +...]
    ppermute x8 -> x6, starting transfers between devices: 10 us -> 4.6 us  [swap(): return lax.ppermute(cells, 'view', [(i, i ^ offset) for i in range(views)])]
    ppermute x8 -> x6, waiting for transfers between devices: 19 us -> 15 us  [swap(): return lax.ppermute(cells, 'view', [(i, i ^ offset) for i in range(views)])]
    ppermute x4 -> x6, waiting for transfers between devices: 2.32 us -> 4.89 us  [the longest x3 4.89 us: swap_bands(): cross = lax.ppermute(jnp.where(odd, tail, head), 'band', crosses)]
    another operation x6 -> x0, local copies, waits for them, and re-layouts: 1.93 us -> none  [the longest x4 1.89 us: pair_weights(): both = jnp.stack([first, second], axis=3)]
    reshape x1 -> x0, local copies, waits for them, and re-layouts: 1.39 us -> none  [pair_weights(): return both.reshape((taps + 1) * taps * channels, 2 * out_channels)]
    ppermute x4 -> x6, starting transfers between devices: 14.9 us -> 13.6 us  [the longest x3 13.4 us: swap_bands(): cross = lax.ppermute(jnp.where(odd, tail, head), 'band', crosses)]
  transfers between devices with their start and end apart: 12 -> 12, of which waited for: 8 -> 6; matrix products, arithmetic and copies ran while one was open for 7% -> 2% of each run, Pallas kernels for 0% -> 28%
where the time goes in v2:
time: 76.7 us; the launch traced here: 76.3 us
  Pallas kernels  31.4 us (41%)
  waiting for transfers between devices  19.9 us (26%)
  starting transfers between devices  18.2 us (24%)
  other arithmetic  3.35 us (4%)
  local copies, waits for them, and re-layouts  1.85 us (2%)
  between operations  1.53 us (2%)
    pallas_call x2, Pallas kernels, attend(): pl.pallas_call(functools.partial(body, len(edges)), in_specs=[in_smem] +...  17.6 us
    ppermute x6, waiting for transfers between devices, swap(): return lax.ppermute(cells, 'view', [(i, i ^ offset) for i in range(views)])  15 us
    ppermute x3, starting transfers between devices, swap_bands(): cross = lax.ppermute(jnp.where(odd, tail, head), 'band', crosses)  13.4 us
    pallas_call x1, Pallas kernels, middle_rows(): pl.pallas_call(middle_body, in_specs=[anywhere] * 7, out_specs=[anywhere]...  7.14 us
    pallas_call x1, Pallas kernels, edge_rows(): pl.pallas_call(edge_body, in_specs=[anywhere] * 10, out_specs=[anywhere]...  6.59 us
    ppermute x3, waiting for transfers between devices, swap_bands(): cross = lax.ppermute(jnp.where(odd, tail, head), 'band', crosses)  4.89 us
    ppermute x6, starting transfers between devices, swap(): return lax.ppermute(cells, 'view', [(i, i ^ offset) for i in range(views)])  4.6 us
    unnamed x22, local copies, waits for them, and re-layouts  1.85 us
  transfers between devices with their start and end apart: 12, of which 6 were waited for; matrix products, arithmetic and copies ran while one was open for 2% of the time, Pallas kernels for 28%

profile of v2, /device:TPU:1, one launch (start us, length us, event | category | flops | bytes accessed | tf_op | source)
XLA Modules:
  0.0 76.3 jit_solution(14302504046479505925)
XLA Ops:
  0.0 0.0 copy-start
  0.0 1.8 %convert.4 = bf16[1,8,512,128]{3,2,1,0:T(8,128)(2,1)S(1)} convert(f32[1,8,512,128]{3,2,1,0:T(8,128)} %param.11) | non-fusion elementwise | flops 524288 | bytes 3145728 | tf_op jit(solution)/shard_map/convert.1
  1.8 4.6 %collective-permute-start.1 = (bf16[2,512,128]{2,1,0:T(8,128)(2,1)S(1)}, bf16[2,512,128]{2,1,0:T(8,128)(2,1)S(1)}, u32[]{:S(2)}, u32[]{:S(2)}) collective-permute-start(bf16[2,512,128]{2,1,0:T(8,128)(2,1)S(1)} %get-tuple-element.41), channel_id=1, source_target_pairs={{1,2},{3,4},{5,6},{2,1},{4,3},{6,5},{9,10},{11,12},{13,14},{10,9},... | collective-permute-start | bytes 786440 | tf_op jit(solution)/shard_map/ppermute | solution.py:441
  6.4 0.1 collective-permute-start
  6.5 7.1 %residual_middle.1 = (f32[4,512,128]{2,1,0:T(8,128)}, f32[4,512,128]{2,1,0:T(8,128)}, bf16[4,512,128]{2,1,0:T(8,128)(2,1)}, bf16[4,512,128]{2,1,0:T(8,128)(2,1)}) custom-call(f32[8,512,128]{2,1,0:T(8,128)} %bitcast.14, bf16[3,3,128,128]{3,2,1,0:T(8,128)(2,1)} %one.3, bf16[3,3,128,128]{3,2,1,0:T(8,128)(2,1)} %two.3, bf16[128,128]{1,0:T(8,128)(2,1)} %query_weight.3, ...), custom_call_target="tpu_custom_call" | custom-call | tf_op jit(solution)/shard_map/residual_middle/pallas_call | solution.py:173
  13.6 1.3 %collective-permute-start.5 = (bf16[4,512,128]{2,1,0:T(8,128)(2,1)}, bf16[4,512,128]{2,1,0:T(8,128)(2,1)S(1)}, u32[]{:S(2)}, u32[]{:S(2)}) collective-permute-start(bf16[4,512,128]{2,1,0:T(8,128)(2,1)} %get-tuple-element.22), channel_id=1, source_target_pairs={{0,16},{8,24},{16,0},{24,8},{1,17},{9,25},{17,1},{25,9},{2,18},{10... | collective-permute-start | bytes 1572872 | tf_op jit(solution)/shard_map/ppermute | solution.py:420
  14.9 1.2 %collective-permute-start.4 = (bf16[4,512,128]{2,1,0:T(8,128)(2,1)}, bf16[4,512,128]{2,1,0:T(8,128)(2,1)S(1)}, u32[]{:S(2)}, u32[]{:S(2)}) collective-permute-start(bf16[4,512,128]{2,1,0:T(8,128)(2,1)} %get-tuple-element.22), channel_id=1, source_target_pairs={{0,8},{8,0},{16,24},{24,16},{1,9},{9,1},{17,25},{25,17},{2,10},{10... | collective-permute-start | bytes 1572872 | tf_op jit(solution)/shard_map/ppermute | solution.py:420
  16.2 0.0 collective-permute-done.1.cross
  16.2 0.0 copy-start.7
  16.2 0.0 collective-permute-done.mate
  16.2 0.0 copy-start.8
  16.2 0.7 copy-done.7
  16.9 0.1 copy-done.8
  17.0 0.0 copy-start.10
  17.0 6.6 %residual_edge.1 = (f32[4,512,128]{2,1,0:T(8,128)}, bf16[4,512,128]{2,1,0:T(8,128)(2,1)}, bf16[4,512,128]{2,1,0:T(8,128)(2,1)}) custom-call(f32[8,512,128]{2,1,0:T(8,128)} %bitcast.15, bf16[2,512,128]{2,1,0:T(8,128)(2,1)} %copy-done.8, bf16[2,512,128]{2,1,0:T(8,128)(2,1)} %copy-done.7, bf16[3,3,128,128]{3,2,1,0:T(8,128)(2,1)} %one.3, ...), custom_call_target="tpu_custom_call" | custom-call | tf_op jit(solution)/shard_map/residual_edge/pallas_call | solution.py:285
  23.6 0.3 collective-permute-start.3
  23.9 0.3 collective-permute-start.2
  24.1 2.8 %collective-permute-done.5.refs_3_.refs_2_ = bf16[4,512,128]{2,1,0:T(8,128)(2,1)S(1)} collective-permute-done((bf16[4,512,128]{2,1,0:T(8,128)(2,1)}, bf16[4,512,128]{2,1,0:T(8,128)(2,1)S(1)}, u32[]{:S(2)}, u32[]{:S(2)}) %collective-permute-start.5) | collective-permute-done | bytes 524320 | tf_op jit(solution)/shard_map/ppermute | solution.py:420
  26.9 0.9 %collective-permute-done.4.refs_2_ = bf16[4,512,128]{2,1,0:T(8,128)(2,1)S(1)} collective-permute-done((bf16[4,512,128]{2,1,0:T(8,128)(2,1)}, bf16[4,512,128]{2,1,0:T(8,128)(2,1)S(1)}, u32[]{:S(2)}, u32[]{:S(2)}) %collective-permute-start.4) | collective-permute-done | bytes 524320 | tf_op jit(solution)/shard_map/ppermute | solution.py:420
  27.8 10.3 %collective-permute-done.3.refs_1_.refs_0_ = bf16[4,512,128]{2,1,0:T(8,128)(2,1)S(1)} collective-permute-done((bf16[4,512,128]{2,1,0:T(8,128)(2,1)}, bf16[4,512,128]{2,1,0:T(8,128)(2,1)S(1)}, u32[]{:S(2)}, u32[]{:S(2)}) %collective-permute-start.3) | collective-permute-done | bytes 524320 | tf_op jit(solution)/shard_map/ppermute | solution.py:420
  38.2 0.9 %collective-permute-done.2.refs_0_ = bf16[4,512,128]{2,1,0:T(8,128)(2,1)S(1)} collective-permute-done((bf16[4,512,128]{2,1,0:T(8,128)(2,1)}, bf16[4,512,128]{2,1,0:T(8,128)(2,1)S(1)}, u32[]{:S(2)}, u32[]{:S(2)}) %collective-permute-start.2) | collective-permute-done | bytes 524320 | tf_op jit(solution)/shard_map/ppermute | solution.py:420
  39.1 0.3 collective-permute-start.6
  39.4 1.2 %collective-permute-start.7 = (bf16[4,512,128]{2,1,0:T(8,128)(2,1)S(1)}, bf16[4,512,128]{2,1,0:T(8,128)(2,1)}, u32[]{:S(2)}, u32[]{:S(2)}) collective-permute-start(bf16[4,512,128]{2,1,0:T(8,128)(2,1)S(1)} %collective-permute-done.5.refs_3_.refs_2_), channel_id=1, source_target_pairs={{0,8},{8,0},{16,24},{24,16},{1,9},{9,1},{17,25},{25,17},{2,10},{10... | collective-permute-start | bytes 1572872 | tf_op jit(solution)/shard_map/ppermute | solution.py:420
  40.6 0.0 copy-done.10
  40.6 0.8 %fusion = (s32[]{:T(128)}, s32[]{:T(128)}) fusion(s32[]{:T(128)S(6)} %axis_index.23, s32[4,2]{0,1:T(2,128)S(1)} %copy-done.10, s32[]{:T(128)S(6)} %select_n.69), kind=kLoop, calls=%fused_computation.12 | loop fusion | flops 4 | bytes 24 | tf_op jit(solution)/shard_map/reduce_min | solution.py:488
  42.1 0.7 broadcast_select_fusion.2
  42.8 5.4 %collective-permute-start.9 = (bf16[1,512,128]{2,1,0:T(8,128)(2,1)}, bf16[1,512,128]{2,1,0:T(8,128)(2,1)S(1)}, u32[]{:S(2)}, u32[]{:S(2)}) collective-permute-start(bf16[1,512,128]{2,1,0:T(8,128)(2,1)} %get-tuple-element.39), channel_id=1, source_target_pairs={{1,2},{3,4},{5,6},{2,1},{4,3},{6,5},{9,10},{11,12},{13,14},{10,9},... | collective-permute-start | bytes 393224 | tf_op jit(solution)/shard_map/ppermute | solution.py:441
  48.2 0.1 collective-permute-start.8
  48.9 2.3 %collective-permute-done.9.refs_5_ = bf16[1,512,128]{2,1,0:T(8,128)(2,1)S(1)} collective-permute-done((bf16[1,512,128]{2,1,0:T(8,128)(2,1)}, bf16[1,512,128]{2,1,0:T(8,128)(2,1)S(1)}, u32[]{:S(2)}, u32[]{:S(2)}) %collective-permute-start.9) | collective-permute-done | bytes 131104 | tf_op jit(solution)/shard_map/ppermute | solution.py:441
  51.2 0.0 collective-permute-done.8.refs_4_
  51.2 0.0 copy-done.1
  51.3 1.0 %copy-done.2 = bf16[4,512,128]{2,1,0:T(8,128)(2,1)S(1)} copy-done((bf16[4,512,128]{2,1,0:T(8,128)(2,1)S(1)}, bf16[4,512,128]{2,1,0:T(8,128)(2,1)}, u32[]{:S(2)}) %copy-start.2) | copy-done | bytes 524312
  52.3 0.0 copy-start.6
  52.3 7.4 %attend_near.1.refs_8_ = bf16[8,512,128]{2,1,0:T(8,128)(2,1)S(1)} custom-call(s32[1]{0:T(128)} %bitcast.6.chosen, bf16[4,512,128]{2,1,0:T(8,128)(2,1)S(1)} %collective-permute-done.2.refs_0_, bf16[4,512,128]{2,1,0:T(8,128)(2,1)S(1)} %collective-permute-done.3.refs_1_.refs_0_, bf16[4,512,128]{2,1,0:T(8,128)(2,1)S(1)} %collective-permute-done.4.refs_2_, ...), custom_call_target="tpu_custom_call" | custom-call | tf_op jit(solution)/shard_map/attend_near/pallas_call | solution.py:405
  59.7 0.0 collective-permute-done.6.refs_1_
  59.7 0.0 collective-permute-done.7.refs_3_
  59.8 3.5 %collective-permute-start.11 = (bf16[1,512,128]{2,1,0:T(8,128)(2,1)S(1)}, bf16[1,512,128]{2,1,0:T(8,128)(2,1)S(1)}, u32[]{:S(2)}, u32[]{:S(2)}) collective-permute-start(bf16[1,512,128]{2,1,0:T(8,128)(2,1)S(1)} %get-tuple-element.37), channel_id=1, source_target_pairs={{1,2},{3,4},{5,6},{2,1},{4,3},{6,5},{9,10},{11,12},{13,14},{10,9},... | collective-permute-start | bytes 393224 | tf_op jit(solution)/shard_map/ppermute | solution.py:441
  63.3 0.1 collective-permute-start.10
  63.3 0.0 copy-done
  63.4 0.0 copy-done.9
  63.4 0.1 convolution_convert_fusion.refs_11_
  63.5 2.6 %collective-permute-done.11.refs_5_ = bf16[1,512,128]{2,1,0:T(8,128)(2,1)S(1)} collective-permute-done((bf16[1,512,128]{2,1,0:T(8,128)(2,1)S(1)}, bf16[1,512,128]{2,1,0:T(8,128)(2,1)S(1)}, u32[]{:S(2)}, u32[]{:S(2)}) %collective-permute-start.11) | collective-permute-done | bytes 131104 | tf_op jit(solution)/shard_map/ppermute | solution.py:441
  66.1 0.0 collective-permute-done.10.refs_4_
  66.1 0.0 copy-done.3
  66.1 0.0 copy-done.4
  66.1 0.0 copy-done.5
  66.1 0.0 copy-done.6
  66.1 10.2 %attend_far.1 = f32[8,512,128]{2,1,0:T(8,128)} custom-call(s32[1]{0:T(128)} %bitcast.chosen, bf16[4,512,128]{2,1,0:T(8,128)(2,1)S(1)} %collective-permute-done.3.refs_1_.refs_0_, bf16[4,512,128]{2,1,0:T(8,128)(2,1)S(1)} %collective-permute-done.6.refs_1_, bf16[4,512,128]{2,1,0:T(8,128)(2,1)S(1)} %collective-permute-done.5.refs_3_.refs_2_, ...), custom_call_target="tpu_custom_call" | custom-call | tf_op jit(solution)/shard_map/attend_far/pallas_call | solution.py:405
  (8 shorter events, 0.1 us)
Async XLA Ops:
  0.0 63.4 %copy-start = (bf16[128,128]{1,0:T(8,128)(2,1)S(1)}, bf16[128,128]{1,0:T(8,128)(2,1)}, u32[]{:S(2)}) copy-start(bf16[128,128]{1,0:T(8,128)(2,1)} %param.18) | copy-start | bytes 98308
  1.8 14.3 %collective-permute-start.1 = (bf16[2,512,128]{2,1,0:T(8,128)(2,1)S(1)}, bf16[2,512,128]{2,1,0:T(8,128)(2,1)S(1)}, u32[]{:S(2)}, u32[]{:S(2)}) collective-permute-start(bf16[2,512,128]{2,1,0:T(8,128)(2,1)S(1)} %get-tuple-element.41), channel_id=1, source_target_pairs={{1,2},{3,4},{5,6},{2,1},{4,3},{6,5},{9,10},{11,12},{13,14},{10,9},... | collective-permute-start | bytes 786440 | tf_op jit(solution)/shard_map/ppermute | solution.py:441
  6.4 9.7 %collective-permute-start = (bf16[2,512,128]{2,1,0:T(8,128)(2,1)S(1)}, bf16[2,512,128]{2,1,0:T(8,128)(2,1)S(1)}, u32[]{:S(2)}, u32[]{:S(2)}) collective-permute-start(bf16[2,512,128]{2,1,0:T(8,128)(2,1)S(1)} %get-tuple-element.42), channel_id=1, source_target_pairs={{0,1},{1,0},{2,3},{3,2},{4,5},{5,4},{6,7},{7,6},{8,9},{9,8},{10,11... | collective-permute-start | bytes 786440 | tf_op jit(solution)/shard_map/ppermute | solution.py:440
  13.6 13.3 %collective-permute-start.5 = (bf16[4,512,128]{2,1,0:T(8,128)(2,1)}, bf16[4,512,128]{2,1,0:T(8,128)(2,1)S(1)}, u32[]{:S(2)}, u32[]{:S(2)}) collective-permute-start(bf16[4,512,128]{2,1,0:T(8,128)(2,1)} %get-tuple-element.22), channel_id=1, source_target_pairs={{0,16},{8,24},{16,0},{24,8},{1,17},{9,25},{17,1},{25,9},{2,18},{10... | collective-permute-start | bytes 1572872 | tf_op jit(solution)/shard_map/ppermute | solution.py:420
  14.9 12.9 %collective-permute-start.4 = (bf16[4,512,128]{2,1,0:T(8,128)(2,1)}, bf16[4,512,128]{2,1,0:T(8,128)(2,1)S(1)}, u32[]{:S(2)}, u32[]{:S(2)}) collective-permute-start(bf16[4,512,128]{2,1,0:T(8,128)(2,1)} %get-tuple-element.22), channel_id=1, source_target_pairs={{0,8},{8,0},{16,24},{24,16},{1,9},{9,1},{17,25},{25,17},{2,10},{10... | collective-permute-start | bytes 1572872 | tf_op jit(solution)/shard_map/ppermute | solution.py:420
  16.2 0.7 copy-start.7
  16.2 0.8 %copy-start.8 = (bf16[2,512,128]{2,1,0:T(8,128)(2,1)}, bf16[2,512,128]{2,1,0:T(8,128)(2,1)S(1)}, u32[]{:S(2)}) copy-start(bf16[2,512,128]{2,1,0:T(8,128)(2,1)S(1)} %collective-permute-done.mate) | copy-start | bytes 786436
  17.0 23.7 %copy-start.10 = (s32[4,2]{0,1:T(2,128)S(1)}, s32[4,2]{0,1:T(2,128)}, u32[]{:S(2)}) copy-start(s32[4,2]{0,1:T(2,128)} %param.13) | copy-start | bytes 100
  17.0 34.3 %copy-start.1 = (bf16[4,512,128]{2,1,0:T(8,128)(2,1)S(1)}, bf16[4,512,128]{2,1,0:T(8,128)(2,1)}, u32[]{:S(2)}) copy-start(bf16[4,512,128]{2,1,0:T(8,128)(2,1)} %get-tuple-element.28.refs_7_) | copy-start | bytes 1572868
  23.6 14.6 %collective-permute-start.3 = (bf16[4,512,128]{2,1,0:T(8,128)(2,1)}, bf16[4,512,128]{2,1,0:T(8,128)(2,1)S(1)}, u32[]{:S(2)}, u32[]{:S(2)}) collective-permute-start(bf16[4,512,128]{2,1,0:T(8,128)(2,1)} %get-tuple-element.21), channel_id=1, source_target_pairs={{0,16},{8,24},{16,0},{24,8},{1,17},{9,25},{17,1},{25,9},{2,18},{10... | collective-permute-start | bytes 1572872 | tf_op jit(solution)/shard_map/ppermute | solution.py:420
  23.9 15.2 %collective-permute-start.2 = (bf16[4,512,128]{2,1,0:T(8,128)(2,1)}, bf16[4,512,128]{2,1,0:T(8,128)(2,1)S(1)}, u32[]{:S(2)}, u32[]{:S(2)}) collective-permute-start(bf16[4,512,128]{2,1,0:T(8,128)(2,1)} %get-tuple-element.21), channel_id=1, source_target_pairs={{0,8},{8,0},{16,24},{24,16},{1,9},{9,1},{17,25},{25,17},{2,10},{10... | collective-permute-start | bytes 1572872 | tf_op jit(solution)/shard_map/ppermute | solution.py:420
  39.1 20.7 %collective-permute-start.6 = (bf16[4,512,128]{2,1,0:T(8,128)(2,1)S(1)}, bf16[4,512,128]{2,1,0:T(8,128)(2,1)S(1)}, u32[]{:S(2)}, u32[]{:S(2)}) collective-permute-start(bf16[4,512,128]{2,1,0:T(8,128)(2,1)S(1)} %collective-permute-done.2.refs_0_), channel_id=1, source_target_pairs={{0,16},{8,24},{16,0},{24,8},{1,17},{9,25},{17,1},{25,9},{2,18},{10... | collective-permute-start | bytes 1572872 | tf_op jit(solution)/shard_map/ppermute | solution.py:420
  39.4 20.3 %collective-permute-start.7 = (bf16[4,512,128]{2,1,0:T(8,128)(2,1)S(1)}, bf16[4,512,128]{2,1,0:T(8,128)(2,1)}, u32[]{:S(2)}, u32[]{:S(2)}) collective-permute-start(bf16[4,512,128]{2,1,0:T(8,128)(2,1)S(1)} %collective-permute-done.5.refs_3_.refs_2_), channel_id=1, source_target_pairs={{0,8},{8,0},{16,24},{24,16},{1,9},{9,1},{17,25},{25,17},{2,10},{10... | collective-permute-start | bytes 1572872 | tf_op jit(solution)/shard_map/ppermute | solution.py:420
  42.8 8.4 %collective-permute-start.9 = (bf16[1,512,128]{2,1,0:T(8,128)(2,1)}, bf16[1,512,128]{2,1,0:T(8,128)(2,1)S(1)}, u32[]{:S(2)}, u32[]{:S(2)}) collective-permute-start(bf16[1,512,128]{2,1,0:T(8,128)(2,1)} %get-tuple-element.39), channel_id=1, source_target_pairs={{1,2},{3,4},{5,6},{2,1},{4,3},{6,5},{9,10},{11,12},{13,14},{10,9},... | collective-permute-start | bytes 393224 | tf_op jit(solution)/shard_map/ppermute | solution.py:441
  48.2 3.1 %collective-permute-start.8 = (bf16[1,512,128]{2,1,0:T(8,128)(2,1)}, bf16[1,512,128]{2,1,0:T(8,128)(2,1)S(1)}, u32[]{:S(2)}, u32[]{:S(2)}) collective-permute-start(bf16[1,512,128]{2,1,0:T(8,128)(2,1)} %get-tuple-element.40), channel_id=1, source_target_pairs={{0,1},{1,0},{2,3},{3,2},{4,5},{5,4},{6,7},{7,6},{8,9},{9,8},{10,11... | collective-permute-start | bytes 393224 | tf_op jit(solution)/shard_map/ppermute | solution.py:440
  51.2 1.0 %copy-start.2 = (bf16[4,512,128]{2,1,0:T(8,128)(2,1)S(1)}, bf16[4,512,128]{2,1,0:T(8,128)(2,1)}, u32[]{:S(2)}) copy-start(bf16[4,512,128]{2,1,0:T(8,128)(2,1)} %get-tuple-element.27.refs_6_) | copy-start | bytes 1572868
  52.3 11.1 %copy-start.9 = (bf16[128,128]{1,0:T(8,128)(2,1)S(1)}, bf16[128,128]{1,0:T(8,128)(2,1)}, u32[]{:S(2)}) copy-start(bf16[128,128]{1,0:T(8,128)(2,1)} %param.19) | copy-start | bytes 98308
  52.3 13.8 %copy-start.3 = (bf16[4,512,128]{2,1,0:T(8,128)(2,1)S(1)}, bf16[4,512,128]{2,1,0:T(8,128)(2,1)}, u32[]{:S(2)}) copy-start(bf16[4,512,128]{2,1,0:T(8,128)(2,1)} %get-tuple-element.27.refs_6_) | copy-start | bytes 1572868
  52.3 13.8 %copy-start.4 = (f32[4,512,128]{2,1,0:T(8,128)S(1)}, f32[4,512,128]{2,1,0:T(8,128)}, u32[]{:S(2)}) copy-start(f32[4,512,128]{2,1,0:T(8,128)} %get-tuple-element.34.refs_10_) | copy-start | bytes 3145732
  52.3 13.8 %copy-start.5 = (f32[4,512,128]{2,1,0:T(8,128)S(1)}, f32[4,512,128]{2,1,0:T(8,128)}, u32[]{:S(2)}) copy-start(f32[4,512,128]{2,1,0:T(8,128)} %get-tuple-element.33.refs_9_) | copy-start | bytes 3145732
  52.3 13.8 %copy-start.6 = (f32[128]{0:T(128)S(1)}, f32[128]{0:T(128)}, u32[]{:S(2)}) copy-start(f32[128]{0:T(128)} %param.21) | copy-start | bytes 1540
  59.8 6.3 %collective-permute-start.11 = (bf16[1,512,128]{2,1,0:T(8,128)(2,1)S(1)}, bf16[1,512,128]{2,1,0:T(8,128)(2,1)S(1)}, u32[]{:S(2)}, u32[]{:S(2)}) collective-permute-start(bf16[1,512,128]{2,1,0:T(8,128)(2,1)S(1)} %get-tuple-element.37), channel_id=1, source_target_pairs={{1,2},{3,4},{5,6},{2,1},{4,3},{6,5},{9,10},{11,12},{13,14},{10,9},... | collective-permute-start | bytes 393224 | tf_op jit(solution)/shard_map/ppermute | solution.py:441
  63.3 2.8 %collective-permute-start.10 = (bf16[1,512,128]{2,1,0:T(8,128)(2,1)S(1)}, bf16[1,512,128]{2,1,0:T(8,128)(2,1)S(1)}, u32[]{:S(2)}, u32[]{:S(2)}) collective-permute-start(bf16[1,512,128]{2,1,0:T(8,128)(2,1)S(1)} %get-tuple-element.38), channel_id=1, source_target_pairs={{0,1},{1,0},{2,3},{3,2},{4,5},{5,4},{6,7},{7,6},{8,9},{9,8},{10,11... | collective-permute-start | bytes 393224 | tf_op jit(solution)/shard_map/ppermute | solution.py:440

commit v3 on v2

--- a/solution.py
+++ b/solution.py
@@ -10,9 +10,11 @@
 
 epsilon = 1e-06
 vmem_bytes = 28 * 1024 * 1024
+near_vmem_bytes = 44 * 1024 * 1024
 whole_vmem_bytes = 56 * 1024 * 1024
 in_vmem = pl.BlockSpec(memory_space=pltpu.VMEM)
 in_smem = pl.BlockSpec(memory_space=pltpu.SMEM)
+no_cost = pl.CostEstimate(flops=0, bytes_accessed=0, transcendentals=0)
 anywhere = pl.BlockSpec(memory_space=pl.ANY)
 
 
@@ -195,6 +197,7 @@
             pltpu.SemaphoreType.DMA((rows + 11,)),
         ],
         compiler_params=pltpu.CompilerParams(vmem_limit_bytes=whole_vmem_bytes),
+        cost_estimate=no_cost,
         name="residual_middle",
     )(*operands)
 
@@ -202,7 +205,7 @@
 def edge_body(
     cells, mate, cross, one, two, state_one, query_weight, key_weight, tempers, gain,
     state_out, norm_out, query_out,
-    held, mate_held, cross_held, one_held, two_held, state_held, query_held, key_held,
+    held, one_held, two_held, state_held, query_held, key_held,
     tempers_held, gain_held, w1, w2, state_two, norm, query, x1, x2, sems,
 ):
     rows = cells.shape[0]
@@ -212,8 +215,6 @@
     loads = [
         copies.start(cells.at[pl.ds(0, 2)], held.at[pl.ds(0, 2)]),
         copies.start(cells.at[pl.ds(rows - 2, 2)], held.at[pl.ds(2, 2)]),
-        copies.start(mate, mate_held),
-        copies.start(cross, cross_held),
     ]
     later = [
         copies.start(one, one_held),
@@ -233,8 +234,8 @@
         place(silu(held[2 + r]), x1, 4 + r)
     outside = []
     for r in range(2):
-        mate_row = mate_held[r].astype(jnp.float32)
-        cross_row = cross_held[r].astype(jnp.float32)
+        mate_row = mate[r].astype(jnp.float32)
+        cross_row = cross[r].astype(jnp.float32)
         over = jnp.where(first_band, 0.0, jnp.where(odd, mate_row, cross_row))
         under = jnp.where(last_band, 0.0, jnp.where(odd, cross_row, mate_row))
         place(silu(over), x1, r)
@@ -284,7 +285,7 @@
     )
     return pl.pallas_call(
         edge_body,
-        in_specs=[anywhere] * 10,
+        in_specs=[anywhere] + [in_vmem] * 2 + [anywhere] * 7,
         out_specs=[anywhere] * 3,
         out_shape=[
             jax.ShapeDtypeStruct((4, *row), jnp.float32),
@@ -292,7 +293,7 @@
             jax.ShapeDtypeStruct((4, *row), jnp.bfloat16),
         ],
         scratch_shapes=[
-            *scratch(((4, *row), jnp.float32), *[(a.shape, a.dtype) for a in operands[1:]]),
+            *scratch(((4, *row), jnp.float32), *[(a.shape, a.dtype) for a in operands[3:]]),
             *scratch(
                 packed,
                 packed,
@@ -305,6 +306,7 @@
             pltpu.SemaphoreType.DMA((14,)),
         ],
         compiler_params=pltpu.CompilerParams(vmem_limit_bytes=whole_vmem_bytes),
+        cost_estimate=no_cost,
         name="residual_edge",
     )(*operands)
 
@@ -339,18 +341,11 @@
     return picked
 
 
-def gather_keys(chosen, edges, middles, mate, cross, keys):
-    rows = keys.shape[0] - 2
-    first_band, last_band, odd = band_place()
-    above = jnp.where(odd, mate[0], cross[0])
-    below = jnp.where(odd, cross[0], mate[0])
-    keys[0] = jnp.where(first_band, jnp.zeros_like(above), above)
-    keys[rows + 1] = jnp.where(last_band, jnp.zeros_like(below), below)
-    for r in range(2):
-        keys[1 + r] = pick(chosen, [edge[r] for edge in edges])
-        keys[rows - 1 + r] = pick(chosen, [edge[2 + r] for edge in edges])
-    for r in range(rows - 4):
-        keys[3 + r] = pick(chosen, [middle[r] for middle in middles])
+def key_offset(partners, low, far):
+    view = lax.axis_index("view")
+    first = jnp.bitwise_xor(partners[view, 0], view)
+    second = jnp.bitwise_xor(partners[view, 1], view)
+    return (jnp.maximum(first, second) if far else jnp.minimum(first, second)) - low
 
 
 def band_row(edge, middle, r):
@@ -362,58 +357,209 @@
     return edge.at[r - inner]
 
 
-def attend_near_body(count, chosen, *refs):
-    edges, middles = refs[:count], refs[count : 2 * count]
-    mate, cross, query_edge, query_middle, out, keys = refs[2 * count :]
+def picked_row(chosen, edges, middles, r):
+    return pick(chosen, [band_row(e, m, r)[...] for e, m in zip(edges, middles)])
+
+
+def finish(r, both, state, value_out, gain, result):
+    message = jnp.dot(both[r], value_out[...], preferred_element_type=jnp.float32)
+    result[r] = state[...] + scaled(message, gain[...])
+
+
+def take(refs, *counts):
+    groups = []
+    for count in counts:
+        groups.append(refs[:count])
+        refs = refs[count:]
+    return (*groups, refs)
+
+
+def gather_keys(chosen, edges, middles, keys):
+    for r in range(keys.shape[0]):
+        keys[r] = pick(chosen, [band_row(e, m, r)[...] for e, m in zip(edges, middles)])
+
+
+def attend_near_body(low, count, partners, *refs):
+    edges, middles, refs = take(refs, count, count)
+    query_edge, query_middle, out, keys, held_edge, held_middle, sems = refs
+    rows, columns, channels = keys.shape
+    copies = Copies(sems)
+    loads = [copies.start(query_edge, held_edge), copies.start(query_middle, held_middle)]
+    gather_keys(key_offset(partners, low, False), edges, middles, keys)
+    for load in loads:
+        load.wait()
+    for r in range(1, rows - 1):
+        window = keys[r - 1 : r + 2].reshape(3 * columns, channels)
+
+        def store(place, value, r=r):
+            out[r - 1, place] = value.astype(jnp.bfloat16)
+
+        blend(band_row(held_edge, held_middle, r), window, store)
+
+
+def attend_far_body(low, count, partners, *refs):
+    edges, middles, refs = take(refs, count, count)
+    (
+        query_edge, query_middle, near, state_edge, state_middle, value_out, gain,
+        out, keys, both, result, sems,
+    ) = refs
     rows, columns, channels = out.shape
-    gather_keys(chosen[0], edges, middles, mate, cross, keys)
-    for r in range(rows):
-        window = keys[r : r + 3].reshape(3 * columns, channels)
+    copies = Copies(sems)
+    gather_keys(key_offset(partners, low, True), edges, middles, keys)
+    for r in range(1, rows - 1):
+        window = keys[r - 1 : r + 2].reshape(3 * columns, channels)
 
         def store(place, value, r=r):
-            out[r, place] = value.astype(jnp.bfloat16)
+            other = near[r - 1, place].astype(jnp.float32)
+            both[r, place] = (value + other).astype(jnp.bfloat16)
 
         blend(band_row(query_edge, query_middle, r), window, store)
-
-
-def attend_far_body(count, chosen, *refs):
-    edges, middles = refs[:count], refs[count : 2 * count]
-    (
-        mate, cross, query_edge, query_middle, near, state_edge, state_middle, value_out, gain,
-        out, keys, both,
-    ) = refs[2 * count :]
-    rows, columns, channels = out.shape
-    gather_keys(chosen[0], edges, middles, mate, cross, keys)
-    for r in range(rows):
-        window = keys[r : r + 3].reshape(3 * columns, channels)
-
-        def store(place, value, r=r):
-            both[r, place] = (value + near[r, place].astype(jnp.float32)).astype(jnp.bfloat16)
-
-        blend(band_row(query_edge, query_middle, r), window, store)
-    for r in range(rows):
-        message = jnp.dot(both[r], value_out[...], preferred_element_type=jnp.float32)
-        state = band_row(state_edge, state_middle, r)[...]
-        out[r] = state + scaled(message, gain[...])
-
-
-def attend(body, name, chosen, edges, middles, mate, cross, queries, rest, out_type, extra):
-    query_edge, query_middle = queries
-    rows = query_edge.shape[0] + query_middle.shape[0]
-    columns, channels = query_edge.shape[1:]
-    operands = [*edges, *middles, mate, cross, *queries, *rest]
+    for r in range(1, rows - 1):
+        finish(r, both, band_row(state_edge, state_middle, r), value_out, gain, result)
+    inner = pl.ds(1, rows - 2)
+    copies.start(result.at[inner], out.at[inner]).wait()
+
+
+def attend_outer_body(lows, counts, partners, *refs):
+    near_count, far_count = counts
+    near_edges, near_above, near_below, refs = take(refs, *[near_count] * 3)
+    far_edges, far_above, far_below, refs = take(refs, *[far_count] * 3)
+    query_edge, state_edge, value_out, gain, given, out, keys, both, result, sems = refs
+    columns, channels = both.shape[1:]
+    copies = Copies(sems)
+    sides = (
+        (key_offset(partners, lows[0], False), near_edges, near_above, near_below),
+        (key_offset(partners, lows[1], True), far_edges, far_above, far_below),
+    )
+    for slot, (chosen, edges, above, below) in enumerate(sides):
+        keys[6 * slot] = pick(chosen, [a[0] for a in above])
+        keys[6 * slot + 5] = pick(chosen, [b[0] for b in below])
+        for r in range(4):
+            keys[6 * slot + 1 + r] = pick(chosen, [e[r] for e in edges])
+    for slot in range(2):
+        for end in range(2):
+            first = 6 * slot + 3 * end
+            window = keys[first : first + 3].reshape(3 * columns, channels)
+
+            def store(place, value, slot=slot, end=end):
+                if slot > 0:
+                    value = value + both[end, place].astype(jnp.float32)
+                both[end, place] = value.astype(jnp.bfloat16)
+
+            blend(query_edge.at[3 * end], window, store)
+    stores = []
+    for end, r in ((0, 0), (1, out.shape[0] - 1)):
+        finish(end, both, state_edge.at[3 * end], value_out, gain, result)
+        stores.append(copies.start(result.at[end], out.at[r]))
+    for store in stores:
+        store.wait()
+
+
+def attend_near(partners, low, candidates, queries):
+    rows = candidates[0][0].shape[0] + candidates[1][0].shape[0]
+    columns, channels = queries[0].shape[1:]
+    operands = [a for group in candidates for a in group]
     return pl.pallas_call(
-        functools.partial(body, len(edges)),
+        functools.partial(attend_near_body, low, len(candidates[0])),
+        in_specs=[in_smem] + [in_vmem] * len(operands) + [anywhere] * 2,
+        out_specs=in_vmem,
+        out_shape=jax.ShapeDtypeStruct((rows - 2, columns, channels), jnp.bfloat16),
+        scratch_shapes=[
+            pltpu.VMEM((rows, columns, channels), jnp.bfloat16),
+            pltpu.VMEM(queries[0].shape, jnp.bfloat16),
+            pltpu.VMEM(queries[1].shape, jnp.bfloat16),
+            pltpu.SemaphoreType.DMA((2,)),
+        ],
+        compiler_params=pltpu.CompilerParams(vmem_limit_bytes=near_vmem_bytes),
+        cost_estimate=no_cost,
+        name="attend_near",
+    )(partners, *operands, *queries)
+
+
+def attend_far(partners, low, candidates, queries, near, states, value_out, gain):
+    shape = (near.shape[0] + 2, *near.shape[1:])
+    operands = [a for group in candidates for a in group]
+    operands += [*queries, near, *states, value_out, gain]
+    return pl.pallas_call(
+        functools.partial(attend_far_body, low, len(candidates[0])),
         in_specs=[in_smem] + [in_vmem] * len(operands),
-        out_specs=in_vmem,
-        out_shape=jax.ShapeDtypeStruct((rows, columns, channels), out_type),
+        out_specs=anywhere,
+        out_shape=jax.ShapeDtypeStruct(shape, jnp.float32),
         scratch_shapes=[
-            pltpu.VMEM((rows + 2, columns, channels), jnp.bfloat16),
-            *[pltpu.VMEM((rows, columns, channels), kind) for kind in extra],
+            pltpu.VMEM(shape, jnp.bfloat16),
+            pltpu.VMEM(shape, jnp.bfloat16),
+            pltpu.VMEM(shape, jnp.float32),
+            pltpu.SemaphoreType.DMA((1,)),
         ],
         compiler_params=pltpu.CompilerParams(vmem_limit_bytes=vmem_bytes),
-        name=name,
-    )(chosen, *operands)
+        cost_estimate=no_cost,
+        name="attend_far",
+    )(partners, *operands)
+
+
+def attend_outer(partners, lows, near_sides, far_sides, query, state, value_out, gain, given):
+    columns, channels = query.shape[1:]
+    operands = [a for group in near_sides + far_sides for a in group]
+    operands += [query, state, value_out, gain]
+    return pl.pallas_call(
+        functools.partial(attend_outer_body, lows, (len(near_sides[0]), len(far_sides[0]))),
+        in_specs=[in_smem] + [in_vmem] * len(operands) + [anywhere],
+        out_specs=anywhere,
+        out_shape=jax.ShapeDtypeStruct(given.shape, given.dtype),
+        scratch_shapes=[
+            pltpu.VMEM((12, columns, channels), jnp.bfloat16),
+            pltpu.VMEM((2, columns, channels), jnp.bfloat16),
+            pltpu.VMEM((2, columns, channels), jnp.float32),
+            pltpu.SemaphoreType.DMA((2,)),
+        ],
+        input_output_aliases={1 + len(operands): 0},
+        compiler_params=pltpu.CompilerParams(vmem_limit_bytes=vmem_bytes),
+        cost_estimate=no_cost,
+        name="attend_outer",
+    )(partners, *operands, given)
+
+
+def edge_halos_body(*refs):
+    edges, (mate, cross) = refs[:-2], refs[-2:]
+    odd = band_place()[2]
+    for i, edge in enumerate(edges):
+        mate[i] = jnp.where(odd, edge[0], edge[3])
+        cross[i] = jnp.where(odd, edge[3], edge[0])
+
+
+def edge_halos(edges):
+    rows = jax.ShapeDtypeStruct((len(edges), *edges[0].shape[1:]), jnp.bfloat16)
+    return pl.pallas_call(
+        edge_halos_body,
+        in_specs=[in_vmem] * len(edges),
+        out_specs=[in_vmem] * 2,
+        out_shape=[rows, rows],
+        compiler_params=pltpu.CompilerParams(vmem_limit_bytes=vmem_bytes),
+        cost_estimate=no_cost,
+        name="edge_halos",
+    )(*edges)
+
+
+def outside_body(mate, cross, *outs):
+    first_band, last_band, odd = band_place()
+    for i in range(mate.shape[0]):
+        above = jnp.where(odd, mate[i], cross[i])
+        below = jnp.where(odd, cross[i], mate[i])
+        outs[2 * i][0] = jnp.where(first_band, jnp.zeros_like(above), above)
+        outs[2 * i + 1][0] = jnp.where(last_band, jnp.zeros_like(below), below)
+
+
+def outside_rows(mate, cross):
+    row = jax.ShapeDtypeStruct((1, *mate.shape[1:]), jnp.bfloat16)
+    return pl.pallas_call(
+        outside_body,
+        in_specs=[in_vmem] * 2,
+        out_specs=[in_vmem] * (2 * mate.shape[0]),
+        out_shape=[row] * (2 * mate.shape[0]),
+        compiler_params=pltpu.CompilerParams(vmem_limit_bytes=vmem_bytes),
+        cost_estimate=no_cost,
+        name="outside_rows",
+    )(mate, cross)
 
 
 def swap(cells, views, offset):
@@ -424,22 +570,18 @@
     return {1 << i: swap(cells, views, 1 << i) for i in range((views - 1).bit_length())}
 
 
-def gather_relayed(edges, middles, views):
+def relay(held, views, by_low):
     for offset in range(1, views):
-        low = offset & -offset
-        high = 1 << (offset.bit_length() - 1)
-        if low != high:
-            edges[offset] = swap(edges[offset ^ high], views, high)
-            middles[offset] = swap(middles[offset ^ low], views, low)
-
-
-def swap_bands(head, tail, odd, bands):
+        bit = offset & -offset if by_low else 1 << (offset.bit_length() - 1)
+        if bit != offset:
+            held[offset] = swap(held[offset ^ bit], views, bit)
+
+
+def swap_bands(mate, cross, bands):
     mates = [(i, i ^ 1) for i in range(bands)]
     crosses = [(i, i + 1) for i in range(1, bands - 1, 2)]
     crosses = crosses + [(j, i) for i, j in crosses]
-    mate = lax.ppermute(jnp.where(odd, head, tail), "band", mates)
-    cross = lax.ppermute(jnp.where(odd, tail, head), "band", crosses)
-    return mate, cross
+    return lax.ppermute(mate, "band", mates), lax.ppermute(cross, "band", crosses)
 
 
 def per_device(
@@ -448,52 +590,51 @@
 ):
     views = lax.axis_size("view")
     bands = lax.axis_size("band")
-    odd = lax.axis_index("band") % 2 > 0
-    view = lax.axis_index("view")
     cells, temper, gain = features[0], tempers[0], norm_gain[None]
-    rows = cells.shape[0]
 
     state_one, state_middle, middle, query_middle = middle_rows(
         cells, conv_one, conv_two, query_weight, key_weight, temper, gain
     )
     middles = gather_direct(middle, views)
-    head, tail = cells[:2].astype(jnp.bfloat16), cells[rows - 2 :].astype(jnp.bfloat16)
-    mate, cross = swap_bands(head, tail, odd, bands)
+    head, tail = cells[:2].astype(jnp.bfloat16), cells[-2:].astype(jnp.bfloat16)
+    odd = band_place()[2]
+    mate, cross = swap_bands(
+        jnp.where(odd, head, tail), jnp.where(odd, tail, head), bands
+    )
     state_edge, edge, query_edge = edge_rows(
         cells, mate, cross, conv_one, conv_two, state_one, query_weight, key_weight, temper, gain
     )
     queries = (query_edge, query_middle)
     edges = gather_direct(edge, views)
     edges, middles = lax.optimization_barrier((edges, middles))
-    gather_relayed(edges, middles, views)
+    direct = list(edges)
+    halos = swap_bands(*edge_halos([edges[i] for i in direct]), bands)
+    relay(edges, views, False)
+    relay(middles, views, True)
+
+    def candidates(groups, low, high):
+        return [[group[i] for i in range(low, high + 1)] for group in groups]
+
+    near_ends, far_ends = (1, max(1, views - 2)), (min(2, views - 1), views - 1)
+    near = attend_near(partners, near_ends[0], candidates((edges, middles), *near_ends), queries)
+    halos, near = lax.optimization_barrier((halos, near))
+    halos = outside_rows(*halos)
+    above = dict(zip(direct, halos[0::2]))
+    below = dict(zip(direct, halos[1::2]))
+    relay(above, views, True)
+    relay(below, views, False)
     value_out = jnp.dot(value_weight, out_weight, preferred_element_type=jnp.float32).astype(
         jnp.bfloat16
     )
-
-    offsets = jnp.bitwise_xor(lax.dynamic_index_in_dim(partners, view, 0, keepdims=False), view)
-
-    def keys_of(offset, low, high, after=None):
-        chosen = offset - low
-        some_edges = [edges[i] for i in range(low, high + 1)]
-        some_middles = [middles[i] for i in range(low, high + 1)]
-        if after is not None:
-            some_edges, some_middles, after = lax.optimization_barrier(
-                (some_edges, some_middles, after)
-            )
-        tail = pick(chosen, [e[-1:] for e in some_edges])
-        head = pick(chosen, [e[:1] for e in some_edges])
-        halos = swap_bands(head, tail, odd, bands)
-        return chosen[None], some_edges, some_middles, *halos
-
-    near_keys = keys_of(jnp.min(offsets), 1, max(1, views - 2))
-    near_blend = attend(
-        attend_near_body, "attend_near", *near_keys, queries, (), jnp.bfloat16, []
-    )
-    far_keys = keys_of(jnp.max(offsets), min(2, views - 1), views - 1, near_blend)
-    refined = attend(
-        attend_far_body, "attend_far", *far_keys, queries,
-        (near_blend, state_edge, state_middle, value_out, message_gain[None]), jnp.float32,
-        [jnp.bfloat16],
+    rest = (value_out, message_gain[None])
+    inner = attend_far(
+        partners, far_ends[0], candidates((edges, middles), *far_ends), queries, near,
+        (state_edge, state_middle), *rest,
+    )
+    sides = (edges, above, below)
+    refined = attend_outer(
+        partners, (near_ends[0], far_ends[0]), candidates(sides, *near_ends),
+        candidates(sides, *far_ends), query_edge, state_edge, *rest, inner,
     )
     return refined[None]
 

time: 76.7 us -> 72.1 us (0.940)
  waiting for transfers between devices: 19.9 us -> 13.4 us
  Pallas kernels: 31.4 us -> 37.4 us
  other arithmetic: 3.35 us -> 1.8 us
  starting transfers between devices: 18.2 us -> 16.7 us
  between operations: 1.53 us -> 0.37 us
    pallas_call x3 -> x6, Pallas kernels: 24.2 us -> 30.2 us  [the longest x1 8.43 us: attend_far(): pl.pallas_call(functools.partial(attend_far_body, low, len(candidates[0])...]
    ppermute x6 -> x4, waiting for transfers between devices: 4.89 us -> 0.01 us  [the longest x2 0.01 us: swap_bands(): lax.ppermute(cross, 'band', crosses)]
    ppermute x6 -> x4, starting transfers between devices: 13.6 us -> 10.7 us  [the longest x2 10.1 us: swap_bands(): lax.ppermute(cross, 'band', crosses)]
    ppermute x6 -> x8, waiting for transfers between devices: 15 us -> 13.4 us  [swap(): return lax.ppermute(cells, 'view', [(i, i ^ offset) for i in range(views)])]
    ppermute x6 -> x8, starting transfers between devices: 4.6 us -> 6.06 us  [swap(): return lax.ppermute(cells, 'view', [(i, i ^ offset) for i in range(views)])]
    reduce_min x1 -> x0, other arithmetic: 0.79 us -> none  [per_device(): near_keys = keys_of(jnp.min(offsets), 1, max(1, views - 2))]
    unnamed x22 -> x21, local copies, waits for them, and re-layouts: 1.85 us -> 1.95 us
  transfers between devices with their start and end apart: 12 -> 12, of which waited for: 6 -> 4; matrix products, arithmetic and copies ran while one was open for 2% -> 0% of each run, Pallas kernels for 28% -> 44%
where the time goes in v3:
time: 72.1 us; the launch traced here: 71.8 us
  Pallas kernels  37.4 us (52%)
  starting transfers between devices  16.7 us (23%)
  waiting for transfers between devices  13.4 us (19%)
  local copies, waits for them, and re-layouts  1.95 us (3%)
  other arithmetic  1.8 us (2%)
    ppermute x8, waiting for transfers between devices, swap(): return lax.ppermute(cells, 'view', [(i, i ^ offset) for i in range(views)])  13.4 us
    ppermute x2, starting transfers between devices, swap_bands(): lax.ppermute(cross, 'band', crosses)  10.1 us
    pallas_call x1, Pallas kernels, attend_far(): pl.pallas_call(functools.partial(attend_far_body, low, len(candidates[0])...  8.43 us
    pallas_call x1, Pallas kernels, edge_rows(): pl.pallas_call(edge_body, in_specs=[anywhere] + [in_vmem] * 2 + [anywhere...  7.47 us
    pallas_call x1, Pallas kernels, middle_rows(): pl.pallas_call(middle_body, in_specs=[anywhere] * 7, out_specs=[anywhere]...  7.16 us
    pallas_call x1, Pallas kernels, attend_near(): pl.pallas_call(functools.partial(attend_near_body, low, len(candidates[0]...  6.73 us
    ppermute x8, starting transfers between devices, swap(): return lax.ppermute(cells, 'view', [(i, i ^ offset) for i in range(views)])  6.06 us
    pallas_call x1, Pallas kernels, attend_outer(): pl.pallas_call(functools.partial(attend_outer_body, lows, (len(near_sides...  5.63 us
  transfers between devices with their start and end apart: 12, of which 4 were waited for; matrix products, arithmetic and copies ran while one was open for 0% of the time, Pallas kernels for 44%

profile of v3, /device:TPU:1, one launch (start us, length us, event | category | flops | bytes accessed | tf_op | source)
XLA Modules:
  0.0 71.8 jit_solution(11340512172827939518)
XLA Ops:
  0.0 0.0 copy-start
  0.0 1.8 %convert.4 = bf16[1,8,512,128]{3,2,1,0:T(8,128)(2,1)S(1)} convert(f32[1,8,512,128]{3,2,1,0:T(8,128)} %param.11) | non-fusion elementwise | flops 524288 | bytes 3145728 | tf_op jit(solution)/shard_map/convert.1
  1.8 0.1 collective-permute-start
  1.9 4.6 %collective-permute-start.1 = (bf16[2,512,128]{2,1,0:T(8,128)(2,1)S(1)}, bf16[2,512,128]{2,1,0:T(8,128)(2,1)S(1)}, u32[]{:S(2)}, u32[]{:S(2)}) collective-permute-start(bf16[2,512,128]{2,1,0:T(8,128)(2,1)S(1)} %get-tuple-element.45), channel_id=1, source_target_pairs={{1,2},{3,4},{5,6},{2,1},{4,3},{6,5},{9,10},{11,12},{13,14},{10,9},... | collective-permute-start | bytes 786440 | tf_op jit(solution)/shard_map/ppermute | solution.py:584
  6.5 7.2 %residual_middle.1 = (f32[4,512,128]{2,1,0:T(8,128)}, f32[4,512,128]{2,1,0:T(8,128)}, bf16[4,512,128]{2,1,0:T(8,128)(2,1)}, bf16[4,512,128]{2,1,0:T(8,128)(2,1)}) custom-call(f32[8,512,128]{2,1,0:T(8,128)} %bitcast.13, bf16[3,3,128,128]{3,2,1,0:T(8,128)(2,1)} %one.3, bf16[3,3,128,128]{3,2,1,0:T(8,128)(2,1)} %two.3, bf16[128,128]{1,0:T(8,128)(2,1)} %query_weight.3, ...), custom_call_target="tpu_custom_call" | custom-call | tf_op jit(solution)/shard_map/residual_middle/pallas_call | solution.py:175
  13.7 1.3 %collective-permute-start.4 = (bf16[4,512,128]{2,1,0:T(8,128)(2,1)}, bf16[4,512,128]{2,1,0:T(8,128)(2,1)S(1)}, u32[]{:S(2)}, u32[]{:S(2)}) collective-permute-start(bf16[4,512,128]{2,1,0:T(8,128)(2,1)} %get-tuple-element.27), channel_id=1, source_target_pairs={{0,8},{8,0},{16,24},{24,16},{1,9},{9,1},{17,25},{25,17},{2,10},{10... | collective-permute-start | bytes 1572872 | tf_op jit(solution)/shard_map/ppermute | solution.py:566
  14.9 1.2 %collective-permute-start.5 = (bf16[4,512,128]{2,1,0:T(8,128)(2,1)}, bf16[4,512,128]{2,1,0:T(8,128)(2,1)S(1)}, u32[]{:S(2)}, u32[]{:S(2)}) collective-permute-start(bf16[4,512,128]{2,1,0:T(8,128)(2,1)} %get-tuple-element.27), channel_id=1, source_target_pairs={{0,16},{8,24},{16,0},{24,8},{1,17},{9,25},{17,1},{25,9},{2,18},{10... | collective-permute-start | bytes 1572872 | tf_op jit(solution)/shard_map/ppermute | solution.py:566
  16.2 0.0 collective-permute-done.mate
  16.2 0.0 copy-start.6
  16.2 0.0 collective-permute-done.1.cross
  16.2 0.0 copy-start.7
  16.2 0.7 copy-done.6
  16.9 0.1 copy-done.7
  17.0 0.0 copy-start.9
  17.0 7.5 %residual_edge.1 = (f32[4,512,128]{2,1,0:T(8,128)}, bf16[4,512,128]{2,1,0:T(8,128)(2,1)}, bf16[4,512,128]{2,1,0:T(8,128)(2,1)}) custom-call(f32[8,512,128]{2,1,0:T(8,128)} %bitcast.14, bf16[2,512,128]{2,1,0:T(8,128)(2,1)} %copy-done.6, bf16[2,512,128]{2,1,0:T(8,128)(2,1)} %copy-done.7, bf16[3,3,128,128]{3,2,1,0:T(8,128)(2,1)} %one.3, ...), custom_call_target="tpu_custom_call" | custom-call | tf_op jit(solution)/shard_map/residual_edge/pallas_call | solution.py:286
  24.5 0.3 collective-permute-start.2
  24.8 0.2 collective-permute-start.3
  25.0 0.8 %collective-permute-done.4.refs_2_ = bf16[4,512,128]{2,1,0:T(8,128)(2,1)S(1)} collective-permute-done((bf16[4,512,128]{2,1,0:T(8,128)(2,1)}, bf16[4,512,128]{2,1,0:T(8,128)(2,1)S(1)}, u32[]{:S(2)}, u32[]{:S(2)}) %collective-permute-start.4) | collective-permute-done | bytes 524320 | tf_op jit(solution)/shard_map/ppermute | solution.py:566
  25.8 2.5 %collective-permute-done.5.refs_3_.refs_2_ = bf16[4,512,128]{2,1,0:T(8,128)(2,1)S(1)} collective-permute-done((bf16[4,512,128]{2,1,0:T(8,128)(2,1)}, bf16[4,512,128]{2,1,0:T(8,128)(2,1)S(1)}, u32[]{:S(2)}, u32[]{:S(2)}) %collective-permute-start.5) | collective-permute-done | bytes 524320 | tf_op jit(solution)/shard_map/ppermute | solution.py:566
  28.3 9.0 %collective-permute-done.2.refs_0_ = bf16[4,512,128]{2,1,0:T(8,128)(2,1)S(1)} collective-permute-done((bf16[4,512,128]{2,1,0:T(8,128)(2,1)}, bf16[4,512,128]{2,1,0:T(8,128)(2,1)S(1)}, u32[]{:S(2)}, u32[]{:S(2)}) %collective-permute-start.2) | collective-permute-done | bytes 524320 | tf_op jit(solution)/shard_map/ppermute | solution.py:566
  37.3 1.1 %collective-permute-done.3.refs_1_.refs_0_.refs_6_ = bf16[4,512,128]{2,1,0:T(8,128)(2,1)S(1)} collective-permute-done((bf16[4,512,128]{2,1,0:T(8,128)(2,1)}, bf16[4,512,128]{2,1,0:T(8,128)(2,1)S(1)}, u32[]{:S(2)}, u32[]{:S(2)}) %collective-permute-start.3) | collective-permute-done | bytes 524320 | tf_op jit(solution)/shard_map/ppermute | solution.py:566
  38.4 0.4 collective-permute-start.11
  38.8 1.1 %collective-permute-start.8 = (bf16[4,512,128]{2,1,0:T(8,128)(2,1)S(1)}, bf16[4,512,128]{2,1,0:T(8,128)(2,1)S(1)}, u32[]{:S(2)}, u32[]{:S(2)}) collective-permute-start(bf16[4,512,128]{2,1,0:T(8,128)(2,1)S(1)} %collective-permute-done.2.refs_0_), channel_id=1, source_target_pairs={{0,16},{8,24},{16,0},{24,8},{1,17},{9,25},{17,1},{25,9},{2,18},{10... | collective-permute-start | bytes 1572872 | tf_op jit(solution)/shard_map/ppermute | solution.py:566
  39.9 0.9 %edge_halos.1 = (bf16[2,512,128]{2,1,0:T(8,128)(2,1)}, bf16[2,512,128]{2,1,0:T(8,128)(2,1)}) custom-call(bf16[4,512,128]{2,1,0:T(8,128)(2,1)S(1)} %collective-permute-done.2.refs_0_, bf16[4,512,128]{2,1,0:T(8,128)(2,1)S(1)} %collective-permute-done.3.refs_1_.refs_0_.refs_6_), custom_call_target="tpu_custom_call" | custom-call | tf_op jit(solution)/shard_map/edge_halos/pallas_call | solution.py:532
  40.7 0.4 collective-permute-start.6
  41.2 5.6 %collective-permute-start.7 = (bf16[2,512,128]{2,1,0:T(8,128)(2,1)}, bf16[2,512,128]{2,1,0:T(8,128)(2,1)}, u32[]{:S(2)}, u32[]{:S(2)}) collective-permute-start(bf16[2,512,128]{2,1,0:T(8,128)(2,1)} %get-tuple-element.31), channel_id=1, source_target_pairs={{1,2},{3,4},{5,6},{2,1},{4,3},{6,5},{9,10},{11,12},{13,14},{10,9},... | collective-permute-start | bytes 786440 | tf_op jit(solution)/shard_map/ppermute | solution.py:584
  46.8 0.0 copy-done.9
  46.8 0.1 copy.15.partners
  46.9 0.0 copy-done.3
  46.9 1.0 %copy-done.1 = bf16[4,512,128]{2,1,0:T(8,128)(2,1)S(1)} copy-done((bf16[4,512,128]{2,1,0:T(8,128)(2,1)S(1)}, bf16[4,512,128]{2,1,0:T(8,128)(2,1)}, u32[]{:S(2)}) %copy-start.1) | copy-done | bytes 524312
  47.9 6.7 %attend_near.1.refs_6_ = bf16[6,512,128]{2,1,0:T(8,128)(2,1)S(1)} custom-call(s32[4,2]{1,0:T(4,128)S(1)} %copy.15.partners, bf16[4,512,128]{2,1,0:T(8,128)(2,1)S(1)} %collective-permute-done.2.refs_0_, bf16[4,512,128]{2,1,0:T(8,128)(2,1)S(1)} %collective-permute-done.3.refs_1_.refs_0_.refs_6_, bf16[4,512,128]{2,1,0:T(8,128)(2,1)S(1)} %collective-permute-done.4.refs_2_, ...), custom_call_target="tpu_custom_call" | custom-call | tf_op jit(solution)/shard_map/attend_near/pallas_call | solution.py:462
  54.7 0.0 collective-permute-done.6.mate
  54.7 0.0 collective-permute-done.7.cross
  54.7 1.1 %outside_rows.1 = (bf16[1,512,128]{2,1,0:T(8,128)(2,1)S(1)}, bf16[1,512,128]{2,1,0:T(8,128)(2,1)S(1)}, bf16[1,512,128]{2,1,0:T(8,128)(2,1)S(1)}, bf16[1,512,128]{2,1,0:T(8,128)(2,1)S(1)}) custom-call(bf16[2,512,128]{2,1,0:T(8,128)(2,1)S(1)} %collective-permute-done.6.mate, bf16[2,512,128]{2,1,0:T(8,128)(2,1)} %collective-permute-done.7.cross), custom_call_target="tpu_custom_call" | custom-call | tf_op jit(solution)/shard_map/outside_rows/pallas_call | solution.py:554
  55.8 0.1 collective-permute-start.10
  55.9 1.4 %collective-permute-start.9 = (bf16[1,512,128]{2,1,0:T(8,128)(2,1)S(1)}, bf16[1,512,128]{2,1,0:T(8,128)(2,1)S(1)}, u32[]{:S(2)}, u32[]{:S(2)}) collective-permute-start(bf16[1,512,128]{2,1,0:T(8,128)(2,1)S(1)} %get-tuple-element.39.refs_3_.refs_8_), channel_id=1, source_target_pairs={{0,8},{8,0},{16,24},{24,16},{1,9},{9,1},{17,25},{25,17},{2,10},{10... | collective-permute-start | bytes 393224 | tf_op jit(solution)/shard_map/ppermute | solution.py:566
  57.3 0.0 copy-done
  57.3 0.0 copy-done.8
  57.3 0.1 convolution_convert_fusion.refs_9_.refs_14_
  57.4 0.0 collective-permute-done.11.refs_3_
  57.4 0.0 collective-permute-done.8.refs_1_.refs_7_
  57.5 0.0 copy-done.2
  57.5 0.0 copy-done.4
  57.5 0.0 copy-done.5
  57.5 8.4 %attend_far.1.refs_16_ = f32[8,512,128]{2,1,0:T(8,128)} custom-call(s32[4,2]{1,0:T(4,128)S(1)} %copy.15.partners, bf16[4,512,128]{2,1,0:T(8,128)(2,1)S(1)} %collective-permute-done.3.refs_1_.refs_0_.refs_6_, bf16[4,512,128]{2,1,0:T(8,128)(2,1)S(1)} %collective-permute-done.8.refs_1_.refs_7_, bf16[4,512,128]{2,1,0:T(8,128)(2,1)S(1)} %collective-permute-done.5.refs_3_.refs_2_, ...), custom_call_target="tpu_custom_call" | custom-call | tf_op jit(solution)/shard_map/attend_far/pallas_call | solution.py:483
  65.9 0.0 collective-permute-done.10.refs_11_
  65.9 0.0 collective-permute-done.9.refs_9_
  65.9 5.6 %attend_outer.1 = f32[8,512,128]{2,1,0:T(8,128)} custom-call(s32[4,2]{1,0:T(4,128)S(1)} %copy.15.partners, bf16[4,512,128]{2,1,0:T(8,128)(2,1)S(1)} %collective-permute-done.2.refs_0_, bf16[4,512,128]{2,1,0:T(8,128)(2,1)S(1)} %collective-permute-done.3.refs_1_.refs_0_.refs_6_, ...), custom_call_target="tpu_custom_call", output_to_operand_aliasing={{}: (17, {})} | custom-call | tf_op jit(solution)/shard_map/attend_outer/pallas_call | solution.py:504
  (7 shorter events, 0.1 us)
Async XLA Ops:
  0.0 57.3 %copy-start = (bf16[128,128]{1,0:T(8,128)(2,1)S(1)}, bf16[128,128]{1,0:T(8,128)(2,1)}, u32[]{:S(2)}) copy-start(bf16[128,128]{1,0:T(8,128)(2,1)} %param.18) | copy-start | bytes 98308
  1.8 14.4 %collective-permute-start = (bf16[2,512,128]{2,1,0:T(8,128)(2,1)S(1)}, bf16[2,512,128]{2,1,0:T(8,128)(2,1)S(1)}, u32[]{:S(2)}, u32[]{:S(2)}) collective-permute-start(bf16[2,512,128]{2,1,0:T(8,128)(2,1)S(1)} %get-tuple-element.46), channel_id=1, source_target_pairs={{0,1},{1,0},{2,3},{3,2},{4,5},{5,4},{6,7},{7,6},{8,9},{9,8},{10,11... | collective-permute-start | bytes 786440 | tf_op jit(solution)/shard_map/ppermute | solution.py:584
  1.9 14.2 %collective-permute-start.1 = (bf16[2,512,128]{2,1,0:T(8,128)(2,1)S(1)}, bf16[2,512,128]{2,1,0:T(8,128)(2,1)S(1)}, u32[]{:S(2)}, u32[]{:S(2)}) collective-permute-start(bf16[2,512,128]{2,1,0:T(8,128)(2,1)S(1)} %get-tuple-element.45), channel_id=1, source_target_pairs={{1,2},{3,4},{5,6},{2,1},{4,3},{6,5},{9,10},{11,12},{13,14},{10,9},... | collective-permute-start | bytes 786440 | tf_op jit(solution)/shard_map/ppermute | solution.py:584
  13.7 12.1 %collective-permute-start.4 = (bf16[4,512,128]{2,1,0:T(8,128)(2,1)}, bf16[4,512,128]{2,1,0:T(8,128)(2,1)S(1)}, u32[]{:S(2)}, u32[]{:S(2)}) collective-permute-start(bf16[4,512,128]{2,1,0:T(8,128)(2,1)} %get-tuple-element.27), channel_id=1, source_target_pairs={{0,8},{8,0},{16,24},{24,16},{1,9},{9,1},{17,25},{25,17},{2,10},{10... | collective-permute-start | bytes 1572872 | tf_op jit(solution)/shard_map/ppermute | solution.py:566
  14.9 13.4 %collective-permute-start.5 = (bf16[4,512,128]{2,1,0:T(8,128)(2,1)}, bf16[4,512,128]{2,1,0:T(8,128)(2,1)S(1)}, u32[]{:S(2)}, u32[]{:S(2)}) collective-permute-start(bf16[4,512,128]{2,1,0:T(8,128)(2,1)} %get-tuple-element.27), channel_id=1, source_target_pairs={{0,16},{8,24},{16,0},{24,8},{1,17},{9,25},{17,1},{25,9},{2,18},{10... | collective-permute-start | bytes 1572872 | tf_op jit(solution)/shard_map/ppermute | solution.py:566
  16.2 0.7 copy-start.6
  16.2 0.8 %copy-start.7 = (bf16[2,512,128]{2,1,0:T(8,128)(2,1)}, bf16[2,512,128]{2,1,0:T(8,128)(2,1)S(1)}, u32[]{:S(2)}) copy-start(bf16[2,512,128]{2,1,0:T(8,128)(2,1)S(1)} %collective-permute-done.1.cross) | copy-start | bytes 786436
  17.0 29.8 %copy-start.9 = (s32[4,2]{0,1:T(2,128)S(1)}, s32[4,2]{0,1:T(2,128)}, u32[]{:S(2)}) copy-start(s32[4,2]{0,1:T(2,128)} %param.13) | copy-start | bytes 100
  17.0 29.9 %copy-start.3 = (bf16[4,512,128]{2,1,0:T(8,128)(2,1)S(1)}, bf16[4,512,128]{2,1,0:T(8,128)(2,1)}, u32[]{:S(2)}) copy-start(bf16[4,512,128]{2,1,0:T(8,128)(2,1)} %get-tuple-element.35.refs_5_) | copy-start | bytes 1572868
  24.5 12.8 %collective-permute-start.2 = (bf16[4,512,128]{2,1,0:T(8,128)(2,1)}, bf16[4,512,128]{2,1,0:T(8,128)(2,1)S(1)}, u32[]{:S(2)}, u32[]{:S(2)}) collective-permute-start(bf16[4,512,128]{2,1,0:T(8,128)(2,1)} %get-tuple-element.26), channel_id=1, source_target_pairs={{0,8},{8,0},{16,24},{24,16},{1,9},{9,1},{17,25},{25,17},{2,10},{10... | collective-permute-start | bytes 1572872 | tf_op jit(solution)/shard_map/ppermute | solution.py:566
  24.8 13.6 %collective-permute-start.3 = (bf16[4,512,128]{2,1,0:T(8,128)(2,1)}, bf16[4,512,128]{2,1,0:T(8,128)(2,1)S(1)}, u32[]{:S(2)}, u32[]{:S(2)}) collective-permute-start(bf16[4,512,128]{2,1,0:T(8,128)(2,1)} %get-tuple-element.26), channel_id=1, source_target_pairs={{0,16},{8,24},{16,0},{24,8},{1,17},{9,25},{17,1},{25,9},{2,18},{10... | collective-permute-start | bytes 1572872 | tf_op jit(solution)/shard_map/ppermute | solution.py:566
  38.4 19.1 %collective-permute-start.11 = (bf16[4,512,128]{2,1,0:T(8,128)(2,1)S(1)}, bf16[4,512,128]{2,1,0:T(8,128)(2,1)}, u32[]{:S(2)}, u32[]{:S(2)}) collective-permute-start(bf16[4,512,128]{2,1,0:T(8,128)(2,1)S(1)} %collective-permute-done.5.refs_3_.refs_2_), channel_id=1, source_target_pairs={{0,8},{8,0},{16,24},{24,16},{1,9},{9,1},{17,25},{25,17},{2,10},{10... | collective-permute-start | bytes 1572872 | tf_op jit(solution)/shard_map/ppermute | solution.py:566
  38.8 18.7 %collective-permute-start.8 = (bf16[4,512,128]{2,1,0:T(8,128)(2,1)S(1)}, bf16[4,512,128]{2,1,0:T(8,128)(2,1)S(1)}, u32[]{:S(2)}, u32[]{:S(2)}) collective-permute-start(bf16[4,512,128]{2,1,0:T(8,128)(2,1)S(1)} %collective-permute-done.2.refs_0_), channel_id=1, source_target_pairs={{0,16},{8,24},{16,0},{24,8},{1,17},{9,25},{17,1},{25,9},{2,18},{10... | collective-permute-start | bytes 1572872 | tf_op jit(solution)/shard_map/ppermute | solution.py:566
  40.7 13.9 %collective-permute-start.6 = (bf16[2,512,128]{2,1,0:T(8,128)(2,1)}, bf16[2,512,128]{2,1,0:T(8,128)(2,1)S(1)}, u32[]{:S(2)}, u32[]{:S(2)}) collective-permute-start(bf16[2,512,128]{2,1,0:T(8,128)(2,1)} %get-tuple-element.30), channel_id=1, source_target_pairs={{0,1},{1,0},{2,3},{3,2},{4,5},{5,4},{6,7},{7,6},{8,9},{9,8},{10,11... | collective-permute-start | bytes 786440 | tf_op jit(solution)/shard_map/ppermute | solution.py:584
  41.2 13.5 %collective-permute-start.7 = (bf16[2,512,128]{2,1,0:T(8,128)(2,1)}, bf16[2,512,128]{2,1,0:T(8,128)(2,1)}, u32[]{:S(2)}, u32[]{:S(2)}) collective-permute-start(bf16[2,512,128]{2,1,0:T(8,128)(2,1)} %get-tuple-element.31), channel_id=1, source_target_pairs={{1,2},{3,4},{5,6},{2,1},{4,3},{6,5},{9,10},{11,12},{13,14},{10,9},... | collective-permute-start | bytes 786440 | tf_op jit(solution)/shard_map/ppermute | solution.py:584
  46.9 1.0 %copy-start.1 = (bf16[4,512,128]{2,1,0:T(8,128)(2,1)S(1)}, bf16[4,512,128]{2,1,0:T(8,128)(2,1)}, u32[]{:S(2)}) copy-start(bf16[4,512,128]{2,1,0:T(8,128)(2,1)} %get-tuple-element.34.refs_4_.refs_12_) | copy-start | bytes 1572868
  47.9 9.4 %copy-start.8 = (bf16[128,128]{1,0:T(8,128)(2,1)S(1)}, bf16[128,128]{1,0:T(8,128)(2,1)}, u32[]{:S(2)}) copy-start(bf16[128,128]{1,0:T(8,128)(2,1)} %param.19) | copy-start | bytes 98308
  47.9 9.5 %copy-start.2 = (f32[4,512,128]{2,1,0:T(8,128)S(1)}, f32[4,512,128]{2,1,0:T(8,128)}, u32[]{:S(2)}) copy-start(f32[4,512,128]{2,1,0:T(8,128)} %get-tuple-element.42.refs_7_.refs_13_) | copy-start | bytes 3145732
  47.9 9.6 %copy-start.4 = (f32[4,512,128]{2,1,0:T(8,128)S(1)}, f32[4,512,128]{2,1,0:T(8,128)}, u32[]{:S(2)}) copy-start(f32[4,512,128]{2,1,0:T(8,128)} %get-tuple-element.44.refs_8_) | copy-start | bytes 3145732
  47.9 9.6 %copy-start.5 = (f32[128]{0:T(128)S(1)}, f32[128]{0:T(128)}, u32[]{:S(2)}) copy-start(f32[128]{0:T(128)} %param.21) | copy-start | bytes 1540
  55.8 10.1 %collective-permute-start.10 = (bf16[1,512,128]{2,1,0:T(8,128)(2,1)S(1)}, bf16[1,512,128]{2,1,0:T(8,128)(2,1)S(1)}, u32[]{:S(2)}, u32[]{:S(2)}) collective-permute-start(bf16[1,512,128]{2,1,0:T(8,128)(2,1)S(1)} %get-tuple-element.40.refs_4_), channel_id=1, source_target_pairs={{0,16},{8,24},{16,0},{24,8},{1,17},{9,25},{17,1},{25,9},{2,18},{10... | collective-permute-start | bytes 393224 | tf_op jit(solution)/shard_map/ppermute | solution.py:566
  55.9 10.1 %collective-permute-start.9 = (bf16[1,512,128]{2,1,0:T(8,128)(2,1)S(1)}, bf16[1,512,128]{2,1,0:T(8,128)(2,1)S(1)}, u32[]{:S(2)}, u32[]{:S(2)}) collective-permute-start(bf16[1,512,128]{2,1,0:T(8,128)(2,1)S(1)} %get-tuple-element.39.refs_3_.refs_8_), channel_id=1, source_target_pairs={{0,8},{8,0},{16,24},{24,16},{1,9},{9,1},{17,25},{25,17},{2,10},{10... | collective-permute-start | bytes 393224 | tf_op jit(solution)/shard_map/ppermute | solution.py:566

commit v4 on v3

v4 whole, which is shorter than its diff:
```python
import functools
import math

import jax
import jax.numpy as jnp
from jax import lax
from jax.experimental import pallas as pl
from jax.experimental.pallas import tpu as pltpu
from jax.sharding import PartitionSpec as P

epsilon = 1e-06
vmem_bytes = 28 * 1024 * 1024
edge_vmem_bytes = 36 * 1024 * 1024
whole_vmem_bytes = 56 * 1024 * 1024
in_vmem = pl.BlockSpec(memory_space=pltpu.VMEM)
in_smem = pl.BlockSpec(memory_space=pltpu.SMEM)
no_cost = pl.CostEstimate(flops=0, bytes_accessed=0, transcendentals=0)
anywhere = pl.BlockSpec(memory_space=pl.ANY)


def silu(v):
    half = 0.5 * v
    return half * jnp.tanh(half) + half


def scaled(values, gain):
    channels = values.shape[-1]
    squares = (values * values).astype(jnp.bfloat16)
    ones = jnp.ones((channels, channels), jnp.bfloat16)
    mean_square = jnp.dot(squares, ones, preferred_element_type=jnp.float32) * (1.0 / channels)
    return values * lax.rsqrt(mean_square + epsilon) * gain


class Copies:
    def __init__(self, semaphores):
        self.semaphores = semaphores
        self.count = 0

    def start(self, source, target):
        copy = pltpu.make_async_copy(source, target, self.semaphores.at[self.count])
        self.count += 1
        copy.start()
        return copy

    def start_one(self, sources, chosen, target):
        slot = self.semaphores.at[self.count]
        self.count += 1
        for i, source in enumerate(sources):

            @pl.when(chosen == i)
            def _(source=source):
                pltpu.make_async_copy(source, target, slot).start()

        return pltpu.make_async_copy(sources[0], target, slot)


def clear(pad):
    slots, length, channels = pad.shape
    zeros = jnp.zeros((8, channels), jnp.float32)
    for slot in range(slots):
        pad[slot, 0:8] = zeros
        pad[slot, length - 8 : length] = zeros


def place(value, pad, slot):
    pad[slot, 8 : 8 + value.shape[0]] = value


def pack(kernel, out):
    channels = kernel.shape[2]
    zero = jnp.zeros((channels, channels), jnp.bfloat16)
    for j in range(4):
        for b in range(3):
            rows = pl.ds((3 * j + b) * channels, channels)
            out[rows, :channels] = kernel[j, b] if j < 3 else zero
            out[rows, channels:] = kernel[j - 1, b] if j > 0 else zero


def row_pair(pad, first, weights):
    columns = pad.shape[1] - 16
    lhs = [pad[first + j, 7 + b : 7 + b + columns] for j in range(4) for b in range(3)]
    lhs = jnp.concatenate(lhs, axis=-1).astype(jnp.bfloat16)
    return jnp.dot(lhs, weights[...], preferred_element_type=jnp.float32)


def ask(norm, query_weight, key_weight, tempers, query_edge, query_middle):
    rows, channels = tempers.shape[0], norm[0].shape[-1]
    mixing = lax.dot_general(
        query_weight[...],
        key_weight[...],
        (((1,), (1,)), ((), ())),
        preferred_element_type=jnp.float32,
    ).astype(jnp.bfloat16)
    scales = tempers[...].T * (math.log2(math.e) / math.sqrt(channels))
    for r in range(rows):
        row = band_row(*norm, r)[...]
        mixed = jnp.dot(row, mixing, preferred_element_type=jnp.float32)
        query = (mixed * scales[:, r : r + 1]).astype(jnp.bfloat16)
        band_row(query_edge, query_middle, r)[...] = query


def middle_body(
    cells, one, two, gain, state_one_out, state_out, norm_out,
    held, one_held, two_held, gain_held, w1, w2, state_one, state_two, norm, x1, x2, sems,
):
    rows = cells.shape[0]
    channels = cells.shape[2]
    copies = Copies(sems)
    loads = [copies.start(cells.at[r], held.at[r]) for r in range(4)]
    later = [copies.start(one, one_held)]
    later += [copies.start(cells.at[r], held.at[r]) for r in range(4, rows)]
    later += [
        copies.start(two, two_held),
        copies.start(gain, gain_held),
    ]
    clear(x1)
    clear(x2)

    def convolve_one(first):
        out = row_pair(x1, first, w1)
        for o in range(2):
            r = first + 1 + o
            state = held[r] + out[:, o * channels : (o + 1) * channels]
            state_one[r - 1] = state
            place(silu(state), x2, r - 1)

    def convolve_two(first):
        out = row_pair(x2, first, w2)
        for o in range(2):
            slot = first + o
            state = state_one[slot + 1] + out[:, o * channels : (o + 1) * channels]
            state_two[slot] = state
            norm[slot] = scaled(state, gain_held[...]).astype(jnp.bfloat16)

    for load in loads:
        load.wait()
    for r in range(4):
        place(silu(held[r]), x1, r)
    for load in later:
        load.wait()
    pack(one_held, w1)
    pack(two_held, w2)
    for first in range(0, rows - 2, 2):
        convolve_one(first)
        for r in range(first + 4, min(first + 6, rows)):
            place(silu(held[r]), x1, r)
        if first >= 2:
            convolve_two(first - 2)
    stores = [
        copies.start(norm, norm_out),
        copies.start(state_one.at[pl.ds(0, 2)], state_one_out.at[pl.ds(0, 2)]),
        copies.start(state_one.at[pl.ds(rows - 4, 2)], state_one_out.at[pl.ds(2, 2)]),
        copies.start(state_two, state_out),
    ]
    for store in stores:
        store.wait()


def scratch(*arrays):
    return [pltpu.VMEM(shape, kind) for shape, kind in arrays]


def middle_rows(cells, one, two, gain):
    rows, columns, channels = cells.shape
    row = (columns, channels)
    padded = (columns + 16, channels)
    packed = ((12 * channels, 2 * channels), jnp.bfloat16)
    operands = (cells, one, two, gain)
    return pl.pallas_call(
        middle_body,
        in_specs=[anywhere] * 4,
        out_specs=[anywhere] * 3,
        out_shape=[
            jax.ShapeDtypeStruct((4, *row), jnp.float32),
            jax.ShapeDtypeStruct((rows - 4, *row), jnp.float32),
            jax.ShapeDtypeStruct((rows - 4, *row), jnp.bfloat16),
        ],
        scratch_shapes=[
            *scratch(*[(a.shape, a.dtype) for a in operands]),
            *scratch(
                packed,
                packed,
                ((rows - 2, *row), jnp.float32),
                ((rows - 4, *row), jnp.float32),
                ((rows - 4, *row), jnp.bfloat16),
                ((rows, *padded), jnp.float32),
                ((rows - 2, *padded), jnp.float32),
            ),
            pltpu.SemaphoreType.DMA((rows + 7,)),
        ],
        compiler_params=pltpu.CompilerParams(vmem_limit_bytes=whole_vmem_bytes),
        cost_estimate=no_cost,
        name="residual_middle",
    )(*operands)


def edge_body(
    cells, mate, cross, one, two, state_one, gain, state_out, norm_out,
    held, one_held, two_held, state_held, gain_held, w1, w2, state_two, norm, x1, x2, sems,
):
    rows = cells.shape[0]
    channels = cells.shape[2]
    first_band, last_band, odd = band_place()
    copies = Copies(sems)
    loads = [
        copies.start(cells.at[pl.ds(0, 2)], held.at[pl.ds(0, 2)]),
        copies.start(cells.at[pl.ds(rows - 2, 2)], held.at[pl.ds(2, 2)]),
    ]
    later = [
        copies.start(one, one_held),
        copies.start(two, two_held),
        copies.start(state_one, state_held),
        copies.start(gain, gain_held),
    ]
    clear(x1)
    clear(x2)
    for load in loads:
        load.wait()
    for r in range(2):
        place(silu(held[r]), x1, 2 + r)
        place(silu(held[2 + r]), x1, 4 + r)
    outside = []
    for r in range(2):
        mate_row = mate[r].astype(jnp.float32)
        cross_row = cross[r].astype(jnp.float32)
        over = jnp.where(first_band, 0.0, jnp.where(odd, mate_row, cross_row))
        under = jnp.where(last_band, 0.0, jnp.where(odd, cross_row, mate_row))
        place(silu(over), x1, r)
        place(silu(under), x1, 6 + r)
        outside.append((over, under))
    over, under = outside[1][0], outside[0][1]
    for load in later:
        load.wait()
    pack(one_held, w1)
    pack(two_held, w2)
    out = row_pair(x1, 0, w1)
    over = over + out[:, :channels]
    top = held[0] + out[:, channels:]
    out = row_pair(x1, 4, w1)
    bottom = held[3] + out[:, :channels]
    under = under + out[:, channels:]
    for r in range(2):
        place(silu(state_held[r]), x2, 2 + r)
        place(silu(state_held[2 + r]), x2, 4 + r)
    place(jnp.where(first_band, 0.0, silu(over)), x2, 0)
    place(silu(top), x2, 1)
    place(silu(bottom), x2, 6)
    place(jnp.where(last_band, 0.0, silu(under)), x2, 7)
    for slot, states in ((0, (top, state_held[0])), (2, (state_held[3], bottom))):
        out = row_pair(x2, 2 * slot, w2)
        for o in range(2):
            state = states[o] + out[:, o * channels : (o + 1) * channels]
            state_two[slot + o] = state
            norm[slot + o] = scaled(state, gain_held[...]).astype(jnp.bfloat16)
    stores = [copies.start(norm, norm_out), copies.start(state_two, state_out)]
    for store in stores:
        store.wait()


def edge_rows(cells, mate, cross, one, two, state_one, gain):
    columns, channels = cells.shape[1:]
    row = (columns, channels)
    padded = (columns + 16, channels)
    packed = ((12 * channels, 2 * channels), jnp.bfloat16)
    operands = (cells, mate, cross, one, two, state_one, gain)
    return pl.pallas_call(
        edge_body,
        in_specs=[anywhere] + [in_vmem] * 2 + [anywhere] * 4,
        out_specs=[anywhere] * 2,
        out_shape=[
            jax.ShapeDtypeStruct((4, *row), jnp.float32),
            jax.ShapeDtypeStruct((4, *row), jnp.bfloat16),
        ],
        scratch_shapes=[
            *scratch(((4, *row), jnp.float32), *[(a.shape, a.dtype) for a in operands[3:]]),
            *scratch(
                packed,
                packed,
                ((4, *row), jnp.float32),
                ((4, *row), jnp.bfloat16),
                ((8, *padded), jnp.float32),
                ((8, *padded), jnp.float32),
            ),
            pltpu.SemaphoreType.DMA((8,)),
        ],
        compiler_params=pltpu.CompilerParams(vmem_limit_bytes=edge_vmem_bytes),
        cost_estimate=no_cost,
        name="residual_edge",
    )(*operands)


def band_place():
    band = lax.axis_index("band")
    return band == 0, band == lax.axis_size("band") - 1, lax.rem(band, 2) == 1


def blend(query, window, store):
    keys, channels = window.shape
    extended = jnp.concatenate([window, jnp.ones((keys, channels), jnp.bfloat16)], axis=1)
    columns = query.shape[0]
    block = 128 if columns % 128 == 0 else columns
    for start in range(0, columns, block):
        scores = lax.dot_general(
            query[pl.ds(start, block)],
            window,
            (((1,), (1,)), ((), ())),
            preferred_element_type=jnp.float32,
        )
        peak = jnp.max(scores, axis=-1, keepdims=True)
        lifted = jnp.exp2(scores - peak).astype(jnp.bfloat16)
        total = jnp.dot(lifted, extended, preferred_element_type=jnp.float32)
        store(pl.ds(start, block), total[:, :channels] / total[:, channels:])


def pick(chosen, candidates):
    picked = candidates[0]
    for i, candidate in enumerate(candidates[1:], 1):
        picked = jnp.where(chosen == i, candidate, picked)
    return picked


def key_offset(partners, low, far):
    view = lax.axis_index("view")
    first = jnp.bitwise_xor(partners[view, 0], view)
    second = jnp.bitwise_xor(partners[view, 1], view)
    return (jnp.maximum(first, second) if far else jnp.minimum(first, second)) - low


def band_row(edge, middle, r):
    inner = middle.shape[0]
    if r < 2:
        return edge.at[r]
    if r < inner + 2:
        return middle.at[r - 2]
    return edge.at[r - inner]


def picked_row(chosen, edges, middles, r):
    return pick(chosen, [band_row(e, m, r)[...] for e, m in zip(edges, middles)])


def finish(r, both, state, value_out, gain, result):
    message = jnp.dot(both[r], value_out[...], preferred_element_type=jnp.float32)
    result[r] = state[...] + scaled(message, gain[...])


def take(refs, *counts):
    groups = []
    for count in counts:
        groups.append(refs[:count])
        refs = refs[count:]
    return (*groups, refs)


def gather_keys(chosen, edges, middles, keys):
    for r in range(keys.shape[0]):
        keys[r] = pick(chosen, [band_row(e, m, r)[...] for e, m in zip(edges, middles)])


def attend_first_body(low, count, partners, *refs):
    middles, refs = take(refs, count)
    (
        edge, middle, query_weight, key_weight, tempers, query_edge, query_middle, out, keys
    ) = refs
    ask((edge, middle), query_weight, key_weight, tempers, query_edge, query_middle)
    columns, channels = out.shape[1:]
    chosen = key_offset(partners, low, False)
    for r in range(keys.shape[0]):
        keys[r] = pick(chosen, [m[r] for m in middles])
    for r in range(out.shape[0]):
        window = keys[r : r + 3].reshape(3 * columns, channels)

        def store(place, value, r=r):
            out[r, place] = value.astype(jnp.bfloat16)

        blend(query_middle.at[r + 1], window, store)


def attend_near_body(low, count, partners, *refs):
    edges, middles, refs = take(refs, count, count)
    query_edge, query_middle, out, keys = refs
    rows, columns, channels = keys.shape
    gather_keys(key_offset(partners, low, False), edges, middles, keys)
    for slot, r in enumerate((1, 2, rows - 3, rows - 2)):
        window = keys[r - 1 : r + 2].reshape(3 * columns, channels)

        def store(place, value, slot=slot):
            out[slot, place] = value.astype(jnp.bfloat16)

        blend(band_row(query_edge, query_middle, r), window, store)


def attend_far_body(low, count, partners, *refs):
    edges, middles, refs = take(refs, count, count)
    (
        query_edge, query_middle, near, first, state_edge, state_middle, value_out, gain,
        out, keys, both,
    ) = refs
    rows, columns, channels = keys.shape
    gather_keys(key_offset(partners, low, True), edges, middles, keys)
    for r in range(1, rows - 1):
        window = keys[r - 1 : r + 2].reshape(3 * columns, channels)
        other = band_row(near, first, r - 1)

        def store(place, value, r=r, other=other):
            both[r - 1, place] = (value + other[place].astype(jnp.float32)).astype(jnp.bfloat16)

        blend(band_row(query_edge, query_middle, r), window, store)
    for r in range(1, rows - 1):
        finish(r - 1, both, band_row(state_edge, state_middle, r), value_out, gain, out)


def end_windows(chosen, edges, above, below, keys):
    keys[0] = above
    keys[5] = below
    for r in range(4):
        keys[1 + r] = pick(chosen, [e[r] for e in edges])


def attend_ends_body(low, count, partners, *refs):
    edges, refs = take(refs, count)
    mate, cross, query_edge, out = refs[:4]
    outs, keys = refs[4:-1], refs[-1]
    columns, channels = out.shape[1:]
    first_band, last_band, odd = band_place()
    for i in range(mate.shape[0]):
        above = jnp.where(odd, mate[i], cross[i])
        below = jnp.where(odd, cross[i], mate[i])
        outs[2 * i][0] = jnp.where(first_band, jnp.zeros_like(above), above)
        outs[2 * i + 1][0] = jnp.where(last_band, jnp.zeros_like(below), below)
    chosen = key_offset(partners, low, False)
    above = pick(chosen, [a[0] for a in outs[0::2]])
    below = pick(chosen, [b[0] for b in outs[1::2]])
    end_windows(chosen, edges, above, below, keys)
    for end in range(2):
        window = keys[3 * end : 3 * end + 3].reshape(3 * columns, channels)

        def store(place, value, end=end):
            out[end, place] = value.astype(jnp.bfloat16)

        blend(query_edge.at[3 * end], window, store)


def attend_outer_body(low, count, partners, *refs):
    edges, aboves, belows, refs = take(refs, count, count, count)
    query_edge, ends, state_edge, value_out, gain, inner, out, keys, both, result, sems = refs
    rows, columns, channels = out.shape
    copies = Copies(sems)
    stores = [copies.start(inner, out.at[pl.ds(1, rows - 2)])]
    chosen = key_offset(partners, low, True)
    above = pick(chosen, [a[0] for a in aboves])
    below = pick(chosen, [b[0] for b in belows])
    end_windows(chosen, edges, above, below, keys)
    for end in range(2):
        window = keys[3 * end : 3 * end + 3].reshape(3 * columns, channels)

        def store(place, value, end=end):
            both[end, place] = (value + ends[end, place].astype(jnp.float32)).astype(jnp.bfloat16)

        blend(query_edge.at[3 * end], window, store)
    for end in range(2):
        finish(end, both, state_edge.at[3 * end], value_out, gain, result)
    stores += [copies.start(result.at[0], out.at[0]), copies.start(result.at[1], out.at[rows - 1])]
    for store in stores:
        store.wait()


def attend_first(partners, low, middles, edge, middle, query_weight, key_weight, tempers):
    rows, columns = tempers.shape
    channels = edge.shape[-1]
    operands = [*middles, edge, middle, query_weight, key_weight, tempers]
    like = jax.ShapeDtypeStruct
    return pl.pallas_call(
        functools.partial(attend_first_body, low, len(middles)),
        in_specs=[in_smem] + [in_vmem] * len(operands),
        out_specs=[in_vmem] * 3,
        out_shape=[
            like(edge.shape, jnp.bfloat16),
            like(middle.shape, jnp.bfloat16),
            like((rows - 6, columns, channels), jnp.bfloat16),
        ],
        scratch_shapes=[pltpu.VMEM(middle.shape, jnp.bfloat16)],
        compiler_params=pltpu.CompilerParams(vmem_limit_bytes=vmem_bytes),
        cost_estimate=no_cost,
        name="attend_first",
    )(partners, *operands)


def attend_near(partners, low, candidates, queries):
    rows = candidates[0][0].shape[0] + candidates[1][0].shape[0]
    columns, channels = queries[0].shape[1:]
    operands = [a for group in candidates for a in group] + list(queries)
    return pl.pallas_call(
        functools.partial(attend_near_body, low, len(candidates[0])),
        in_specs=[in_smem] + [in_vmem] * len(operands),
        out_specs=in_vmem,
        out_shape=jax.ShapeDtypeStruct((4, columns, channels), jnp.bfloat16),
        scratch_shapes=[pltpu.VMEM((rows, columns, channels), jnp.bfloat16)],
        compiler_params=pltpu.CompilerParams(vmem_limit_bytes=vmem_bytes),
        cost_estimate=no_cost,
        name="attend_near",
    )(partners, *operands)


def attend_far(partners, low, candidates, queries, near, first, states, value_out, gain):
    columns, channels = near.shape[1:]
    rows = near.shape[0] + first.shape[0]
    operands = [a for group in candidates for a in group]
    operands += [*queries, near, first, *states, value_out, gain]
    return pl.pallas_call(
        functools.partial(attend_far_body, low, len(candidates[0])),
        in_specs=[in_smem] + [in_vmem] * len(operands),
        out_specs=in_vmem,
        out_shape=jax.ShapeDtypeStruct((rows, columns, channels), jnp.float32),
        scratch_shapes=[
            pltpu.VMEM((rows + 2, columns, channels), jnp.bfloat16),
            pltpu.VMEM((rows, columns, channels), jnp.bfloat16),
        ],
        compiler_params=pltpu.CompilerParams(vmem_limit_bytes=vmem_bytes),
        cost_estimate=no_cost,
        name="attend_far",
    )(partners, *operands)


def attend_ends(partners, low, edges, mate, cross, query):
    columns, channels = query.shape[1:]
    row = jax.ShapeDtypeStruct((1, columns, channels), jnp.bfloat16)
    operands = [*edges, mate, cross, query]
    return pl.pallas_call(
        functools.partial(attend_ends_body, low, len(edges)),
        in_specs=[in_smem] + [in_vmem] * len(operands),
        out_specs=[in_vmem] * (1 + 2 * mate.shape[0]),
        out_shape=[jax.ShapeDtypeStruct((2, columns, channels), jnp.bfloat16)]
        + [row] * (2 * mate.shape[0]),
        scratch_shapes=[pltpu.VMEM((6, columns, channels), jnp.bfloat16)],
        compiler_params=pltpu.CompilerParams(vmem_limit_bytes=vmem_bytes),
        cost_estimate=no_cost,
        name="attend_ends",
    )(partners, *operands)


def attend_outer(partners, low, sides, query, ends, state, value_out, gain, inner):
    rows, columns, channels = inner.shape
    operands = [a for group in sides for a in group]
    operands += [query, ends, state, value_out, gain, inner]
    return pl.pallas_call(
        functools.partial(attend_outer_body, low, len(sides[0])),
        in_specs=[in_smem] + [in_vmem] * len(operands),
        out_specs=anywhere,
        out_shape=jax.ShapeDtypeStruct((rows + 2, columns, channels), jnp.float32),
        scratch_shapes=[
            pltpu.VMEM((6, columns, channels), jnp.bfloat16),
            pltpu.VMEM((2, columns, channels), jnp.bfloat16),
            pltpu.VMEM((2, columns, channels), jnp.float32),
            pltpu.SemaphoreType.DMA((3,)),
        ],
        compiler_params=pltpu.CompilerParams(vmem_limit_bytes=vmem_bytes),
        cost_estimate=no_cost,
        name="attend_outer",
    )(partners, *operands)


def edge_halos_body(*refs):
    edges, (mate, cross) = refs[:-2], refs[-2:]
    odd = band_place()[2]
    for i, edge in enumerate(edges):
        mate[i] = jnp.where(odd, edge[0], edge[3])
        cross[i] = jnp.where(odd, edge[3], edge[0])


def edge_halos(edges):
    rows = jax.ShapeDtypeStruct((len(edges), *edges[0].shape[1:]), jnp.bfloat16)
    return pl.pallas_call(
        edge_halos_body,
        in_specs=[in_vmem] * len(edges),
        out_specs=[in_vmem] * 2,
        out_shape=[rows, rows],
        compiler_params=pltpu.CompilerParams(vmem_limit_bytes=vmem_bytes),
        cost_estimate=no_cost,
        name="edge_halos",
    )(*edges)


def swap(cells, views, offset):
    return lax.ppermute(cells, "view", [(i, i ^ offset) for i in range(views)])


def gather_direct(cells, views):
    return {1 << i: swap(cells, views, 1 << i) for i in range((views - 1).bit_length())}


def relay(held, views, by_low):
    for offset in range(1, views):
        bit = offset & -offset if by_low else 1 << (offset.bit_length() - 1)
        if bit != offset:
            held[offset] = swap(held[offset ^ bit], views, bit)


def swap_bands(mate, cross, bands):
    mates = [(i, i ^ 1) for i in range(bands)]
    crosses = [(i, i + 1) for i in range(1, bands - 1, 2)]
    crosses = crosses + [(j, i) for i, j in crosses]
    return lax.ppermute(mate, "band", mates), lax.ppermute(cross, "band", crosses)


def per_device(
    features, tempers, partners, conv_one, conv_two, query_weight, key_weight,
    value_weight, out_weight, norm_gain, message_gain,
):
    views = lax.axis_size("view")
    bands = lax.axis_size("band")
    cells, temper, gain = features[0], tempers[0], norm_gain[None]

    state_one, state_middle, middle = middle_rows(cells, conv_one, conv_two, gain)
    middles = gather_direct(middle, views)
    halo_cells, middle = lax.optimization_barrier((cells, middle))
    head, tail = halo_cells[:2].astype(jnp.bfloat16), halo_cells[-2:].astype(jnp.bfloat16)
    odd = band_place()[2]
    mate, cross = swap_bands(jnp.where(odd, head, tail), jnp.where(odd, tail, head), bands)
    state_edge, edge = edge_rows(cells, mate, cross, conv_one, conv_two, state_one, gain)
    edges = gather_direct(edge, views)

    def candidates(groups, low, high):
        return [[group[i] for i in range(low, high + 1)] for group in groups]

    near_ends, far_ends = (1, max(1, views - 2)), (min(2, views - 1), views - 1)
    direct = list(edges)
    *queries, first = attend_first(
        partners, 1, [middles[i] for i in direct], edge, middle, query_weight, key_weight, temper
    )
    value_out = jnp.dot(value_weight, out_weight, preferred_element_type=jnp.float32).astype(
        jnp.bfloat16
    )
    edges, middles, queries, first, value_out = lax.optimization_barrier(
        (edges, middles, queries, first, value_out)
    )
    mate, cross = swap_bands(*edge_halos([edges[i] for i in direct]), bands)
    relay(edges, views, False)
    relay(middles, views, True)
    near = attend_near(partners, near_ends[0], candidates((edges, middles), *near_ends), queries)
    mate, cross, near = lax.optimization_barrier((mate, cross, near))
    near_edges = candidates((edges,), *near_ends)[0]
    ends, *halos = attend_ends(partners, near_ends[0], near_edges, mate, cross, queries[0])
    edges, middles, halos, ends = lax.optimization_barrier((edges, middles, halos, ends))
    above = dict(zip(direct, halos[0::2]))
    below = dict(zip(direct, halos[1::2]))
    relay(above, views, True)
    relay(below, views, False)
    rest = (value_out, message_gain[None])
    inner = attend_far(
        partners, far_ends[0], candidates((edges, middles), *far_ends), queries, near, first,
        (state_edge, state_middle), *rest,
    )
    refined = attend_outer(
        partners, far_ends[0], candidates((edges, above, below), *far_ends), queries[0], ends,
        state_edge, *rest, inner,
    )
    return refined[None]


def solution(mesh):
    whole = P()
    in_specs = (P("view", "band", None, None), P("view", "band", None)) + (whole,) * 9
    return jax.shard_map(
        per_device, mesh=mesh, in_specs=in_specs,
        out_specs=P("view", "band", None, None), check_vma=False,
    )
```

time: 72.1 us -> 65.5 us (0.908)
  Pallas kernels: 37.4 us -> 34.4 us
  waiting for transfers between devices: 13.4 us -> 10.4 us
  starting transfers between devices: 16.7 us -> 18.4 us
  other arithmetic: 1.8 us -> 0.21 us
  local copies, waits for them, and re-layouts: 1.95 us -> 1.13 us
    ppermute x8, waiting for transfers between devices: 13.4 us -> 8.65 us  [swap(): return lax.ppermute(cells, 'view', [(i, i ^ offset) for i in range(views)])]
    pallas_call x3 -> x4, Pallas kernels: 13.9 us -> 18 us  [the longest x1 6.98 us: middle_rows(): pl.pallas_call(middle_body, in_specs=[anywhere] * 4, out_specs=[anywhere]...]
    pallas_call x1, Pallas kernels: 7.47 us -> 4.77 us  [edge_rows(): pl.pallas_call(edge_body, in_specs=[anywhere] + [in_vmem] * 2 + [anywhere...]
    pallas_call x1, Pallas kernels: 6.73 us -> 4.64 us  [attend_near(): pl.pallas_call(functools.partial(attend_near_body, low, len(candidates[0]...]
    ppermute x8, starting transfers between devices: 6.06 us -> 8.05 us  [swap(): return lax.ppermute(cells, 'view', [(i, i ^ offset) for i in range(views)])]
    ppermute x2, starting transfers between devices: 10.1 us -> 8.17 us  [swap_bands(): lax.ppermute(cross, 'band', crosses)]
    ppermute x2, waiting for transfers between devices: 0.01 us -> 1.74 us  [swap_bands(): lax.ppermute(cross, 'band', crosses)]
    ppermute x2, starting transfers between devices: 0.57 us -> 2.19 us  [swap_bands(): lax.ppermute(mate, 'band', mates)]
  transfers between devices with their start and end apart: 12 -> 12, of which waited for: 4 -> 5; matrix products, arithmetic and copies ran while one was open for 0% -> 0% of each run, Pallas kernels for 44% -> 36%
where the time goes in v4:
time: 65.5 us; the launch traced here: 65.1 us
  Pallas kernels  34.4 us (53%)
  starting transfers between devices  18.4 us (28%)
  waiting for transfers between devices  10.4 us (16%)
  local copies, waits for them, and re-layouts  1.13 us (2%)
    ppermute x8, waiting for transfers between devices, swap(): return lax.ppermute(cells, 'view', [(i, i ^ offset) for i in range(views)])  8.65 us
    ppermute x2, starting transfers between devices, swap_bands(): lax.ppermute(cross, 'band', crosses)  8.17 us
    ppermute x8, starting transfers between devices, swap(): return lax.ppermute(cells, 'view', [(i, i ^ offset) for i in range(views)])  8.05 us
    pallas_call x1, Pallas kernels, middle_rows(): pl.pallas_call(middle_body, in_specs=[anywhere] * 4, out_specs=[anywhere]...  6.98 us
    pallas_call x1, Pallas kernels, attend_far(): pl.pallas_call(functools.partial(attend_far_body, low, len(candidates[0])...  6.89 us
    pallas_call x1, Pallas kernels, edge_rows(): pl.pallas_call(edge_body, in_specs=[anywhere] + [in_vmem] * 2 + [anywhere...  4.77 us
    pallas_call x1, Pallas kernels, attend_near(): pl.pallas_call(functools.partial(attend_near_body, low, len(candidates[0]...  4.64 us
    pallas_call x1, Pallas kernels, attend_first(): pl.pallas_call(functools.partial(attend_first_body, low, len(middles)), i...  4.07 us
  transfers between devices with their start and end apart: 12, of which 5 were waited for; matrix products, arithmetic and copies ran while one was open for 0% of the time, Pallas kernels for 36%

profile of v4, /device:TPU:1, one launch (start us, length us, event | category | flops | bytes accessed | tf_op | source)
XLA Modules:
  0.0 65.1 jit_solution(3623066001263005448)
XLA Ops:
  0.0 7.0 %residual_middle.1 = (f32[4,512,128]{2,1,0:T(8,128)}, f32[4,512,128]{2,1,0:T(8,128)}, bf16[4,512,128]{2,1,0:T(8,128)(2,1)}) custom-call(f32[8,512,128]{2,1,0:T(8,128)} %bitcast.7, bf16[3,3,128,128]{3,2,1,0:T(8,128)(2,1)} %one.3, bf16[3,3,128,128]{3,2,1,0:T(8,128)(2,1)} %two.3, f32[1,128]{1,0:T(1,128)} %bitcast.11), custom_call_target="tpu_custom_call" | custom-call | tf_op jit(solution)/shard_map/residual_middle/pallas_call | solution.py:169
  7.0 0.0 copy-start.4
  7.0 0.0 copy-start.5
  7.0 0.0 copy-start.6
  7.0 0.0 copy-start.11
  7.0 0.2 convert.4
  7.3 4.7 %collective-permute-start.1 = (bf16[2,512,128]{2,1,0:T(8,128)(2,1)S(1)}, bf16[2,512,128]{2,1,0:T(8,128)(2,1)S(1)}, u32[]{:S(2)}, u32[]{:S(2)}) collective-permute-start(bf16[2,512,128]{2,1,0:T(8,128)(2,1)S(1)} %get-tuple-element.75), channel_id=1, source_target_pairs={{1,2},{3,4},{5,6},{2,1},{4,3},{6,5},{9,10},{11,12},{13,14},{10,9},... | collective-permute-start | bytes 786440 | tf_op jit(solution)/shard_map/ppermute | solution.py:603
  12.0 0.1 collective-permute-start
  12.1 1.3 %collective-permute-start.5 = (bf16[4,512,128]{2,1,0:T(8,128)(2,1)}, bf16[4,512,128]{2,1,0:T(8,128)(2,1)S(1)}, u32[]{:S(2)}, u32[]{:S(2)}) collective-permute-start(bf16[4,512,128]{2,1,0:T(8,128)(2,1)} %get-tuple-element.44.refs_3_), channel_id=1, source_target_pairs={{0,16},{8,24},{16,0},{24,8},{1,17},{9,25},{17,1},{25,9},{2,18},{10... | collective-permute-start | bytes 1572872 | tf_op jit(solution)/shard_map/ppermute | solution.py:585
  13.4 1.2 %collective-permute-start.4 = (bf16[4,512,128]{2,1,0:T(8,128)(2,1)}, bf16[4,512,128]{2,1,0:T(8,128)(2,1)S(1)}, u32[]{:S(2)}, u32[]{:S(2)}) collective-permute-start(bf16[4,512,128]{2,1,0:T(8,128)(2,1)} %get-tuple-element.44.refs_3_), channel_id=1, source_target_pairs={{0,8},{8,0},{16,24},{24,16},{1,9},{9,1},{17,25},{25,17},{2,10},{10... | collective-permute-start | bytes 1572872 | tf_op jit(solution)/shard_map/ppermute | solution.py:585
  14.6 1.7 %collective-permute-done.1.cross = bf16[2,512,128]{2,1,0:T(8,128)(2,1)S(1)} collective-permute-done((bf16[2,512,128]{2,1,0:T(8,128)(2,1)S(1)}, bf16[2,512,128]{2,1,0:T(8,128)(2,1)S(1)}, u32[]{:S(2)}, u32[]{:S(2)}) %collective-permute-start.1) | collective-permute-done | bytes 262176 | tf_op jit(solution)/shard_map/ppermute | solution.py:603
  16.3 0.0 collective-permute-done.mate
  16.4 0.0 copy-start.14
  16.4 0.0 copy-start.13
  16.4 0.0 copy-start.8
  16.4 0.0 copy-start.9
  16.4 0.0 copy-start.10
  16.4 4.8 %residual_edge.1 = (f32[4,512,128]{2,1,0:T(8,128)S(1)}, bf16[4,512,128]{2,1,0:T(8,128)(2,1)}) custom-call(f32[8,512,128]{2,1,0:T(8,128)S(1)} %bitcast.9, bf16[2,512,128]{2,1,0:T(8,128)(2,1)S(1)} %collective-permute-done.mate, bf16[2,512,128]{2,1,0:T(8,128)(2,1)S(1)} %collective-permute-done.1.cross, bf16[3,3,128,128]{3,2,1,0:T(8,128)(2,1)S(1)} %copy-done.4, ...), custom_call_target="tpu_custom_call" | custom-call | tf_op jit(solution)/shard_map/residual_edge/pallas_call | solution.py:266
  21.2 0.0 copy-start.2
  21.2 1.0 %copy-done.2 = f32[4,512,128]{2,1,0:T(8,128)} copy-done((f32[4,512,128]{2,1,0:T(8,128)}, f32[4,512,128]{2,1,0:T(8,128)S(1)}, u32[]{:S(2)}) %copy-start.2) | copy-done | bytes 1048600
  22.2 1.2 %collective-permute-start.3 = (bf16[4,512,128]{2,1,0:T(8,128)(2,1)}, bf16[4,512,128]{2,1,0:T(8,128)(2,1)S(1)}, u32[]{:S(2)}, u32[]{:S(2)}) collective-permute-start(bf16[4,512,128]{2,1,0:T(8,128)(2,1)} %get-tuple-element.43.refs_2_), channel_id=1, source_target_pairs={{0,16},{8,24},{16,0},{24,8},{1,17},{9,25},{17,1},{25,9},{2,18},{10... | collective-permute-start | bytes 1572872 | tf_op jit(solution)/shard_map/ppermute | solution.py:585
  23.4 1.2 %collective-permute-start.2 = (bf16[4,512,128]{2,1,0:T(8,128)(2,1)}, bf16[4,512,128]{2,1,0:T(8,128)(2,1)S(1)}, u32[]{:S(2)}, u32[]{:S(2)}) collective-permute-start(bf16[4,512,128]{2,1,0:T(8,128)(2,1)} %get-tuple-element.43.refs_2_), channel_id=1, source_target_pairs={{0,8},{8,0},{16,24},{24,16},{1,9},{9,1},{17,25},{25,17},{2,10},{10... | collective-permute-start | bytes 1572872 | tf_op jit(solution)/shard_map/ppermute | solution.py:585
  24.6 0.1 copy.16.partners
  24.7 0.0 copy-done.13
  24.7 0.1 convolution_convert_fusion.refs_10_.refs_9_
  24.9 0.6 collective-permute-done.5.refs_1_.refs_3_.refs_2_
  25.4 0.9 %collective-permute-done.4.refs_0_.refs_2_ = bf16[4,512,128]{2,1,0:T(8,128)(2,1)S(1)} collective-permute-done((bf16[4,512,128]{2,1,0:T(8,128)(2,1)}, bf16[4,512,128]{2,1,0:T(8,128)(2,1)S(1)}, u32[]{:S(2)}, u32[]{:S(2)}) %collective-permute-start.4) | collective-permute-done | bytes 524320 | tf_op jit(solution)/shard_map/ppermute | solution.py:585
  26.4 0.0 copy-done.9
  26.4 4.1 %attend_first.1 = (bf16[4,512,128]{2,1,0:T(8,128)(2,1)S(1)}, bf16[4,512,128]{2,1,0:T(8,128)(2,1)S(1)}, bf16[2,512,128]{2,1,0:T(8,128)(2,1)S(1)}) custom-call(s32[4,2]{1,0:T(4,128)S(1)} %copy.16.partners, bf16[4,512,128]{2,1,0:T(8,128)(2,1)S(1)} %collective-permute-done.4.refs_0_.refs_2_, ...), custom_call_target="tpu_custom_call" | custom-call | tf_op jit(solution)/shard_map/attend_first/pallas_call | solution.py:473
  30.4 6.2 %collective-permute-done.3.refs_1_.refs_0_ = bf16[4,512,128]{2,1,0:T(8,128)(2,1)S(1)} collective-permute-done((bf16[4,512,128]{2,1,0:T(8,128)(2,1)}, bf16[4,512,128]{2,1,0:T(8,128)(2,1)S(1)}, u32[]{:S(2)}, u32[]{:S(2)}) %collective-permute-start.3) | collective-permute-done | bytes 524320 | tf_op jit(solution)/shard_map/ppermute | solution.py:585
  36.7 0.9 %collective-permute-done.2.refs_0_ = bf16[4,512,128]{2,1,0:T(8,128)(2,1)S(1)} collective-permute-done((bf16[4,512,128]{2,1,0:T(8,128)(2,1)}, bf16[4,512,128]{2,1,0:T(8,128)(2,1)S(1)}, u32[]{:S(2)}, u32[]{:S(2)}) %collective-permute-start.2) | collective-permute-done | bytes 524320 | tf_op jit(solution)/shard_map/ppermute | solution.py:585
  37.6 1.2 %collective-permute-start.7 = (bf16[4,512,128]{2,1,0:T(8,128)(2,1)S(1)}, bf16[4,512,128]{2,1,0:T(8,128)(2,1)S(1)}, u32[]{:S(2)}, u32[]{:S(2)}) collective-permute-start(bf16[4,512,128]{2,1,0:T(8,128)(2,1)S(1)} %collective-permute-done.5.refs_1_.refs_3_.refs_2_), channel_id=1, source_target_pairs={{0,8},{8,0},{16,24},{24,16},{1,9},{9,1},{17,25},{25,17},{2,10},{10... | collective-permute-start | bytes 1572872 | tf_op jit(solution)/shard_map/ppermute | solution.py:585
  38.8 0.3 collective-permute-start.6
  39.1 0.1 edge_halos.1
  39.2 2.1 %collective-permute-start.8 = (bf16[2,512,128]{2,1,0:T(8,128)(2,1)S(1)}, bf16[2,512,128]{2,1,0:T(8,128)(2,1)S(1)}, u32[]{:S(2)}, u32[]{:S(2)}) collective-permute-start(bf16[2,512,128]{2,1,0:T(8,128)(2,1)S(1)} %get-tuple-element.52), channel_id=1, source_target_pairs={{0,1},{1,0},{2,3},{3,2},{4,5},{5,4},{6,7},{7,6},{8,9},{9,8},{10,11... | collective-permute-start | bytes 786440 | tf_op jit(solution)/shard_map/ppermute | solution.py:603
  41.4 3.4 %collective-permute-start.9 = (bf16[2,512,128]{2,1,0:T(8,128)(2,1)S(1)}, bf16[2,512,128]{2,1,0:T(8,128)(2,1)S(1)}, u32[]{:S(2)}, u32[]{:S(2)}) collective-permute-start(bf16[2,512,128]{2,1,0:T(8,128)(2,1)S(1)} %get-tuple-element.53), channel_id=1, source_target_pairs={{1,2},{3,4},{5,6},{2,1},{4,3},{6,5},{9,10},{11,12},{13,14},{10,9},... | collective-permute-start | bytes 786440 | tf_op jit(solution)/shard_map/ppermute | solution.py:603
  44.8 4.6 %attend_near.1.refs_6_ = bf16[4,512,128]{2,1,0:T(8,128)(2,1)S(1)} custom-call(s32[4,2]{1,0:T(4,128)S(1)} %copy.16.partners, bf16[4,512,128]{2,1,0:T(8,128)(2,1)S(1)} %collective-permute-done.2.refs_0_, bf16[4,512,128]{2,1,0:T(8,128)(2,1)S(1)} %collective-permute-done.3.refs_1_.refs_0_, bf16[4,512,128]{2,1,0:T(8,128)(2,1)S(1)} %collective-permute-done.4.refs_0_.refs_2_, ...), custom_call_target="tpu_custom_call" | custom-call | tf_op jit(solution)/shard_map/attend_near/pallas_call | solution.py:493
  49.5 0.0 collective-permute-done.8.refs_2_
  49.5 0.0 collective-permute-done.9.refs_3_
  49.5 3.0 %attend_ends.1 = (bf16[2,512,128]{2,1,0:T(8,128)(2,1)S(1)}, bf16[1,512,128]{2,1,0:T(8,128)(2,1)}, bf16[1,512,128]{2,1,0:T(8,128)(2,1)S(1)}, bf16[1,512,128]{2,1,0:T(8,128)(2,1)S(1)}, bf16[1,512,128]{2,1,0:T(8,128)(2,1)S(1)}) custom-call(s32[4,2]{1,0:T(4,128)S(1)} %copy.16.partners, bf16[4,512,128]{2,1,0:T(8,128)(2,1)S(1)} %collective-permute-done.2.refs_0_, ...), custom_call_target="tpu_custom_call" | custom-call | tf_op jit(solution)/shard_map/attend_ends/pallas_call | solution.py:529
  52.5 0.0 collective-permute-done.7.refs_3_
  52.5 0.0 collective-permute-done.6.refs_1_
  52.5 1.3 %collective-permute-start.11 = (bf16[1,512,128]{2,1,0:T(8,128)(2,1)S(1)}, bf16[1,512,128]{2,1,0:T(8,128)(2,1)S(1)}, u32[]{:S(2)}, u32[]{:S(2)}) collective-permute-start(bf16[1,512,128]{2,1,0:T(8,128)(2,1)S(1)} %get-tuple-element.66), channel_id=1, source_target_pairs={{0,16},{8,24},{16,0},{24,8},{1,17},{9,25},{17,1},{25,9},{2,18},{10... | collective-permute-start | bytes 393224 | tf_op jit(solution)/shard_map/ppermute | solution.py:585
  53.8 0.3 collective-permute-start.10
  54.1 6.9 %attend_far.1.refs_11_ = f32[6,512,128]{2,1,0:T(8,128)S(1)} custom-call(s32[4,2]{1,0:T(4,128)S(1)} %copy.16.partners, bf16[4,512,128]{2,1,0:T(8,128)(2,1)S(1)} %collective-permute-done.3.refs_1_.refs_0_, bf16[4,512,128]{2,1,0:T(8,128)(2,1)S(1)} %collective-permute-done.6.refs_1_, bf16[4,512,128]{2,1,0:T(8,128)(2,1)S(1)} %collective-permute-done.5.refs_1_.refs_3_.refs_2_, ...), custom_call_target="tpu_custom_call" | custom-call | tf_op jit(solution)/shard_map/attend_far/pallas_call | solution.py:510
  61.0 0.0 collective-permute-done.11.refs_5_
  61.0 0.0 collective-permute-done.10.refs_3_
  61.0 4.0 %attend_outer.1 = f32[8,512,128]{2,1,0:T(8,128)} custom-call(s32[4,2]{1,0:T(4,128)S(1)} %copy.16.partners, bf16[4,512,128]{2,1,0:T(8,128)(2,1)S(1)} %collective-permute-done.3.refs_1_.refs_0_, bf16[4,512,128]{2,1,0:T(8,128)(2,1)S(1)} %collective-permute-done.6.refs_1_, bf16[1,512,128]{2,1,0:T(8,128)(2,1)S(1)} %get-tuple-element.64.refs_2_, ...), custom_call_target="tpu_custom_call" | custom-call | tf_op jit(solution)/shard_map/attend_outer/pallas_call | solution.py:546
  (18 shorter events, 0.1 us)
Async XLA Ops:
  0.0 24.7 %copy-start = (bf16[128,128]{1,0:T(8,128)(2,1)S(1)}, bf16[128,128]{1,0:T(8,128)(2,1)}, u32[]{:S(2)}) copy-start(bf16[128,128]{1,0:T(8,128)(2,1)} %param.18) | copy-start | bytes 98308
  0.0 7.0 %copy-start.1 = (f32[1,8,512,128]{3,2,1,0:T(8,128)S(1)}, f32[1,8,512,128]{3,2,1,0:T(8,128)}, u32[]{:S(2)}) copy-start(f32[1,8,512,128]{3,2,1,0:T(8,128)} %param.11) | copy-start | bytes 6291460
  7.0 9.3 %copy-start.4 = (bf16[3,3,128,128]{3,2,1,0:T(8,128)(2,1)S(1)}, bf16[3,3,128,128]{3,2,1,0:T(8,128)(2,1)}, u32[]{:S(2)}) copy-start(bf16[3,3,128,128]{3,2,1,0:T(8,128)(2,1)} %one.3) | copy-start | bytes 884740
  7.0 9.3 %copy-start.5 = (bf16[3,3,128,128]{3,2,1,0:T(8,128)(2,1)S(1)}, bf16[3,3,128,128]{3,2,1,0:T(8,128)(2,1)}, u32[]{:S(2)}) copy-start(bf16[3,3,128,128]{3,2,1,0:T(8,128)(2,1)} %two.3) | copy-start | bytes 884740
  7.0 9.3 %copy-start.6 = (f32[4,512,128]{2,1,0:T(8,128)S(1)}, f32[4,512,128]{2,1,0:T(8,128)}, u32[]{:S(2)}) copy-start(f32[4,512,128]{2,1,0:T(8,128)} %get-tuple-element.42.state_one) | copy-start | bytes 3145732
  7.0 9.3 %copy-start.11 = (f32[128]{0:T(128)S(1)}, f32[128]{0:T(128)}, u32[]{:S(2)}) copy-start(f32[128]{0:T(128)} %param.20) | copy-start | bytes 1540
  7.3 9.1 %collective-permute-start.1 = (bf16[2,512,128]{2,1,0:T(8,128)(2,1)S(1)}, bf16[2,512,128]{2,1,0:T(8,128)(2,1)S(1)}, u32[]{:S(2)}, u32[]{:S(2)}) collective-permute-start(bf16[2,512,128]{2,1,0:T(8,128)(2,1)S(1)} %get-tuple-element.75), channel_id=1, source_target_pairs={{1,2},{3,4},{5,6},{2,1},{4,3},{6,5},{9,10},{11,12},{13,14},{10,9},... | collective-permute-start | bytes 786440 | tf_op jit(solution)/shard_map/ppermute | solution.py:603
  12.0 4.3 %collective-permute-start = (bf16[2,512,128]{2,1,0:T(8,128)(2,1)S(1)}, bf16[2,512,128]{2,1,0:T(8,128)(2,1)S(1)}, u32[]{:S(2)}, u32[]{:S(2)}) collective-permute-start(bf16[2,512,128]{2,1,0:T(8,128)(2,1)S(1)} %get-tuple-element.76), channel_id=1, source_target_pairs={{0,1},{1,0},{2,3},{3,2},{4,5},{5,4},{6,7},{7,6},{8,9},{9,8},{10,11... | collective-permute-start | bytes 786440 | tf_op jit(solution)/shard_map/ppermute | solution.py:603
  12.1 13.3 %collective-permute-start.5 = (bf16[4,512,128]{2,1,0:T(8,128)(2,1)}, bf16[4,512,128]{2,1,0:T(8,128)(2,1)S(1)}, u32[]{:S(2)}, u32[]{:S(2)}) collective-permute-start(bf16[4,512,128]{2,1,0:T(8,128)(2,1)} %get-tuple-element.44.refs_3_), channel_id=1, source_target_pairs={{0,16},{8,24},{16,0},{24,8},{1,17},{9,25},{17,1},{25,9},{2,18},{10... | collective-permute-start | bytes 1572872 | tf_op jit(solution)/shard_map/ppermute | solution.py:585
  13.4 13.0 %collective-permute-start.4 = (bf16[4,512,128]{2,1,0:T(8,128)(2,1)}, bf16[4,512,128]{2,1,0:T(8,128)(2,1)S(1)}, u32[]{:S(2)}, u32[]{:S(2)}) collective-permute-start(bf16[4,512,128]{2,1,0:T(8,128)(2,1)} %get-tuple-element.44.refs_3_), channel_id=1, source_target_pairs={{0,8},{8,0},{16,24},{24,16},{1,9},{9,1},{17,25},{25,17},{2,10},{10... | collective-permute-start | bytes 1572872 | tf_op jit(solution)/shard_map/ppermute | solution.py:585
  16.4 8.3 %copy-start.14 = (s32[4,2]{0,1:T(2,128)S(1)}, s32[4,2]{0,1:T(2,128)}, u32[]{:S(2)}) copy-start(s32[4,2]{0,1:T(2,128)} %param.13) | copy-start | bytes 100
  16.4 8.3 %copy-start.13 = (bf16[128,128]{1,0:T(8,128)(2,1)S(1)}, bf16[128,128]{1,0:T(8,128)(2,1)}, u32[]{:S(2)}) copy-start(bf16[128,128]{1,0:T(8,128)(2,1)} %param.19) | copy-start | bytes 98308
  16.4 10.0 %copy-start.8 = (bf16[128,128]{1,0:T(8,128)(2,1)S(1)}, bf16[128,128]{1,0:T(8,128)(2,1)}, u32[]{:S(2)}) copy-start(bf16[128,128]{1,0:T(8,128)(2,1)} %refs_4_.1) | copy-start | bytes 98308
  16.4 9.9 %copy-start.9 = (bf16[128,128]{1,0:T(8,128)(2,1)S(1)}, bf16[128,128]{1,0:T(8,128)(2,1)}, u32[]{:S(2)}) copy-start(bf16[128,128]{1,0:T(8,128)(2,1)} %refs_5_.1) | copy-start | bytes 98308
  16.4 9.9 %copy-start.10 = (f32[1,8,512]{2,1,0:T(8,128)S(1)}, f32[1,8,512]{2,1,0:T(8,128)}, u32[]{:S(2)}) copy-start(f32[1,8,512]{2,1,0:T(8,128)} %param.12) | copy-start | bytes 49156
  21.2 1.0 %copy-start.2 = (f32[4,512,128]{2,1,0:T(8,128)}, f32[4,512,128]{2,1,0:T(8,128)S(1)}, u32[]{:S(2)}) copy-start(f32[4,512,128]{2,1,0:T(8,128)S(1)} %get-tuple-element.68.refs_8_) | copy-start | bytes 3145732
  22.2 14.5 %collective-permute-start.3 = (bf16[4,512,128]{2,1,0:T(8,128)(2,1)}, bf16[4,512,128]{2,1,0:T(8,128)(2,1)S(1)}, u32[]{:S(2)}, u32[]{:S(2)}) collective-permute-start(bf16[4,512,128]{2,1,0:T(8,128)(2,1)} %get-tuple-element.43.refs_2_), channel_id=1, source_target_pairs={{0,16},{8,24},{16,0},{24,8},{1,17},{9,25},{17,1},{25,9},{2,18},{10... | collective-permute-start | bytes 1572872 | tf_op jit(solution)/shard_map/ppermute | solution.py:585
  23.4 14.2 %collective-permute-start.2 = (bf16[4,512,128]{2,1,0:T(8,128)(2,1)}, bf16[4,512,128]{2,1,0:T(8,128)(2,1)S(1)}, u32[]{:S(2)}, u32[]{:S(2)}) collective-permute-start(bf16[4,512,128]{2,1,0:T(8,128)(2,1)} %get-tuple-element.43.refs_2_), channel_id=1, source_target_pairs={{0,8},{8,0},{16,24},{24,16},{1,9},{9,1},{17,25},{25,17},{2,10},{10... | collective-permute-start | bytes 1572872 | tf_op jit(solution)/shard_map/ppermute | solution.py:585
  37.6 14.9 %collective-permute-start.7 = (bf16[4,512,128]{2,1,0:T(8,128)(2,1)S(1)}, bf16[4,512,128]{2,1,0:T(8,128)(2,1)S(1)}, u32[]{:S(2)}, u32[]{:S(2)}) collective-permute-start(bf16[4,512,128]{2,1,0:T(8,128)(2,1)S(1)} %collective-permute-done.5.refs_1_.refs_3_.refs_2_), channel_id=1, source_target_pairs={{0,8},{8,0},{16,24},{24,16},{1,9},{9,1},{17,25},{25,17},{2,10},{10... | collective-permute-start | bytes 1572872 | tf_op jit(solution)/shard_map/ppermute | solution.py:585
  38.8 13.7 %collective-permute-start.6 = (bf16[4,512,128]{2,1,0:T(8,128)(2,1)S(1)}, bf16[4,512,128]{2,1,0:T(8,128)(2,1)S(1)}, u32[]{:S(2)}, u32[]{:S(2)}) collective-permute-start(bf16[4,512,128]{2,1,0:T(8,128)(2,1)S(1)} %collective-permute-done.2.refs_0_), channel_id=1, source_target_pairs={{0,16},{8,24},{16,0},{24,8},{1,17},{9,25},{17,1},{25,9},{2,18},{10... | collective-permute-start | bytes 1572872 | tf_op jit(solution)/shard_map/ppermute | solution.py:585
  39.2 10.2 %collective-permute-start.8 = (bf16[2,512,128]{2,1,0:T(8,128)(2,1)S(1)}, bf16[2,512,128]{2,1,0:T(8,128)(2,1)S(1)}, u32[]{:S(2)}, u32[]{:S(2)}) collective-permute-start(bf16[2,512,128]{2,1,0:T(8,128)(2,1)S(1)} %get-tuple-element.52), channel_id=1, source_target_pairs={{0,1},{1,0},{2,3},{3,2},{4,5},{5,4},{6,7},{7,6},{8,9},{9,8},{10,11... | collective-permute-start | bytes 786440 | tf_op jit(solution)/shard_map/ppermute | solution.py:603
  41.3 12.7 %copy-start.3 = (f32[4,512,128]{2,1,0:T(8,128)S(1)}, f32[4,512,128]{2,1,0:T(8,128)}, u32[]{:S(2)}) copy-start(f32[4,512,128]{2,1,0:T(8,128)} %copy-done.2) | copy-start | bytes 3145732
  41.4 12.7 %copy-start.7 = (f32[4,512,128]{2,1,0:T(8,128)S(1)}, f32[4,512,128]{2,1,0:T(8,128)}, u32[]{:S(2)}) copy-start(f32[4,512,128]{2,1,0:T(8,128)} %get-tuple-element.74.refs_9_) | copy-start | bytes 3145732
  41.4 12.7 %copy-start.12 = (f32[128]{0:T(128)S(1)}, f32[128]{0:T(128)}, u32[]{:S(2)}) copy-start(f32[128]{0:T(128)} %param.21) | copy-start | bytes 1540
  41.4 8.1 %collective-permute-start.9 = (bf16[2,512,128]{2,1,0:T(8,128)(2,1)S(1)}, bf16[2,512,128]{2,1,0:T(8,128)(2,1)S(1)}, u32[]{:S(2)}, u32[]{:S(2)}) collective-permute-start(bf16[2,512,128]{2,1,0:T(8,128)(2,1)S(1)} %get-tuple-element.53), channel_id=1, source_target_pairs={{1,2},{3,4},{5,6},{2,1},{4,3},{6,5},{9,10},{11,12},{13,14},{10,9},... | collective-permute-start | bytes 786440 | tf_op jit(solution)/shard_map/ppermute | solution.py:603
  52.5 8.5 %collective-permute-start.11 = (bf16[1,512,128]{2,1,0:T(8,128)(2,1)S(1)}, bf16[1,512,128]{2,1,0:T(8,128)(2,1)S(1)}, u32[]{:S(2)}, u32[]{:S(2)}) collective-permute-start(bf16[1,512,128]{2,1,0:T(8,128)(2,1)S(1)} %get-tuple-element.66), channel_id=1, source_target_pairs={{0,16},{8,24},{16,0},{24,8},{1,17},{9,25},{17,1},{25,9},{2,18},{10... | collective-permute-start | bytes 393224 | tf_op jit(solution)/shard_map/ppermute | solution.py:585
  53.8 7.2 %collective-permute-start.10 = (bf16[1,512,128]{2,1,0:T(8,128)(2,1)S(1)}, bf16[1,512,128]{2,1,0:T(8,128)(2,1)S(1)}, u32[]{:S(2)}, u32[]{:S(2)}) collective-permute-start(bf16[1,512,128]{2,1,0:T(8,128)(2,1)S(1)} %get-tuple-element.64.refs_2_), channel_id=1, source_target_pairs={{0,8},{8,0},{16,24},{24,16},{1,9},{9,1},{17,25},{25,17},{2,10},{10... | collective-permute-start | bytes 393224 | tf_op jit(solution)/shard_map/ppermute | solution.py:585

commit v5 on v4

--- a/solution.py
+++ b/solution.py
@@ -10,7 +10,7 @@
 
 epsilon = 1e-06
 vmem_bytes = 28 * 1024 * 1024
-edge_vmem_bytes = 36 * 1024 * 1024
+edge_vmem_bytes = 50 * 1024 * 1024
 whole_vmem_bytes = 56 * 1024 * 1024
 in_vmem = pl.BlockSpec(memory_space=pltpu.VMEM)
 in_smem = pl.BlockSpec(memory_space=pltpu.SMEM)
@@ -24,10 +24,7 @@
 
 
 def scaled(values, gain):
-    channels = values.shape[-1]
-    squares = (values * values).astype(jnp.bfloat16)
-    ones = jnp.ones((channels, channels), jnp.bfloat16)
-    mean_square = jnp.dot(squares, ones, preferred_element_type=jnp.float32) * (1.0 / channels)
+    mean_square = jnp.mean(values * values, axis=-1, keepdims=True)
     return values * lax.rsqrt(mean_square + epsilon) * gain
 
 
@@ -144,13 +141,19 @@
         convolve_one(first)
         for r in range(first + 4, min(first + 6, rows)):
             place(silu(held[r]), x1, r)
-        if first >= 2:
+        if 2 <= first < rows - 4:
             convolve_two(first - 2)
     stores = [
-        copies.start(norm, norm_out),
         copies.start(state_one.at[pl.ds(0, 2)], state_one_out.at[pl.ds(0, 2)]),
         copies.start(state_one.at[pl.ds(rows - 4, 2)], state_one_out.at[pl.ds(2, 2)]),
-        copies.start(state_two, state_out),
+        copies.start(norm.at[pl.ds(0, rows - 6)], norm_out.at[pl.ds(0, rows - 6)]),
+        copies.start(state_two.at[pl.ds(0, rows - 6)], state_out.at[pl.ds(0, rows - 6)]),
+    ]
+    convolve_two(rows - 6)
+    last = pl.ds(rows - 6, 2)
+    stores += [
+        copies.start(norm.at[last], norm_out.at[last]),
+        copies.start(state_two.at[last], state_out.at[last]),
     ]
     for store in stores:
         store.wait()
@@ -186,7 +189,7 @@
                 ((rows, *padded), jnp.float32),
                 ((rows - 2, *padded), jnp.float32),
             ),
-            pltpu.SemaphoreType.DMA((rows + 7,)),
+            pltpu.SemaphoreType.DMA((rows + 9,)),
         ],
         compiler_params=pltpu.CompilerParams(vmem_limit_bytes=whole_vmem_bytes),
         cost_estimate=no_cost,

time: 65.5 us -> 64.3 us (0.982)
  Pallas kernels: 34.4 us -> 33.4 us
  local copies, waits for them, and re-layouts: 1.13 us -> 0.16 us
  waiting for transfers between devices: 10.4 us -> 11.2 us
    unnamed x31 -> x27, local copies, waits for them, and re-layouts: 1.13 us -> 0.16 us
    pallas_call x1, Pallas kernels: 6.98 us -> 6.02 us  [middle_rows(): pl.pallas_call(middle_body, in_specs=[anywhere] * 4, out_specs=[anywhere]...]
    ppermute x8, waiting for transfers between devices: 8.65 us -> 9.43 us  [swap(): return lax.ppermute(cells, 'view', [(i, i ^ offset) for i in range(views)])]
  transfers between devices with their start and end apart: 12 -> 12, of which waited for: 5 -> 5; matrix products, arithmetic and copies ran while one was open for 0% -> 0% of each run, Pallas kernels for 36% -> 37%
where the time goes in v5:
time: 64.3 us; the launch traced here: 64 us
  Pallas kernels  33.4 us (52%)
  starting transfers between devices  18.5 us (29%)
  waiting for transfers between devices  11.2 us (17%)
    ppermute x8, waiting for transfers between devices, swap(): return lax.ppermute(cells, 'view', [(i, i ^ offset) for i in range(views)])  9.43 us
    ppermute x2, starting transfers between devices, swap_bands(): lax.ppermute(cross, 'band', crosses)  8.16 us
    ppermute x8, starting transfers between devices, swap(): return lax.ppermute(cells, 'view', [(i, i ^ offset) for i in range(views)])  8.14 us
    pallas_call x1, Pallas kernels, attend_far(): pl.pallas_call(functools.partial(attend_far_body, low, len(candidates[0])...  6.75 us
    pallas_call x1, Pallas kernels, middle_rows(): pl.pallas_call(middle_body, in_specs=[anywhere] * 4, out_specs=[anywhere]...  6.02 us
    pallas_call x1, Pallas kernels, edge_rows(): pl.pallas_call(edge_body, in_specs=[anywhere] + [in_vmem] * 2 + [anywhere...  4.88 us
    pallas_call x1, Pallas kernels, attend_near(): pl.pallas_call(functools.partial(attend_near_body, low, len(candidates[0]...  4.64 us
    pallas_call x1, Pallas kernels, attend_first(): pl.pallas_call(functools.partial(attend_first_body, low, len(middles)), i...  4.07 us
  transfers between devices with their start and end apart: 12, of which 5 were waited for; matrix products, arithmetic and copies ran while one was open for 0% of the time, Pallas kernels for 37%

profile of v5, /device:TPU:1, one launch (start us, length us, event | category | flops | bytes accessed | tf_op | source)
XLA Modules:
  0.0 64.0 jit_solution(15133085573609903286)
XLA Ops:
  0.0 6.0 %residual_middle.1 = (f32[4,512,128]{2,1,0:T(8,128)}, f32[4,512,128]{2,1,0:T(8,128)}, bf16[4,512,128]{2,1,0:T(8,128)(2,1)}) custom-call(f32[8,512,128]{2,1,0:T(8,128)} %bitcast.12, bf16[3,3,128,128]{3,2,1,0:T(8,128)(2,1)} %one.3, bf16[3,3,128,128]{3,2,1,0:T(8,128)(2,1)} %two.3, f32[1,128]{1,0:T(1,128)} %bitcast.8), custom_call_target="tpu_custom_call" | custom-call | tf_op jit(solution)/shard_map/residual_middle/pallas_call | solution.py:172
  6.0 0.0 copy-start.1
  6.1 0.0 copy-start.2
  6.1 0.0 copy-start.3
  6.1 0.0 copy-start.8
  6.1 0.2 convert.4
  6.3 4.7 %collective-permute-start.1 = (bf16[2,512,128]{2,1,0:T(8,128)(2,1)S(1)}, bf16[2,512,128]{2,1,0:T(8,128)(2,1)S(1)}, u32[]{:S(2)}, u32[]{:S(2)}) collective-permute-start(bf16[2,512,128]{2,1,0:T(8,128)(2,1)S(1)} %get-tuple-element.75), channel_id=1, source_target_pairs={{1,2},{3,4},{5,6},{2,1},{4,3},{6,5},{9,10},{11,12},{13,14},{10,9},... | collective-permute-start | bytes 786440 | tf_op jit(solution)/shard_map/ppermute | solution.py:606
  11.0 0.1 collective-permute-start
  11.1 1.3 %collective-permute-start.5 = (bf16[4,512,128]{2,1,0:T(8,128)(2,1)}, bf16[4,512,128]{2,1,0:T(8,128)(2,1)S(1)}, u32[]{:S(2)}, u32[]{:S(2)}) collective-permute-start(bf16[4,512,128]{2,1,0:T(8,128)(2,1)} %get-tuple-element.44.refs_3_), channel_id=1, source_target_pairs={{0,16},{8,24},{16,0},{24,8},{1,17},{9,25},{17,1},{25,9},{2,18},{10... | collective-permute-start | bytes 1572872 | tf_op jit(solution)/shard_map/ppermute | solution.py:588
  12.4 1.2 %collective-permute-start.4 = (bf16[4,512,128]{2,1,0:T(8,128)(2,1)}, bf16[4,512,128]{2,1,0:T(8,128)(2,1)S(1)}, u32[]{:S(2)}, u32[]{:S(2)}) collective-permute-start(bf16[4,512,128]{2,1,0:T(8,128)(2,1)} %get-tuple-element.44.refs_3_), channel_id=1, source_target_pairs={{0,8},{8,0},{16,24},{24,16},{1,9},{9,1},{17,25},{25,17},{2,10},{10... | collective-permute-start | bytes 1572872 | tf_op jit(solution)/shard_map/ppermute | solution.py:588
  13.6 1.7 %collective-permute-done.1.cross = bf16[2,512,128]{2,1,0:T(8,128)(2,1)S(1)} collective-permute-done((bf16[2,512,128]{2,1,0:T(8,128)(2,1)S(1)}, bf16[2,512,128]{2,1,0:T(8,128)(2,1)S(1)}, u32[]{:S(2)}, u32[]{:S(2)}) %collective-permute-start.1) | collective-permute-done | bytes 262176 | tf_op jit(solution)/shard_map/ppermute | solution.py:606
  15.4 0.0 collective-permute-done.mate
  15.4 0.0 copy-done.2
  15.4 0.0 copy-start.12
  15.4 0.0 copy-start.11
  15.4 0.0 copy-start.5
  15.4 0.0 copy-start.6
  15.5 0.0 copy-start.7
  15.5 4.9 %residual_edge.1 = (f32[4,512,128]{2,1,0:T(8,128)S(1)}, bf16[4,512,128]{2,1,0:T(8,128)(2,1)}) custom-call(f32[8,512,128]{2,1,0:T(8,128)} %bitcast.13, bf16[2,512,128]{2,1,0:T(8,128)(2,1)S(1)} %collective-permute-done.mate, bf16[2,512,128]{2,1,0:T(8,128)(2,1)S(1)} %collective-permute-done.1.cross, bf16[3,3,128,128]{3,2,1,0:T(8,128)(2,1)S(1)} %copy-done.1, ...), custom_call_target="tpu_custom_call" | custom-call | tf_op jit(solution)/shard_map/residual_edge/pallas_call | solution.py:269
  20.4 1.3 %collective-permute-start.3 = (bf16[4,512,128]{2,1,0:T(8,128)(2,1)}, bf16[4,512,128]{2,1,0:T(8,128)(2,1)S(1)}, u32[]{:S(2)}, u32[]{:S(2)}) collective-permute-start(bf16[4,512,128]{2,1,0:T(8,128)(2,1)} %get-tuple-element.43.refs_2_), channel_id=1, source_target_pairs={{0,16},{8,24},{16,0},{24,8},{1,17},{9,25},{17,1},{25,9},{2,18},{10... | collective-permute-start | bytes 1572872 | tf_op jit(solution)/shard_map/ppermute | solution.py:588
  21.7 1.2 %collective-permute-start.2 = (bf16[4,512,128]{2,1,0:T(8,128)(2,1)}, bf16[4,512,128]{2,1,0:T(8,128)(2,1)S(1)}, u32[]{:S(2)}, u32[]{:S(2)}) collective-permute-start(bf16[4,512,128]{2,1,0:T(8,128)(2,1)} %get-tuple-element.43.refs_2_), channel_id=1, source_target_pairs={{0,8},{8,0},{16,24},{24,16},{1,9},{9,1},{17,25},{25,17},{2,10},{10... | collective-permute-start | bytes 1572872 | tf_op jit(solution)/shard_map/ppermute | solution.py:588
  22.9 0.0 copy-done.12
  22.9 0.1 copy.16.partners
  23.0 0.1 convolution_convert_fusion.refs_10_.refs_9_
  23.1 1.3 %collective-permute-done.5.refs_1_.refs_3_.refs_2_ = bf16[4,512,128]{2,1,0:T(8,128)(2,1)S(1)} collective-permute-done((bf16[4,512,128]{2,1,0:T(8,128)(2,1)}, bf16[4,512,128]{2,1,0:T(8,128)(2,1)S(1)}, u32[]{:S(2)}, u32[]{:S(2)}) %collective-permute-start.5) | collective-permute-done | bytes 524320 | tf_op jit(solution)/shard_map/ppermute | solution.py:588
  24.5 0.9 %collective-permute-done.4.refs_0_.refs_2_ = bf16[4,512,128]{2,1,0:T(8,128)(2,1)S(1)} collective-permute-done((bf16[4,512,128]{2,1,0:T(8,128)(2,1)}, bf16[4,512,128]{2,1,0:T(8,128)(2,1)S(1)}, u32[]{:S(2)}, u32[]{:S(2)}) %collective-permute-start.4) | collective-permute-done | bytes 524320 | tf_op jit(solution)/shard_map/ppermute | solution.py:588
  25.4 0.0 copy-done.6
  25.4 4.1 %attend_first.1 = (bf16[4,512,128]{2,1,0:T(8,128)(2,1)S(1)}, bf16[4,512,128]{2,1,0:T(8,128)(2,1)S(1)}, bf16[2,512,128]{2,1,0:T(8,128)(2,1)S(1)}) custom-call(s32[4,2]{1,0:T(4,128)S(1)} %copy.16.partners, bf16[4,512,128]{2,1,0:T(8,128)(2,1)S(1)} %collective-permute-done.4.refs_0_.refs_2_, ...), custom_call_target="tpu_custom_call" | custom-call | tf_op jit(solution)/shard_map/attend_first/pallas_call | solution.py:476
  29.5 6.2 %collective-permute-done.3.refs_1_.refs_0_ = bf16[4,512,128]{2,1,0:T(8,128)(2,1)S(1)} collective-permute-done((bf16[4,512,128]{2,1,0:T(8,128)(2,1)}, bf16[4,512,128]{2,1,0:T(8,128)(2,1)S(1)}, u32[]{:S(2)}, u32[]{:S(2)}) %collective-permute-start.3) | collective-permute-done | bytes 524320 | tf_op jit(solution)/shard_map/ppermute | solution.py:588
  35.7 0.9 %collective-permute-done.2.refs_0_ = bf16[4,512,128]{2,1,0:T(8,128)(2,1)S(1)} collective-permute-done((bf16[4,512,128]{2,1,0:T(8,128)(2,1)}, bf16[4,512,128]{2,1,0:T(8,128)(2,1)S(1)}, u32[]{:S(2)}, u32[]{:S(2)}) %collective-permute-start.2) | collective-permute-done | bytes 524320 | tf_op jit(solution)/shard_map/ppermute | solution.py:588
  36.6 1.2 %collective-permute-start.7 = (bf16[4,512,128]{2,1,0:T(8,128)(2,1)S(1)}, bf16[4,512,128]{2,1,0:T(8,128)(2,1)S(1)}, u32[]{:S(2)}, u32[]{:S(2)}) collective-permute-start(bf16[4,512,128]{2,1,0:T(8,128)(2,1)S(1)} %collective-permute-done.5.refs_1_.refs_3_.refs_2_), channel_id=1, source_target_pairs={{0,8},{8,0},{16,24},{24,16},{1,9},{9,1},{17,25},{25,17},{2,10},{10... | collective-permute-start | bytes 1572872 | tf_op jit(solution)/shard_map/ppermute | solution.py:588
  37.8 0.3 collective-permute-start.6
  38.2 0.1 edge_halos.1
  38.3 2.1 %collective-permute-start.8 = (bf16[2,512,128]{2,1,0:T(8,128)(2,1)S(1)}, bf16[2,512,128]{2,1,0:T(8,128)(2,1)S(1)}, u32[]{:S(2)}, u32[]{:S(2)}) collective-permute-start(bf16[2,512,128]{2,1,0:T(8,128)(2,1)S(1)} %get-tuple-element.52), channel_id=1, source_target_pairs={{0,1},{1,0},{2,3},{3,2},{4,5},{5,4},{6,7},{7,6},{8,9},{9,8},{10,11... | collective-permute-start | bytes 786440 | tf_op jit(solution)/shard_map/ppermute | solution.py:606
  40.4 3.4 %collective-permute-start.9 = (bf16[2,512,128]{2,1,0:T(8,128)(2,1)S(1)}, bf16[2,512,128]{2,1,0:T(8,128)(2,1)S(1)}, u32[]{:S(2)}, u32[]{:S(2)}) collective-permute-start(bf16[2,512,128]{2,1,0:T(8,128)(2,1)S(1)} %get-tuple-element.53), channel_id=1, source_target_pairs={{1,2},{3,4},{5,6},{2,1},{4,3},{6,5},{9,10},{11,12},{13,14},{10,9},... | collective-permute-start | bytes 786440 | tf_op jit(solution)/shard_map/ppermute | solution.py:606
  43.8 4.6 %attend_near.1.refs_6_ = bf16[4,512,128]{2,1,0:T(8,128)(2,1)S(1)} custom-call(s32[4,2]{1,0:T(4,128)S(1)} %copy.16.partners, bf16[4,512,128]{2,1,0:T(8,128)(2,1)S(1)} %collective-permute-done.2.refs_0_, bf16[4,512,128]{2,1,0:T(8,128)(2,1)S(1)} %collective-permute-done.3.refs_1_.refs_0_, bf16[4,512,128]{2,1,0:T(8,128)(2,1)S(1)} %collective-permute-done.4.refs_0_.refs_2_, ...), custom_call_target="tpu_custom_call" | custom-call | tf_op jit(solution)/shard_map/attend_near/pallas_call | solution.py:496
  48.5 0.0 collective-permute-done.8.refs_2_
  48.5 0.0 collective-permute-done.9.refs_3_
  48.5 3.0 %attend_ends.1 = (bf16[2,512,128]{2,1,0:T(8,128)(2,1)S(1)}, bf16[1,512,128]{2,1,0:T(8,128)(2,1)}, bf16[1,512,128]{2,1,0:T(8,128)(2,1)S(1)}, bf16[1,512,128]{2,1,0:T(8,128)(2,1)S(1)}, bf16[1,512,128]{2,1,0:T(8,128)(2,1)S(1)}) custom-call(s32[4,2]{1,0:T(4,128)S(1)} %copy.16.partners, bf16[4,512,128]{2,1,0:T(8,128)(2,1)S(1)} %collective-permute-done.2.refs_0_, ...), custom_call_target="tpu_custom_call" | custom-call | tf_op jit(solution)/shard_map/attend_ends/pallas_call | solution.py:532
  51.5 0.0 collective-permute-done.7.refs_3_
  51.5 0.0 collective-permute-done.6.refs_1_
  51.5 1.3 %collective-permute-start.11 = (bf16[1,512,128]{2,1,0:T(8,128)(2,1)S(1)}, bf16[1,512,128]{2,1,0:T(8,128)(2,1)S(1)}, u32[]{:S(2)}, u32[]{:S(2)}) collective-permute-start(bf16[1,512,128]{2,1,0:T(8,128)(2,1)S(1)} %get-tuple-element.66), channel_id=1, source_target_pairs={{0,16},{8,24},{16,0},{24,8},{1,17},{9,25},{17,1},{25,9},{2,18},{10... | collective-permute-start | bytes 393224 | tf_op jit(solution)/shard_map/ppermute | solution.py:588
  52.9 0.3 collective-permute-start.10
  53.1 0.0 copy-done.4
  53.1 6.8 %attend_far.1.refs_11_ = f32[6,512,128]{2,1,0:T(8,128)S(1)} custom-call(s32[4,2]{1,0:T(4,128)S(1)} %copy.16.partners, bf16[4,512,128]{2,1,0:T(8,128)(2,1)S(1)} %collective-permute-done.3.refs_1_.refs_0_, bf16[4,512,128]{2,1,0:T(8,128)(2,1)S(1)} %collective-permute-done.6.refs_1_, bf16[4,512,128]{2,1,0:T(8,128)(2,1)S(1)} %collective-permute-done.5.refs_1_.refs_3_.refs_2_, ...), custom_call_target="tpu_custom_call" | custom-call | tf_op jit(solution)/shard_map/attend_far/pallas_call | solution.py:513
  59.9 0.0 collective-permute-done.11.refs_5_
  59.9 0.0 collective-permute-done.10.refs_3_
  59.9 3.9 %attend_outer.1 = f32[8,512,128]{2,1,0:T(8,128)} custom-call(s32[4,2]{1,0:T(4,128)S(1)} %copy.16.partners, bf16[4,512,128]{2,1,0:T(8,128)(2,1)S(1)} %collective-permute-done.3.refs_1_.refs_0_, bf16[4,512,128]{2,1,0:T(8,128)(2,1)S(1)} %collective-permute-done.6.refs_1_, bf16[1,512,128]{2,1,0:T(8,128)(2,1)S(1)} %get-tuple-element.64.refs_2_, ...), custom_call_target="tpu_custom_call" | custom-call | tf_op jit(solution)/shard_map/attend_outer/pallas_call | solution.py:549
  (14 shorter events, 0.1 us)
Async XLA Ops:
  0.0 23.0 %copy-start = (bf16[128,128]{1,0:T(8,128)(2,1)S(1)}, bf16[128,128]{1,0:T(8,128)(2,1)}, u32[]{:S(2)}) copy-start(bf16[128,128]{1,0:T(8,128)(2,1)} %param.18) | copy-start | bytes 98308
  0.0 6.0 %copy-start.10 = (f32[1,8,512,128]{3,2,1,0:T(8,128)S(1)}, f32[1,8,512,128]{3,2,1,0:T(8,128)}, u32[]{:S(2)}) copy-start(f32[1,8,512,128]{3,2,1,0:T(8,128)} %param.11) | copy-start | bytes 6291460
  6.0 9.3 %copy-start.1 = (bf16[3,3,128,128]{3,2,1,0:T(8,128)(2,1)S(1)}, bf16[3,3,128,128]{3,2,1,0:T(8,128)(2,1)}, u32[]{:S(2)}) copy-start(bf16[3,3,128,128]{3,2,1,0:T(8,128)(2,1)} %one.3) | copy-start | bytes 884740
  6.1 9.3 %copy-start.2 = (bf16[3,3,128,128]{3,2,1,0:T(8,128)(2,1)S(1)}, bf16[3,3,128,128]{3,2,1,0:T(8,128)(2,1)}, u32[]{:S(2)}) copy-start(bf16[3,3,128,128]{3,2,1,0:T(8,128)(2,1)} %two.3) | copy-start | bytes 884740
  6.1 9.3 %copy-start.3 = (f32[4,512,128]{2,1,0:T(8,128)S(1)}, f32[4,512,128]{2,1,0:T(8,128)}, u32[]{:S(2)}) copy-start(f32[4,512,128]{2,1,0:T(8,128)} %get-tuple-element.42.state_one) | copy-start | bytes 3145732
  6.1 9.3 %copy-start.8 = (f32[128]{0:T(128)S(1)}, f32[128]{0:T(128)}, u32[]{:S(2)}) copy-start(f32[128]{0:T(128)} %param.20) | copy-start | bytes 1540
  6.3 9.1 %collective-permute-start.1 = (bf16[2,512,128]{2,1,0:T(8,128)(2,1)S(1)}, bf16[2,512,128]{2,1,0:T(8,128)(2,1)S(1)}, u32[]{:S(2)}, u32[]{:S(2)}) collective-permute-start(bf16[2,512,128]{2,1,0:T(8,128)(2,1)S(1)} %get-tuple-element.75), channel_id=1, source_target_pairs={{1,2},{3,4},{5,6},{2,1},{4,3},{6,5},{9,10},{11,12},{13,14},{10,9},... | collective-permute-start | bytes 786440 | tf_op jit(solution)/shard_map/ppermute | solution.py:606
  11.0 4.3 %collective-permute-start = (bf16[2,512,128]{2,1,0:T(8,128)(2,1)S(1)}, bf16[2,512,128]{2,1,0:T(8,128)(2,1)S(1)}, u32[]{:S(2)}, u32[]{:S(2)}) collective-permute-start(bf16[2,512,128]{2,1,0:T(8,128)(2,1)S(1)} %get-tuple-element.76), channel_id=1, source_target_pairs={{0,1},{1,0},{2,3},{3,2},{4,5},{5,4},{6,7},{7,6},{8,9},{9,8},{10,11... | collective-permute-start | bytes 786440 | tf_op jit(solution)/shard_map/ppermute | solution.py:606
  11.1 13.3 %collective-permute-start.5 = (bf16[4,512,128]{2,1,0:T(8,128)(2,1)}, bf16[4,512,128]{2,1,0:T(8,128)(2,1)S(1)}, u32[]{:S(2)}, u32[]{:S(2)}) collective-permute-start(bf16[4,512,128]{2,1,0:T(8,128)(2,1)} %get-tuple-element.44.refs_3_), channel_id=1, source_target_pairs={{0,16},{8,24},{16,0},{24,8},{1,17},{9,25},{17,1},{25,9},{2,18},{10... | collective-permute-start | bytes 1572872 | tf_op jit(solution)/shard_map/ppermute | solution.py:588
  12.4 13.0 %collective-permute-start.4 = (bf16[4,512,128]{2,1,0:T(8,128)(2,1)}, bf16[4,512,128]{2,1,0:T(8,128)(2,1)S(1)}, u32[]{:S(2)}, u32[]{:S(2)}) collective-permute-start(bf16[4,512,128]{2,1,0:T(8,128)(2,1)} %get-tuple-element.44.refs_3_), channel_id=1, source_target_pairs={{0,8},{8,0},{16,24},{24,16},{1,9},{9,1},{17,25},{25,17},{2,10},{10... | collective-permute-start | bytes 1572872 | tf_op jit(solution)/shard_map/ppermute | solution.py:588
  15.4 7.5 %copy-start.12 = (s32[4,2]{0,1:T(2,128)S(1)}, s32[4,2]{0,1:T(2,128)}, u32[]{:S(2)}) copy-start(s32[4,2]{0,1:T(2,128)} %param.13) | copy-start | bytes 100
  15.4 7.6 %copy-start.11 = (bf16[128,128]{1,0:T(8,128)(2,1)S(1)}, bf16[128,128]{1,0:T(8,128)(2,1)}, u32[]{:S(2)}) copy-start(bf16[128,128]{1,0:T(8,128)(2,1)} %param.19) | copy-start | bytes 98308
  15.4 10.0 %copy-start.5 = (bf16[128,128]{1,0:T(8,128)(2,1)S(1)}, bf16[128,128]{1,0:T(8,128)(2,1)}, u32[]{:S(2)}) copy-start(bf16[128,128]{1,0:T(8,128)(2,1)} %refs_4_.1) | copy-start | bytes 98308
  15.4 9.9 %copy-start.6 = (bf16[128,128]{1,0:T(8,128)(2,1)S(1)}, bf16[128,128]{1,0:T(8,128)(2,1)}, u32[]{:S(2)}) copy-start(bf16[128,128]{1,0:T(8,128)(2,1)} %refs_5_.1) | copy-start | bytes 98308
  15.5 9.9 %copy-start.7 = (f32[1,8,512]{2,1,0:T(8,128)S(1)}, f32[1,8,512]{2,1,0:T(8,128)}, u32[]{:S(2)}) copy-start(f32[1,8,512]{2,1,0:T(8,128)} %param.12) | copy-start | bytes 49156
  20.4 15.3 %collective-permute-start.3 = (bf16[4,512,128]{2,1,0:T(8,128)(2,1)}, bf16[4,512,128]{2,1,0:T(8,128)(2,1)S(1)}, u32[]{:S(2)}, u32[]{:S(2)}) collective-permute-start(bf16[4,512,128]{2,1,0:T(8,128)(2,1)} %get-tuple-element.43.refs_2_), channel_id=1, source_target_pairs={{0,16},{8,24},{16,0},{24,8},{1,17},{9,25},{17,1},{25,9},{2,18},{10... | collective-permute-start | bytes 1572872 | tf_op jit(solution)/shard_map/ppermute | solution.py:588
  21.7 15.0 %collective-permute-start.2 = (bf16[4,512,128]{2,1,0:T(8,128)(2,1)}, bf16[4,512,128]{2,1,0:T(8,128)(2,1)S(1)}, u32[]{:S(2)}, u32[]{:S(2)}) collective-permute-start(bf16[4,512,128]{2,1,0:T(8,128)(2,1)} %get-tuple-element.43.refs_2_), channel_id=1, source_target_pairs={{0,8},{8,0},{16,24},{24,16},{1,9},{9,1},{17,25},{25,17},{2,10},{10... | collective-permute-start | bytes 1572872 | tf_op jit(solution)/shard_map/ppermute | solution.py:588
  36.6 14.9 %collective-permute-start.7 = (bf16[4,512,128]{2,1,0:T(8,128)(2,1)S(1)}, bf16[4,512,128]{2,1,0:T(8,128)(2,1)S(1)}, u32[]{:S(2)}, u32[]{:S(2)}) collective-permute-start(bf16[4,512,128]{2,1,0:T(8,128)(2,1)S(1)} %collective-permute-done.5.refs_1_.refs_3_.refs_2_), channel_id=1, source_target_pairs={{0,8},{8,0},{16,24},{24,16},{1,9},{9,1},{17,25},{25,17},{2,10},{10... | collective-permute-start | bytes 1572872 | tf_op jit(solution)/shard_map/ppermute | solution.py:588
  37.8 13.7 %collective-permute-start.6 = (bf16[4,512,128]{2,1,0:T(8,128)(2,1)S(1)}, bf16[4,512,128]{2,1,0:T(8,128)(2,1)S(1)}, u32[]{:S(2)}, u32[]{:S(2)}) collective-permute-start(bf16[4,512,128]{2,1,0:T(8,128)(2,1)S(1)} %collective-permute-done.2.refs_0_), channel_id=1, source_target_pairs={{0,16},{8,24},{16,0},{24,8},{1,17},{9,25},{17,1},{25,9},{2,18},{10... | collective-permute-start | bytes 1572872 | tf_op jit(solution)/shard_map/ppermute | solution.py:588
  38.3 10.2 %collective-permute-start.8 = (bf16[2,512,128]{2,1,0:T(8,128)(2,1)S(1)}, bf16[2,512,128]{2,1,0:T(8,128)(2,1)S(1)}, u32[]{:S(2)}, u32[]{:S(2)}) collective-permute-start(bf16[2,512,128]{2,1,0:T(8,128)(2,1)S(1)} %get-tuple-element.52), channel_id=1, source_target_pairs={{0,1},{1,0},{2,3},{3,2},{4,5},{5,4},{6,7},{7,6},{8,9},{9,8},{10,11... | collective-permute-start | bytes 786440 | tf_op jit(solution)/shard_map/ppermute | solution.py:606
  40.4 12.7 %copy-start.4 = (f32[4,512,128]{2,1,0:T(8,128)S(1)}, f32[4,512,128]{2,1,0:T(8,128)}, u32[]{:S(2)}) copy-start(f32[4,512,128]{2,1,0:T(8,128)} %get-tuple-element.74.refs_9_) | copy-start | bytes 3145732
  40.4 12.7 %copy-start.9 = (f32[128]{0:T(128)S(1)}, f32[128]{0:T(128)}, u32[]{:S(2)}) copy-start(f32[128]{0:T(128)} %param.21) | copy-start | bytes 1540
  40.4 8.1 %collective-permute-start.9 = (bf16[2,512,128]{2,1,0:T(8,128)(2,1)S(1)}, bf16[2,512,128]{2,1,0:T(8,128)(2,1)S(1)}, u32[]{:S(2)}, u32[]{:S(2)}) collective-permute-start(bf16[2,512,128]{2,1,0:T(8,128)(2,1)S(1)} %get-tuple-element.53), channel_id=1, source_target_pairs={{1,2},{3,4},{5,6},{2,1},{4,3},{6,5},{9,10},{11,12},{13,14},{10,9},... | collective-permute-start | bytes 786440 | tf_op jit(solution)/shard_map/ppermute | solution.py:606
  51.5 8.3 %collective-permute-start.11 = (bf16[1,512,128]{2,1,0:T(8,128)(2,1)S(1)}, bf16[1,512,128]{2,1,0:T(8,128)(2,1)S(1)}, u32[]{:S(2)}, u32[]{:S(2)}) collective-permute-start(bf16[1,512,128]{2,1,0:T(8,128)(2,1)S(1)} %get-tuple-element.66), channel_id=1, source_target_pairs={{0,16},{8,24},{16,0},{24,8},{1,17},{9,25},{17,1},{25,9},{2,18},{10... | collective-permute-start | bytes 393224 | tf_op jit(solution)/shard_map/ppermute | solution.py:588
  52.9 7.0 %collective-permute-start.10 = (bf16[1,512,128]{2,1,0:T(8,128)(2,1)S(1)}, bf16[1,512,128]{2,1,0:T(8,128)(2,1)S(1)}, u32[]{:S(2)}, u32[]{:S(2)}) collective-permute-start(bf16[1,512,128]{2,1,0:T(8,128)(2,1)S(1)} %get-tuple-element.64.refs_2_), channel_id=1, source_target_pairs={{0,8},{8,0},{16,24},{24,16},{1,9},{9,1},{17,25},{25,17},{2,10},{10... | collective-permute-start | bytes 393224 | tf_op jit(solution)/shard_map/ppermute | solution.py:588

commit v6 on v5

--- a/solution.py
+++ b/solution.py
@@ -75,9 +75,13 @@
 
 def row_pair(pad, first, weights):
     columns = pad.shape[1] - 16
-    lhs = [pad[first + j, 7 + b : 7 + b + columns] for j in range(4) for b in range(3)]
-    lhs = jnp.concatenate(lhs, axis=-1).astype(jnp.bfloat16)
-    return jnp.dot(lhs, weights[...], preferred_element_type=jnp.float32)
+    block = 128 if columns % 128 == 0 else columns
+    outs = []
+    for start in range(7, 7 + columns, block):
+        lhs = [pad[first + j, start + b : start + b + block] for j in range(4) for b in range(3)]
+        lhs = jnp.concatenate(lhs, axis=-1).astype(jnp.bfloat16)
+        outs.append(jnp.dot(lhs, weights[...], preferred_element_type=jnp.float32))
+    return jnp.concatenate(outs, axis=0)
 
 
 def ask(norm, query_weight, key_weight, tempers, query_edge, query_middle):
@@ -97,19 +101,17 @@
 
 
 def middle_body(
-    cells, one, two, gain, state_one_out, state_out, norm_out,
-    held, one_held, two_held, gain_held, w1, w2, state_one, state_two, norm, x1, x2, sems,
+    cells, one, two, gain, mate_out, cross_out, state_one_out, state_out, norm_out,
+    held, one_held, two_held, gain_held, mate, cross, w1, w2, state_one, state_two, norm, x1, x2,
+    sems,
 ):
     rows = cells.shape[0]
     channels = cells.shape[2]
     copies = Copies(sems)
+    kernels = [copies.start(one, one_held), copies.start(two, two_held)]
     loads = [copies.start(cells.at[r], held.at[r]) for r in range(4)]
-    later = [copies.start(one, one_held)]
-    later += [copies.start(cells.at[r], held.at[r]) for r in range(4, rows)]
-    later += [
-        copies.start(two, two_held),
-        copies.start(gain, gain_held),
-    ]
+    later = [copies.start(cells.at[r], held.at[r]) for r in range(4, rows)]
+    later.append(copies.start(gain, gain_held))
     clear(x1)
     clear(x2)
 
@@ -129,14 +131,21 @@
             state_two[slot] = state
             norm[slot] = scaled(state, gain_held[...]).astype(jnp.bfloat16)
 
+    for load in kernels:
+        load.wait()
+    pack(one_held, w1)
+    pack(two_held, w2)
     for load in loads:
         load.wait()
     for r in range(4):
         place(silu(held[r]), x1, r)
     for load in later:
         load.wait()
-    pack(one_held, w1)
-    pack(two_held, w2)
+    odd = band_place()[2]
+    for r in range(2):
+        head, tail = held[r].astype(jnp.bfloat16), held[rows - 2 + r].astype(jnp.bfloat16)
+        mate[r] = jnp.where(odd, head, tail)
+        cross[r] = jnp.where(odd, tail, head)
     for first in range(0, rows - 2, 2):
         convolve_one(first)
         for r in range(first + 4, min(first + 6, rows)):
@@ -144,6 +153,8 @@
         if 2 <= first < rows - 4:
             convolve_two(first - 2)
     stores = [
+        copies.start(mate, mate_out),
+        copies.start(cross, cross_out),
         copies.start(state_one.at[pl.ds(0, 2)], state_one_out.at[pl.ds(0, 2)]),
         copies.start(state_one.at[pl.ds(rows - 4, 2)], state_one_out.at[pl.ds(2, 2)]),
         copies.start(norm.at[pl.ds(0, rows - 6)], norm_out.at[pl.ds(0, rows - 6)]),
@@ -172,8 +183,10 @@
     return pl.pallas_call(
         middle_body,
         in_specs=[anywhere] * 4,
-        out_specs=[anywhere] * 3,
+        out_specs=[anywhere] * 5,
         out_shape=[
+            jax.ShapeDtypeStruct((2, *row), jnp.bfloat16),
+            jax.ShapeDtypeStruct((2, *row), jnp.bfloat16),
             jax.ShapeDtypeStruct((4, *row), jnp.float32),
             jax.ShapeDtypeStruct((rows - 4, *row), jnp.float32),
             jax.ShapeDtypeStruct((rows - 4, *row), jnp.bfloat16),
@@ -181,6 +194,8 @@
         scratch_shapes=[
             *scratch(*[(a.shape, a.dtype) for a in operands]),
             *scratch(
+                ((2, *row), jnp.bfloat16),
+                ((2, *row), jnp.bfloat16),
                 packed,
                 packed,
                 ((rows - 2, *row), jnp.float32),
@@ -189,7 +204,7 @@
                 ((rows, *padded), jnp.float32),
                 ((rows - 2, *padded), jnp.float32),
             ),
-            pltpu.SemaphoreType.DMA((rows + 9,)),
+            pltpu.SemaphoreType.DMA((rows + 11,)),
         ],
         compiler_params=pltpu.CompilerParams(vmem_limit_bytes=whole_vmem_bytes),
         cost_estimate=no_cost,
@@ -614,12 +629,9 @@
     bands = lax.axis_size("band")
     cells, temper, gain = features[0], tempers[0], norm_gain[None]
 
-    state_one, state_middle, middle = middle_rows(cells, conv_one, conv_two, gain)
+    mate, cross, state_one, state_middle, middle = middle_rows(cells, conv_one, conv_two, gain)
     middles = gather_direct(middle, views)
-    halo_cells, middle = lax.optimization_barrier((cells, middle))
-    head, tail = halo_cells[:2].astype(jnp.bfloat16), halo_cells[-2:].astype(jnp.bfloat16)
-    odd = band_place()[2]
-    mate, cross = swap_bands(jnp.where(odd, head, tail), jnp.where(odd, tail, head), bands)
+    mate, cross = swap_bands(mate, cross, bands)
     state_edge, edge = edge_rows(cells, mate, cross, conv_one, conv_two, state_one, gain)
     edges = gather_direct(edge, views)
 

time: 64.3 us -> 63.6 us (0.989)
  waiting for transfers between devices: 11.2 us -> 7.99 us
  local copies, waits for them, and re-layouts: 0.16 us -> 2.39 us
  starting transfers between devices: 18.5 us -> 19.6 us
    ppermute x8, waiting for transfers between devices: 9.43 us -> 5.96 us  [swap(): return lax.ppermute(cells, 'view', [(i, i ^ offset) for i in range(views)])]
    ppermute x2, starting transfers between devices: 8.16 us -> 10.9 us  [swap_bands(): lax.ppermute(cross, 'band', crosses)]
    unnamed x27, local copies, waits for them, and re-layouts: 0.16 us -> 2.39 us
    ppermute x2, starting transfers between devices: 2.19 us -> 0.19 us  [swap_bands(): lax.ppermute(mate, 'band', mates)]
  transfers between devices with their start and end apart: 12 -> 12, of which waited for: 5 -> 4; matrix products, arithmetic and copies ran while one was open for 0% -> 0% of each run, Pallas kernels for 37% -> 37%
where the time goes in v6:
time: 63.6 us; the launch traced here: 63.3 us
  Pallas kernels  32.8 us (52%)
  starting transfers between devices  19.6 us (31%)
  waiting for transfers between devices  7.99 us (13%)
  local copies, waits for them, and re-layouts  2.39 us (4%)
    ppermute x2, starting transfers between devices, swap_bands(): lax.ppermute(cross, 'band', crosses)  10.9 us
    ppermute x8, starting transfers between devices, swap(): return lax.ppermute(cells, 'view', [(i, i ^ offset) for i in range(views)])  8.56 us
    pallas_call x1, Pallas kernels, attend_far(): pl.pallas_call(functools.partial(attend_far_body, low, len(candidates[0])...  6.75 us
    ppermute x8, waiting for transfers between devices, swap(): return lax.ppermute(cells, 'view', [(i, i ^ offset) for i in range(views)])  5.96 us
    pallas_call x1, Pallas kernels, middle_rows(): pl.pallas_call(middle_body, in_specs=[anywhere] * 4, out_specs=[anywhere]...  5.75 us
    pallas_call x1, Pallas kernels, edge_rows(): pl.pallas_call(edge_body, in_specs=[anywhere] + [in_vmem] * 2 + [anywhere...  4.71 us
    pallas_call x1, Pallas kernels, attend_near(): pl.pallas_call(functools.partial(attend_near_body, low, len(candidates[0]...  4.64 us
    pallas_call x1, Pallas kernels, attend_outer(): pl.pallas_call(functools.partial(attend_outer_body, low, len(sides[0])),...  3.92 us
  transfers between devices with their start and end apart: 12, of which 4 were waited for; matrix products, arithmetic and copies ran while one was open for 0% of the time, Pallas kernels for 37%

profile of v6, /device:TPU:1, one launch (start us, length us, event | category | flops | bytes accessed | tf_op | source)
XLA Modules:
  0.0 63.3 jit_solution(10763717792086014119)
XLA Ops:
  0.0 0.0 copy-start
  0.0 0.0 copy-start.9
  0.0 5.7 %residual_middle.1 = (bf16[2,512,128]{2,1,0:T(8,128)(2,1)}, bf16[2,512,128]{2,1,0:T(8,128)(2,1)}, f32[4,512,128]{2,1,0:T(8,128)}, f32[4,512,128]{2,1,0:T(8,128)}, bf16[4,512,128]{2,1,0:T(8,128)(2,1)}) custom-call(f32[8,512,128]{2,1,0:T(8,128)} %bitcast.12, bf16[3,3,128,128]{3,2,1,0:T(8,128)(2,1)} %one.3, bf16[3,3,128,128]{3,2,1,0:T(8,128)(2,1)} %two.3, ...), custom_call_target="tpu_custom_call" | custom-call | tf_op jit(solution)/shard_map/residual_middle/pallas_call | solution.py:183
  5.8 0.1 collective-permute-start
  5.9 4.6 %collective-permute-start.1 = (bf16[2,512,128]{2,1,0:T(8,128)(2,1)}, bf16[2,512,128]{2,1,0:T(8,128)(2,1)S(1)}, u32[]{:S(2)}, u32[]{:S(2)}) collective-permute-start(bf16[2,512,128]{2,1,0:T(8,128)(2,1)} %get-tuple-element.41), channel_id=1, source_target_pairs={{1,2},{3,4},{5,6},{2,1},{4,3},{6,5},{9,10},{11,12},{13,14},{10,9},... | collective-permute-start | bytes 786440 | tf_op jit(solution)/shard_map/ppermute | solution.py:621
  10.5 1.3 %collective-permute-start.5 = (bf16[4,512,128]{2,1,0:T(8,128)(2,1)}, bf16[4,512,128]{2,1,0:T(8,128)(2,1)S(1)}, u32[]{:S(2)}, u32[]{:S(2)}) collective-permute-start(bf16[4,512,128]{2,1,0:T(8,128)(2,1)} %get-tuple-element.44.refs_3_), channel_id=1, source_target_pairs={{0,16},{8,24},{16,0},{24,8},{1,17},{9,25},{17,1},{25,9},{2,18},{10... | collective-permute-start | bytes 1572872 | tf_op jit(solution)/shard_map/ppermute | solution.py:603
  11.8 1.2 %collective-permute-start.4 = (bf16[4,512,128]{2,1,0:T(8,128)(2,1)}, bf16[4,512,128]{2,1,0:T(8,128)(2,1)S(1)}, u32[]{:S(2)}, u32[]{:S(2)}) collective-permute-start(bf16[4,512,128]{2,1,0:T(8,128)(2,1)} %get-tuple-element.44.refs_3_), channel_id=1, source_target_pairs={{0,8},{8,0},{16,24},{24,16},{1,9},{9,1},{17,25},{25,17},{2,10},{10... | collective-permute-start | bytes 1572872 | tf_op jit(solution)/shard_map/ppermute | solution.py:603
  13.0 0.0 collective-permute-done.mate
  13.0 2.0 %collective-permute-done.1.cross = bf16[2,512,128]{2,1,0:T(8,128)(2,1)S(1)} collective-permute-done((bf16[2,512,128]{2,1,0:T(8,128)(2,1)}, bf16[2,512,128]{2,1,0:T(8,128)(2,1)S(1)}, u32[]{:S(2)}, u32[]{:S(2)}) %collective-permute-start.1) | collective-permute-done | bytes 262176 | tf_op jit(solution)/shard_map/ppermute | solution.py:621
  15.0 0.0 copy-done.2
  15.0 0.0 copy-done.1
  15.0 0.0 copy-done.9
  15.0 0.0 copy-start.3
  15.0 1.2 %copy-done.3 = f32[4,512,128]{2,1,0:T(8,128)S(1)} copy-done((f32[4,512,128]{2,1,0:T(8,128)S(1)}, f32[4,512,128]{2,1,0:T(8,128)}, u32[]{:S(2)}) %copy-start.3) | copy-done | bytes 1048600
  16.3 0.0 copy-start.8
  16.3 4.7 %residual_edge.1 = (f32[4,512,128]{2,1,0:T(8,128)S(1)}, bf16[4,512,128]{2,1,0:T(8,128)(2,1)}) custom-call(f32[8,512,128]{2,1,0:T(8,128)} %bitcast.13, bf16[2,512,128]{2,1,0:T(8,128)(2,1)S(1)} %collective-permute-done.mate, bf16[2,512,128]{2,1,0:T(8,128)(2,1)S(1)} %collective-permute-done.1.cross, bf16[3,3,128,128]{3,2,1,0:T(8,128)(2,1)S(1)} %copy-done.1, ...), custom_call_target="tpu_custom_call" | custom-call | tf_op jit(solution)/shard_map/residual_edge/pallas_call | solution.py:284
  21.0 1.8 %collective-permute-start.3 = (bf16[4,512,128]{2,1,0:T(8,128)(2,1)}, bf16[4,512,128]{2,1,0:T(8,128)(2,1)S(1)}, u32[]{:S(2)}, u32[]{:S(2)}) collective-permute-start(bf16[4,512,128]{2,1,0:T(8,128)(2,1)} %get-tuple-element.43.refs_2_), channel_id=1, source_target_pairs={{0,16},{8,24},{16,0},{24,8},{1,17},{9,25},{17,1},{25,9},{2,18},{10... | collective-permute-start | bytes 1572872 | tf_op jit(solution)/shard_map/ppermute | solution.py:603
  22.8 1.2 %collective-permute-start.2 = (bf16[4,512,128]{2,1,0:T(8,128)(2,1)}, bf16[4,512,128]{2,1,0:T(8,128)(2,1)S(1)}, u32[]{:S(2)}, u32[]{:S(2)}) collective-permute-start(bf16[4,512,128]{2,1,0:T(8,128)(2,1)} %get-tuple-element.43.refs_2_), channel_id=1, source_target_pairs={{0,8},{8,0},{16,24},{24,16},{1,9},{9,1},{17,25},{25,17},{2,10},{10... | collective-permute-start | bytes 1572872 | tf_op jit(solution)/shard_map/ppermute | solution.py:603
  24.0 0.0 copy-done.12
  24.0 0.1 copy.16.partners
  24.1 0.0 copy-done
  24.1 0.1 convolution_convert_fusion.refs_10_.refs_9_
  24.3 0.0 collective-permute-done.5.refs_1_.refs_3_.refs_2_
  24.3 1.7 %collective-permute-done.4.refs_0_.refs_2_ = bf16[4,512,128]{2,1,0:T(8,128)(2,1)S(1)} collective-permute-done((bf16[4,512,128]{2,1,0:T(8,128)(2,1)}, bf16[4,512,128]{2,1,0:T(8,128)(2,1)S(1)}, u32[]{:S(2)}, u32[]{:S(2)}) %collective-permute-start.4) | collective-permute-done | bytes 524320 | tf_op jit(solution)/shard_map/ppermute | solution.py:603
  26.0 0.0 copy-done.7
  26.0 1.0 %copy-done.5 = bf16[4,512,128]{2,1,0:T(8,128)(2,1)S(1)} copy-done((bf16[4,512,128]{2,1,0:T(8,128)(2,1)S(1)}, bf16[4,512,128]{2,1,0:T(8,128)(2,1)}, u32[]{:S(2)}) %copy-start.5) | copy-done | bytes 524312
  27.0 3.9 %attend_first.1 = (bf16[4,512,128]{2,1,0:T(8,128)(2,1)S(1)}, bf16[4,512,128]{2,1,0:T(8,128)(2,1)S(1)}, bf16[2,512,128]{2,1,0:T(8,128)(2,1)S(1)}) custom-call(s32[4,2]{1,0:T(4,128)S(1)} %copy.16.partners, bf16[4,512,128]{2,1,0:T(8,128)(2,1)S(1)} %collective-permute-done.4.refs_0_.refs_2_, ...), custom_call_target="tpu_custom_call" | custom-call | tf_op jit(solution)/shard_map/attend_first/pallas_call | solution.py:491
  31.0 2.5 %collective-permute-done.3.refs_1_.refs_0_ = bf16[4,512,128]{2,1,0:T(8,128)(2,1)S(1)} collective-permute-done((bf16[4,512,128]{2,1,0:T(8,128)(2,1)}, bf16[4,512,128]{2,1,0:T(8,128)(2,1)S(1)}, u32[]{:S(2)}, u32[]{:S(2)}) %collective-permute-start.3) | collective-permute-done | bytes 524320 | tf_op jit(solution)/shard_map/ppermute | solution.py:603
  33.5 1.7 %collective-permute-done.2.refs_0_ = bf16[4,512,128]{2,1,0:T(8,128)(2,1)S(1)} collective-permute-done((bf16[4,512,128]{2,1,0:T(8,128)(2,1)}, bf16[4,512,128]{2,1,0:T(8,128)(2,1)S(1)}, u32[]{:S(2)}, u32[]{:S(2)}) %collective-permute-start.2) | collective-permute-done | bytes 524320 | tf_op jit(solution)/shard_map/ppermute | solution.py:603
  35.2 1.2 %collective-permute-start.7 = (bf16[4,512,128]{2,1,0:T(8,128)(2,1)S(1)}, bf16[4,512,128]{2,1,0:T(8,128)(2,1)S(1)}, u32[]{:S(2)}, u32[]{:S(2)}) collective-permute-start(bf16[4,512,128]{2,1,0:T(8,128)(2,1)S(1)} %collective-permute-done.5.refs_1_.refs_3_.refs_2_), channel_id=1, source_target_pairs={{0,8},{8,0},{16,24},{24,16},{1,9},{9,1},{17,25},{25,17},{2,10},{10... | collective-permute-start | bytes 1572872 | tf_op jit(solution)/shard_map/ppermute | solution.py:603
  36.4 0.2 collective-permute-start.6
  36.6 0.1 edge_halos.1
  36.7 0.1 collective-permute-start.8
  36.8 0.0 copy-start.10
  36.8 6.3 %collective-permute-start.9 = (bf16[2,512,128]{2,1,0:T(8,128)(2,1)S(1)}, bf16[2,512,128]{2,1,0:T(8,128)(2,1)S(1)}, u32[]{:S(2)}, u32[]{:S(2)}) collective-permute-start(bf16[2,512,128]{2,1,0:T(8,128)(2,1)S(1)} %get-tuple-element.53), channel_id=1, source_target_pairs={{1,2},{3,4},{5,6},{2,1},{4,3},{6,5},{9,10},{11,12},{13,14},{10,9},... | collective-permute-start | bytes 786440 | tf_op jit(solution)/shard_map/ppermute | solution.py:621
  43.2 4.6 %attend_near.1.refs_6_ = bf16[4,512,128]{2,1,0:T(8,128)(2,1)S(1)} custom-call(s32[4,2]{1,0:T(4,128)S(1)} %copy.16.partners, bf16[4,512,128]{2,1,0:T(8,128)(2,1)S(1)} %collective-permute-done.2.refs_0_, bf16[4,512,128]{2,1,0:T(8,128)(2,1)S(1)} %collective-permute-done.3.refs_1_.refs_0_, bf16[4,512,128]{2,1,0:T(8,128)(2,1)S(1)} %collective-permute-done.4.refs_0_.refs_2_, ...), custom_call_target="tpu_custom_call" | custom-call | tf_op jit(solution)/shard_map/attend_near/pallas_call | solution.py:511
  47.8 0.0 collective-permute-done.8.refs_2_
  47.8 0.0 collective-permute-done.9.refs_3_
  47.8 3.0 %attend_ends.1 = (bf16[2,512,128]{2,1,0:T(8,128)(2,1)S(1)}, bf16[1,512,128]{2,1,0:T(8,128)(2,1)}, bf16[1,512,128]{2,1,0:T(8,128)(2,1)S(1)}, bf16[1,512,128]{2,1,0:T(8,128)(2,1)S(1)}, bf16[1,512,128]{2,1,0:T(8,128)(2,1)S(1)}) custom-call(s32[4,2]{1,0:T(4,128)S(1)} %copy.16.partners, bf16[4,512,128]{2,1,0:T(8,128)(2,1)S(1)} %collective-permute-done.2.refs_0_, ...), custom_call_target="tpu_custom_call" | custom-call | tf_op jit(solution)/shard_map/attend_ends/pallas_call | solution.py:547
  50.9 0.0 collective-permute-done.7.refs_3_
  50.9 0.0 collective-permute-done.6.refs_1_
  50.9 1.3 %collective-permute-start.11 = (bf16[1,512,128]{2,1,0:T(8,128)(2,1)S(1)}, bf16[1,512,128]{2,1,0:T(8,128)(2,1)S(1)}, u32[]{:S(2)}, u32[]{:S(2)}) collective-permute-start(bf16[1,512,128]{2,1,0:T(8,128)(2,1)S(1)} %get-tuple-element.66), channel_id=1, source_target_pairs={{0,16},{8,24},{16,0},{24,8},{1,17},{9,25},{17,1},{25,9},{2,18},{10... | collective-permute-start | bytes 393224 | tf_op jit(solution)/shard_map/ppermute | solution.py:603
  52.2 0.3 collective-permute-start.10
  52.4 0.0 copy-done.10
  52.4 6.8 %attend_far.1.refs_11_ = f32[6,512,128]{2,1,0:T(8,128)S(1)} custom-call(s32[4,2]{1,0:T(4,128)S(1)} %copy.16.partners, bf16[4,512,128]{2,1,0:T(8,128)(2,1)S(1)} %collective-permute-done.3.refs_1_.refs_0_, bf16[4,512,128]{2,1,0:T(8,128)(2,1)S(1)} %collective-permute-done.6.refs_1_, bf16[4,512,128]{2,1,0:T(8,128)(2,1)S(1)} %collective-permute-done.5.refs_1_.refs_3_.refs_2_, ...), custom_call_target="tpu_custom_call" | custom-call | tf_op jit(solution)/shard_map/attend_far/pallas_call | solution.py:528
  59.2 0.0 collective-permute-done.11.refs_5_
  59.2 0.0 collective-permute-done.10.refs_3_
  59.2 3.9 %attend_outer.1 = f32[8,512,128]{2,1,0:T(8,128)} custom-call(s32[4,2]{1,0:T(4,128)S(1)} %copy.16.partners, bf16[4,512,128]{2,1,0:T(8,128)(2,1)S(1)} %collective-permute-done.3.refs_1_.refs_0_, bf16[4,512,128]{2,1,0:T(8,128)(2,1)S(1)} %collective-permute-done.6.refs_1_, bf16[1,512,128]{2,1,0:T(8,128)(2,1)S(1)} %get-tuple-element.64.refs_2_, ...), custom_call_target="tpu_custom_call" | custom-call | tf_op jit(solution)/shard_map/attend_outer/pallas_call | solution.py:564
  (12 shorter events, 0.0 us)
Async XLA Ops:
  0.0 24.1 %copy-start = (bf16[128,128]{1,0:T(8,128)(2,1)S(1)}, bf16[128,128]{1,0:T(8,128)(2,1)}, u32[]{:S(2)}) copy-start(bf16[128,128]{1,0:T(8,128)(2,1)} %param.18) | copy-start | bytes 98308
  0.0 15.0 %copy-start.2 = (bf16[3,3,128,128]{3,2,1,0:T(8,128)(2,1)S(1)}, bf16[3,3,128,128]{3,2,1,0:T(8,128)(2,1)}, u32[]{:S(2)}) copy-start(bf16[3,3,128,128]{3,2,1,0:T(8,128)(2,1)} %two.3) | copy-start | bytes 884740
  0.0 15.0 %copy-start.1 = (bf16[3,3,128,128]{3,2,1,0:T(8,128)(2,1)S(1)}, bf16[3,3,128,128]{3,2,1,0:T(8,128)(2,1)}, u32[]{:S(2)}) copy-start(bf16[3,3,128,128]{3,2,1,0:T(8,128)(2,1)} %one.3) | copy-start | bytes 884740
  0.0 15.0 %copy-start.9 = (f32[128]{0:T(128)S(1)}, f32[128]{0:T(128)}, u32[]{:S(2)}) copy-start(f32[128]{0:T(128)} %param.20) | copy-start | bytes 1540
  5.8 7.2 %collective-permute-start = (bf16[2,512,128]{2,1,0:T(8,128)(2,1)}, bf16[2,512,128]{2,1,0:T(8,128)(2,1)S(1)}, u32[]{:S(2)}, u32[]{:S(2)}) collective-permute-start(bf16[2,512,128]{2,1,0:T(8,128)(2,1)} %get-tuple-element.40), channel_id=1, source_target_pairs={{0,1},{1,0},{2,3},{3,2},{4,5},{5,4},{6,7},{7,6},{8,9},{9,8},{10,11... | collective-permute-start | bytes 786440 | tf_op jit(solution)/shard_map/ppermute | solution.py:621
  5.9 9.1 %collective-permute-start.1 = (bf16[2,512,128]{2,1,0:T(8,128)(2,1)}, bf16[2,512,128]{2,1,0:T(8,128)(2,1)S(1)}, u32[]{:S(2)}, u32[]{:S(2)}) collective-permute-start(bf16[2,512,128]{2,1,0:T(8,128)(2,1)} %get-tuple-element.41), channel_id=1, source_target_pairs={{1,2},{3,4},{5,6},{2,1},{4,3},{6,5},{9,10},{11,12},{13,14},{10,9},... | collective-permute-start | bytes 786440 | tf_op jit(solution)/shard_map/ppermute | solution.py:621
  10.5 13.8 %collective-permute-start.5 = (bf16[4,512,128]{2,1,0:T(8,128)(2,1)}, bf16[4,512,128]{2,1,0:T(8,128)(2,1)S(1)}, u32[]{:S(2)}, u32[]{:S(2)}) collective-permute-start(bf16[4,512,128]{2,1,0:T(8,128)(2,1)} %get-tuple-element.44.refs_3_), channel_id=1, source_target_pairs={{0,16},{8,24},{16,0},{24,8},{1,17},{9,25},{17,1},{25,9},{2,18},{10... | collective-permute-start | bytes 1572872 | tf_op jit(solution)/shard_map/ppermute | solution.py:603
  11.8 14.2 %collective-permute-start.4 = (bf16[4,512,128]{2,1,0:T(8,128)(2,1)}, bf16[4,512,128]{2,1,0:T(8,128)(2,1)S(1)}, u32[]{:S(2)}, u32[]{:S(2)}) collective-permute-start(bf16[4,512,128]{2,1,0:T(8,128)(2,1)} %get-tuple-element.44.refs_3_), channel_id=1, source_target_pairs={{0,8},{8,0},{16,24},{24,16},{1,9},{9,1},{17,25},{25,17},{2,10},{10... | collective-permute-start | bytes 1572872 | tf_op jit(solution)/shard_map/ppermute | solution.py:603
  15.0 1.2 %copy-start.3 = (f32[4,512,128]{2,1,0:T(8,128)S(1)}, f32[4,512,128]{2,1,0:T(8,128)}, u32[]{:S(2)}) copy-start(f32[4,512,128]{2,1,0:T(8,128)} %get-tuple-element.42.state_one) | copy-start | bytes 3145732
  16.2 7.8 %copy-start.12 = (s32[4,2]{0,1:T(2,128)S(1)}, s32[4,2]{0,1:T(2,128)}, u32[]{:S(2)}) copy-start(s32[4,2]{0,1:T(2,128)} %param.13) | copy-start | bytes 100
  16.2 7.9 %copy-start.11 = (bf16[128,128]{1,0:T(8,128)(2,1)S(1)}, bf16[128,128]{1,0:T(8,128)(2,1)}, u32[]{:S(2)}) copy-start(bf16[128,128]{1,0:T(8,128)(2,1)} %param.19) | copy-start | bytes 98308
  16.2 9.7 %copy-start.6 = (bf16[128,128]{1,0:T(8,128)(2,1)S(1)}, bf16[128,128]{1,0:T(8,128)(2,1)}, u32[]{:S(2)}) copy-start(bf16[128,128]{1,0:T(8,128)(2,1)} %refs_4_.1) | copy-start | bytes 98308
  16.2 9.7 %copy-start.7 = (bf16[128,128]{1,0:T(8,128)(2,1)S(1)}, bf16[128,128]{1,0:T(8,128)(2,1)}, u32[]{:S(2)}) copy-start(bf16[128,128]{1,0:T(8,128)(2,1)} %refs_5_.1) | copy-start | bytes 98308
  16.3 9.7 %copy-start.8 = (f32[1,8,512]{2,1,0:T(8,128)S(1)}, f32[1,8,512]{2,1,0:T(8,128)}, u32[]{:S(2)}) copy-start(f32[1,8,512]{2,1,0:T(8,128)} %param.12) | copy-start | bytes 49156
  21.0 12.5 %collective-permute-start.3 = (bf16[4,512,128]{2,1,0:T(8,128)(2,1)}, bf16[4,512,128]{2,1,0:T(8,128)(2,1)S(1)}, u32[]{:S(2)}, u32[]{:S(2)}) collective-permute-start(bf16[4,512,128]{2,1,0:T(8,128)(2,1)} %get-tuple-element.43.refs_2_), channel_id=1, source_target_pairs={{0,16},{8,24},{16,0},{24,8},{1,17},{9,25},{17,1},{25,9},{2,18},{10... | collective-permute-start | bytes 1572872 | tf_op jit(solution)/shard_map/ppermute | solution.py:603
  22.8 12.4 %collective-permute-start.2 = (bf16[4,512,128]{2,1,0:T(8,128)(2,1)}, bf16[4,512,128]{2,1,0:T(8,128)(2,1)S(1)}, u32[]{:S(2)}, u32[]{:S(2)}) collective-permute-start(bf16[4,512,128]{2,1,0:T(8,128)(2,1)} %get-tuple-element.43.refs_2_), channel_id=1, source_target_pairs={{0,8},{8,0},{16,24},{24,16},{1,9},{9,1},{17,25},{25,17},{2,10},{10... | collective-permute-start | bytes 1572872 | tf_op jit(solution)/shard_map/ppermute | solution.py:603
  26.0 1.0 %copy-start.5 = (bf16[4,512,128]{2,1,0:T(8,128)(2,1)S(1)}, bf16[4,512,128]{2,1,0:T(8,128)(2,1)}, u32[]{:S(2)}) copy-start(bf16[4,512,128]{2,1,0:T(8,128)(2,1)} %get-tuple-element.44.refs_3_) | copy-start | bytes 1572868
  35.2 15.7 %collective-permute-start.7 = (bf16[4,512,128]{2,1,0:T(8,128)(2,1)S(1)}, bf16[4,512,128]{2,1,0:T(8,128)(2,1)S(1)}, u32[]{:S(2)}, u32[]{:S(2)}) collective-permute-start(bf16[4,512,128]{2,1,0:T(8,128)(2,1)S(1)} %collective-permute-done.5.refs_1_.refs_3_.refs_2_), channel_id=1, source_target_pairs={{0,8},{8,0},{16,24},{24,16},{1,9},{9,1},{17,25},{25,17},{2,10},{10... | collective-permute-start | bytes 1572872 | tf_op jit(solution)/shard_map/ppermute | solution.py:603
  36.4 14.5 %collective-permute-start.6 = (bf16[4,512,128]{2,1,0:T(8,128)(2,1)S(1)}, bf16[4,512,128]{2,1,0:T(8,128)(2,1)S(1)}, u32[]{:S(2)}, u32[]{:S(2)}) collective-permute-start(bf16[4,512,128]{2,1,0:T(8,128)(2,1)S(1)} %collective-permute-done.2.refs_0_), channel_id=1, source_target_pairs={{0,16},{8,24},{16,0},{24,8},{1,17},{9,25},{17,1},{25,9},{2,18},{10... | collective-permute-start | bytes 1572872 | tf_op jit(solution)/shard_map/ppermute | solution.py:603
  36.7 11.1 %collective-permute-start.8 = (bf16[2,512,128]{2,1,0:T(8,128)(2,1)S(1)}, bf16[2,512,128]{2,1,0:T(8,128)(2,1)S(1)}, u32[]{:S(2)}, u32[]{:S(2)}) collective-permute-start(bf16[2,512,128]{2,1,0:T(8,128)(2,1)S(1)} %get-tuple-element.52), channel_id=1, source_target_pairs={{0,1},{1,0},{2,3},{3,2},{4,5},{5,4},{6,7},{7,6},{8,9},{9,8},{10,11... | collective-permute-start | bytes 786440 | tf_op jit(solution)/shard_map/ppermute | solution.py:621
  36.8 15.6 %copy-start.4 = (f32[4,512,128]{2,1,0:T(8,128)S(1)}, f32[4,512,128]{2,1,0:T(8,128)}, u32[]{:S(2)}) copy-start(f32[4,512,128]{2,1,0:T(8,128)} %get-tuple-element.74.refs_9_) | copy-start | bytes 3145732
  36.8 15.6 %copy-start.10 = (f32[128]{0:T(128)S(1)}, f32[128]{0:T(128)}, u32[]{:S(2)}) copy-start(f32[128]{0:T(128)} %param.21) | copy-start | bytes 1540
  36.8 11.0 %collective-permute-start.9 = (bf16[2,512,128]{2,1,0:T(8,128)(2,1)S(1)}, bf16[2,512,128]{2,1,0:T(8,128)(2,1)S(1)}, u32[]{:S(2)}, u32[]{:S(2)}) collective-permute-start(bf16[2,512,128]{2,1,0:T(8,128)(2,1)S(1)} %get-tuple-element.53), channel_id=1, source_target_pairs={{1,2},{3,4},{5,6},{2,1},{4,3},{6,5},{9,10},{11,12},{13,14},{10,9},... | collective-permute-start | bytes 786440 | tf_op jit(solution)/shard_map/ppermute | solution.py:621
  50.9 8.3 %collective-permute-start.11 = (bf16[1,512,128]{2,1,0:T(8,128)(2,1)S(1)}, bf16[1,512,128]{2,1,0:T(8,128)(2,1)S(1)}, u32[]{:S(2)}, u32[]{:S(2)}) collective-permute-start(bf16[1,512,128]{2,1,0:T(8,128)(2,1)S(1)} %get-tuple-element.66), channel_id=1, source_target_pairs={{0,16},{8,24},{16,0},{24,8},{1,17},{9,25},{17,1},{25,9},{2,18},{10... | collective-permute-start | bytes 393224 | tf_op jit(solution)/shard_map/ppermute | solution.py:603
  52.2 7.0 %collective-permute-start.10 = (bf16[1,512,128]{2,1,0:T(8,128)(2,1)S(1)}, bf16[1,512,128]{2,1,0:T(8,128)(2,1)S(1)}, u32[]{:S(2)}, u32[]{:S(2)}) collective-permute-start(bf16[1,512,128]{2,1,0:T(8,128)(2,1)S(1)} %get-tuple-element.64.refs_2_), channel_id=1, source_target_pairs={{0,8},{8,0},{16,24},{24,16},{1,9},{9,1},{17,25},{25,17},{2,10},{10... | collective-permute-start | bytes 393224 | tf_op jit(solution)/shard_map/ppermute | solution.py:603

commit v7 on v6

--- a/solution.py
+++ b/solution.py
@@ -150,15 +150,17 @@
         convolve_one(first)
         for r in range(first + 4, min(first + 6, rows)):
             place(silu(held[r]), x1, r)
-        if 2 <= first < rows - 4:
-            convolve_two(first - 2)
-    stores = [
+    early = [
         copies.start(mate, mate_out),
         copies.start(cross, cross_out),
         copies.start(state_one.at[pl.ds(0, 2)], state_one_out.at[pl.ds(0, 2)]),
         copies.start(state_one.at[pl.ds(rows - 4, 2)], state_one_out.at[pl.ds(2, 2)]),
+    ]
+    for first in range(0, rows - 6, 2):
+        convolve_two(first)
+    stores = early + [
+        copies.start(state_two.at[pl.ds(0, rows - 6)], state_out.at[pl.ds(0, rows - 6)]),
         copies.start(norm.at[pl.ds(0, rows - 6)], norm_out.at[pl.ds(0, rows - 6)]),
-        copies.start(state_two.at[pl.ds(0, rows - 6)], state_out.at[pl.ds(0, rows - 6)]),
     ]
     convolve_two(rows - 6)
     last = pl.ds(rows - 6, 2)
@@ -656,7 +658,7 @@
     mate, cross, near = lax.optimization_barrier((mate, cross, near))
     near_edges = candidates((edges,), *near_ends)[0]
     ends, *halos = attend_ends(partners, near_ends[0], near_edges, mate, cross, queries[0])
-    edges, middles, halos, ends = lax.optimization_barrier((edges, middles, halos, ends))
+    halos, ends = lax.optimization_barrier((halos, ends))
     above = dict(zip(direct, halos[0::2]))
     below = dict(zip(direct, halos[1::2]))
     relay(above, views, True)

time: 63.6 us -> 63.6 us (level)
  no operation moved by 1% of the time
where the time goes in v7:
time: 63.6 us; the launch traced here: 63.3 us
  Pallas kernels  32.8 us (52%)
  starting transfers between devices  19.6 us (31%)
  waiting for transfers between devices  7.99 us (13%)
  local copies, waits for them, and re-layouts  2.39 us (4%)
    ppermute x2, starting transfers between devices, swap_bands(): lax.ppermute(cross, 'band', crosses)  10.9 us
    ppermute x8, starting transfers between devices, swap(): return lax.ppermute(cells, 'view', [(i, i ^ offset) for i in range(views)])  8.58 us
    pallas_call x1, Pallas kernels, attend_far(): pl.pallas_call(functools.partial(attend_far_body, low, len(candidates[0])...  6.75 us
    ppermute x8, waiting for transfers between devices, swap(): return lax.ppermute(cells, 'view', [(i, i ^ offset) for i in range(views)])  5.96 us
    pallas_call x1, Pallas kernels, middle_rows(): pl.pallas_call(middle_body, in_specs=[anywhere] * 4, out_specs=[anywhere]...  5.75 us
    pallas_call x1, Pallas kernels, edge_rows(): pl.pallas_call(edge_body, in_specs=[anywhere] + [in_vmem] * 2 + [anywhere...  4.7 us
    pallas_call x1, Pallas kernels, attend_near(): pl.pallas_call(functools.partial(attend_near_body, low, len(candidates[0]...  4.64 us
    pallas_call x1, Pallas kernels, attend_outer(): pl.pallas_call(functools.partial(attend_outer_body, low, len(sides[0])),...  3.92 us
  transfers between devices with their start and end apart: 12, of which 4 were waited for; matrix products, arithmetic and copies ran while one was open for 0% of the time, Pallas kernels for 37%

profile of v7, /device:TPU:1, one launch (start us, length us, event | category | flops | bytes accessed | tf_op | source)
XLA Modules:
  0.0 63.3 jit_solution(7149276007865847974)
XLA Ops:
  0.0 0.0 copy-start
  0.0 0.0 copy-start.9
  0.0 5.7 %residual_middle.1 = (bf16[2,512,128]{2,1,0:T(8,128)(2,1)}, bf16[2,512,128]{2,1,0:T(8,128)(2,1)}, f32[4,512,128]{2,1,0:T(8,128)}, f32[4,512,128]{2,1,0:T(8,128)}, bf16[4,512,128]{2,1,0:T(8,128)(2,1)}) custom-call(f32[8,512,128]{2,1,0:T(8,128)} %bitcast.12, bf16[3,3,128,128]{3,2,1,0:T(8,128)(2,1)} %one.3, bf16[3,3,128,128]{3,2,1,0:T(8,128)(2,1)} %two.3, ...), custom_call_target="tpu_custom_call" | custom-call | tf_op jit(solution)/shard_map/residual_middle/pallas_call | solution.py:185
  5.8 0.1 collective-permute-start
  5.9 4.6 %collective-permute-start.1 = (bf16[2,512,128]{2,1,0:T(8,128)(2,1)}, bf16[2,512,128]{2,1,0:T(8,128)(2,1)S(1)}, u32[]{:S(2)}, u32[]{:S(2)}) collective-permute-start(bf16[2,512,128]{2,1,0:T(8,128)(2,1)} %get-tuple-element.37), channel_id=1, source_target_pairs={{1,2},{3,4},{5,6},{2,1},{4,3},{6,5},{9,10},{11,12},{13,14},{10,9},... | collective-permute-start | bytes 786440 | tf_op jit(solution)/shard_map/ppermute | solution.py:623
  10.5 1.3 %collective-permute-start.5 = (bf16[4,512,128]{2,1,0:T(8,128)(2,1)}, bf16[4,512,128]{2,1,0:T(8,128)(2,1)S(1)}, u32[]{:S(2)}, u32[]{:S(2)}) collective-permute-start(bf16[4,512,128]{2,1,0:T(8,128)(2,1)} %get-tuple-element.40.refs_3_), channel_id=1, source_target_pairs={{0,16},{8,24},{16,0},{24,8},{1,17},{9,25},{17,1},{25,9},{2,18},{10... | collective-permute-start | bytes 1572872 | tf_op jit(solution)/shard_map/ppermute | solution.py:605
  11.8 1.2 %collective-permute-start.4 = (bf16[4,512,128]{2,1,0:T(8,128)(2,1)}, bf16[4,512,128]{2,1,0:T(8,128)(2,1)S(1)}, u32[]{:S(2)}, u32[]{:S(2)}) collective-permute-start(bf16[4,512,128]{2,1,0:T(8,128)(2,1)} %get-tuple-element.40.refs_3_), channel_id=1, source_target_pairs={{0,8},{8,0},{16,24},{24,16},{1,9},{9,1},{17,25},{25,17},{2,10},{10... | collective-permute-start | bytes 1572872 | tf_op jit(solution)/shard_map/ppermute | solution.py:605
  13.0 0.0 collective-permute-done.mate
  13.0 2.0 %collective-permute-done.1.cross = bf16[2,512,128]{2,1,0:T(8,128)(2,1)S(1)} collective-permute-done((bf16[2,512,128]{2,1,0:T(8,128)(2,1)}, bf16[2,512,128]{2,1,0:T(8,128)(2,1)S(1)}, u32[]{:S(2)}, u32[]{:S(2)}) %collective-permute-start.1) | collective-permute-done | bytes 262176 | tf_op jit(solution)/shard_map/ppermute | solution.py:623
  15.0 0.0 copy-done.2
  15.0 0.0 copy-done.1
  15.0 0.0 copy-done.9
  15.0 0.0 copy-start.3
  15.0 1.2 %copy-done.3 = f32[4,512,128]{2,1,0:T(8,128)S(1)} copy-done((f32[4,512,128]{2,1,0:T(8,128)S(1)}, f32[4,512,128]{2,1,0:T(8,128)}, u32[]{:S(2)}) %copy-start.3) | copy-done | bytes 1048600
  16.2 0.0 copy-start.8
  16.3 4.7 %residual_edge.1 = (f32[4,512,128]{2,1,0:T(8,128)S(1)}, bf16[4,512,128]{2,1,0:T(8,128)(2,1)}) custom-call(f32[8,512,128]{2,1,0:T(8,128)} %bitcast.13, bf16[2,512,128]{2,1,0:T(8,128)(2,1)S(1)} %collective-permute-done.mate, bf16[2,512,128]{2,1,0:T(8,128)(2,1)S(1)} %collective-permute-done.1.cross, bf16[3,3,128,128]{3,2,1,0:T(8,128)(2,1)S(1)} %copy-done.1, ...), custom_call_target="tpu_custom_call" | custom-call | tf_op jit(solution)/shard_map/residual_edge/pallas_call | solution.py:286
  21.0 1.8 %collective-permute-start.3 = (bf16[4,512,128]{2,1,0:T(8,128)(2,1)}, bf16[4,512,128]{2,1,0:T(8,128)(2,1)S(1)}, u32[]{:S(2)}, u32[]{:S(2)}) collective-permute-start(bf16[4,512,128]{2,1,0:T(8,128)(2,1)} %get-tuple-element.39.refs_2_), channel_id=1, source_target_pairs={{0,16},{8,24},{16,0},{24,8},{1,17},{9,25},{17,1},{25,9},{2,18},{10... | collective-permute-start | bytes 1572872 | tf_op jit(solution)/shard_map/ppermute | solution.py:605
  22.8 1.2 %collective-permute-start.2 = (bf16[4,512,128]{2,1,0:T(8,128)(2,1)}, bf16[4,512,128]{2,1,0:T(8,128)(2,1)S(1)}, u32[]{:S(2)}, u32[]{:S(2)}) collective-permute-start(bf16[4,512,128]{2,1,0:T(8,128)(2,1)} %get-tuple-element.39.refs_2_), channel_id=1, source_target_pairs={{0,8},{8,0},{16,24},{24,16},{1,9},{9,1},{17,25},{25,17},{2,10},{10... | collective-permute-start | bytes 1572872 | tf_op jit(solution)/shard_map/ppermute | solution.py:605
  24.0 0.0 copy-done.12
  24.0 0.1 copy.16.partners
  24.1 0.0 copy-done
  24.1 0.0 copy-done.11
  24.1 0.1 convolution_convert_fusion.refs_10_.refs_9_
  24.3 0.0 collective-permute-done.5.refs_1_.refs_3_.refs_2_
  24.3 1.7 %collective-permute-done.4.refs_0_.refs_2_ = bf16[4,512,128]{2,1,0:T(8,128)(2,1)S(1)} collective-permute-done((bf16[4,512,128]{2,1,0:T(8,128)(2,1)}, bf16[4,512,128]{2,1,0:T(8,128)(2,1)S(1)}, u32[]{:S(2)}, u32[]{:S(2)}) %collective-permute-start.4) | collective-permute-done | bytes 524320 | tf_op jit(solution)/shard_map/ppermute | solution.py:605
  26.0 0.0 copy-done.7
  26.0 1.0 %copy-done.5 = bf16[4,512,128]{2,1,0:T(8,128)(2,1)S(1)} copy-done((bf16[4,512,128]{2,1,0:T(8,128)(2,1)S(1)}, bf16[4,512,128]{2,1,0:T(8,128)(2,1)}, u32[]{:S(2)}) %copy-start.5) | copy-done | bytes 524312
  27.0 3.9 %attend_first.1 = (bf16[4,512,128]{2,1,0:T(8,128)(2,1)S(1)}, bf16[4,512,128]{2,1,0:T(8,128)(2,1)S(1)}, bf16[2,512,128]{2,1,0:T(8,128)(2,1)S(1)}) custom-call(s32[4,2]{1,0:T(4,128)S(1)} %copy.16.partners, bf16[4,512,128]{2,1,0:T(8,128)(2,1)S(1)} %collective-permute-done.4.refs_0_.refs_2_, ...), custom_call_target="tpu_custom_call" | custom-call | tf_op jit(solution)/shard_map/attend_first/pallas_call | solution.py:493
  30.9 2.5 %collective-permute-done.3.refs_1_.refs_0_ = bf16[4,512,128]{2,1,0:T(8,128)(2,1)S(1)} collective-permute-done((bf16[4,512,128]{2,1,0:T(8,128)(2,1)}, bf16[4,512,128]{2,1,0:T(8,128)(2,1)S(1)}, u32[]{:S(2)}, u32[]{:S(2)}) %collective-permute-start.3) | collective-permute-done | bytes 524320 | tf_op jit(solution)/shard_map/ppermute | solution.py:605
  33.5 1.7 %collective-permute-done.2.refs_0_ = bf16[4,512,128]{2,1,0:T(8,128)(2,1)S(1)} collective-permute-done((bf16[4,512,128]{2,1,0:T(8,128)(2,1)}, bf16[4,512,128]{2,1,0:T(8,128)(2,1)S(1)}, u32[]{:S(2)}, u32[]{:S(2)}) %collective-permute-start.2) | collective-permute-done | bytes 524320 | tf_op jit(solution)/shard_map/ppermute | solution.py:605
  35.2 1.2 %collective-permute-start.11 = (bf16[4,512,128]{2,1,0:T(8,128)(2,1)S(1)}, bf16[4,512,128]{2,1,0:T(8,128)(2,1)S(1)}, u32[]{:S(2)}, u32[]{:S(2)}) collective-permute-start(bf16[4,512,128]{2,1,0:T(8,128)(2,1)S(1)} %collective-permute-done.5.refs_1_.refs_3_.refs_2_), channel_id=1, source_target_pairs={{0,8},{8,0},{16,24},{24,16},{1,9},{9,1},{17,25},{25,17},{2,10},{10... | collective-permute-start | bytes 1572872 | tf_op jit(solution)/shard_map/ppermute | solution.py:605
  36.4 0.2 collective-permute-start.6
  36.6 0.1 edge_halos.1
  36.7 0.1 collective-permute-start.7
  36.8 0.0 copy-start.10
  36.8 6.3 %collective-permute-start.8 = (bf16[2,512,128]{2,1,0:T(8,128)(2,1)S(1)}, bf16[2,512,128]{2,1,0:T(8,128)(2,1)S(1)}, u32[]{:S(2)}, u32[]{:S(2)}) collective-permute-start(bf16[2,512,128]{2,1,0:T(8,128)(2,1)S(1)} %get-tuple-element.47), channel_id=1, source_target_pairs={{1,2},{3,4},{5,6},{2,1},{4,3},{6,5},{9,10},{11,12},{13,14},{10,9},... | collective-permute-start | bytes 786440 | tf_op jit(solution)/shard_map/ppermute | solution.py:623
  43.2 4.6 %attend_near.1.refs_6_ = bf16[4,512,128]{2,1,0:T(8,128)(2,1)S(1)} custom-call(s32[4,2]{1,0:T(4,128)S(1)} %copy.16.partners, bf16[4,512,128]{2,1,0:T(8,128)(2,1)S(1)} %collective-permute-done.2.refs_0_, bf16[4,512,128]{2,1,0:T(8,128)(2,1)S(1)} %collective-permute-done.3.refs_1_.refs_0_, bf16[4,512,128]{2,1,0:T(8,128)(2,1)S(1)} %collective-permute-done.4.refs_0_.refs_2_, ...), custom_call_target="tpu_custom_call" | custom-call | tf_op jit(solution)/shard_map/attend_near/pallas_call | solution.py:513
  47.8 0.0 collective-permute-done.7.refs_2_
  47.8 0.0 collective-permute-done.8.refs_3_
  47.8 3.0 %attend_ends.1 = (bf16[2,512,128]{2,1,0:T(8,128)(2,1)S(1)}, bf16[1,512,128]{2,1,0:T(8,128)(2,1)}, bf16[1,512,128]{2,1,0:T(8,128)(2,1)S(1)}, bf16[1,512,128]{2,1,0:T(8,128)(2,1)S(1)}, bf16[1,512,128]{2,1,0:T(8,128)(2,1)S(1)}) custom-call(s32[4,2]{1,0:T(4,128)S(1)} %copy.16.partners, bf16[4,512,128]{2,1,0:T(8,128)(2,1)S(1)} %collective-permute-done.2.refs_0_, ...), custom_call_target="tpu_custom_call" | custom-call | tf_op jit(solution)/shard_map/attend_ends/pallas_call | solution.py:549
  50.9 1.3 %collective-permute-start.10 = (bf16[1,512,128]{2,1,0:T(8,128)(2,1)S(1)}, bf16[1,512,128]{2,1,0:T(8,128)(2,1)S(1)}, u32[]{:S(2)}, u32[]{:S(2)}) collective-permute-start(bf16[1,512,128]{2,1,0:T(8,128)(2,1)S(1)} %get-tuple-element.60), channel_id=1, source_target_pairs={{0,16},{8,24},{16,0},{24,8},{1,17},{9,25},{17,1},{25,9},{2,18},{10... | collective-permute-start | bytes 393224 | tf_op jit(solution)/shard_map/ppermute | solution.py:605
  52.2 0.3 collective-permute-start.9
  52.4 0.0 collective-permute-done.11.refs_3_
  52.4 0.0 collective-permute-done.6.refs_1_
  52.4 6.8 %attend_far.1.refs_11_ = f32[6,512,128]{2,1,0:T(8,128)S(1)} custom-call(s32[4,2]{1,0:T(4,128)S(1)} %copy.16.partners, bf16[4,512,128]{2,1,0:T(8,128)(2,1)S(1)} %collective-permute-done.3.refs_1_.refs_0_, bf16[4,512,128]{2,1,0:T(8,128)(2,1)S(1)} %collective-permute-done.6.refs_1_, bf16[4,512,128]{2,1,0:T(8,128)(2,1)S(1)} %collective-permute-done.5.refs_1_.refs_3_.refs_2_, ...), custom_call_target="tpu_custom_call" | custom-call | tf_op jit(solution)/shard_map/attend_far/pallas_call | solution.py:530
  59.2 0.0 collective-permute-done.10.refs_5_
  59.2 0.0 collective-permute-done.9.refs_3_
  59.2 3.9 %attend_outer.1 = f32[8,512,128]{2,1,0:T(8,128)} custom-call(s32[4,2]{1,0:T(4,128)S(1)} %copy.16.partners, bf16[4,512,128]{2,1,0:T(8,128)(2,1)S(1)} %collective-permute-done.3.refs_1_.refs_0_, bf16[4,512,128]{2,1,0:T(8,128)(2,1)S(1)} %collective-permute-done.6.refs_1_, bf16[1,512,128]{2,1,0:T(8,128)(2,1)S(1)} %get-tuple-element.58.refs_2_, ...), custom_call_target="tpu_custom_call" | custom-call | tf_op jit(solution)/shard_map/attend_outer/pallas_call | solution.py:566
  (12 shorter events, 0.0 us)
Async XLA Ops:
  0.0 24.1 %copy-start = (bf16[128,128]{1,0:T(8,128)(2,1)S(1)}, bf16[128,128]{1,0:T(8,128)(2,1)}, u32[]{:S(2)}) copy-start(bf16[128,128]{1,0:T(8,128)(2,1)} %param.18) | copy-start | bytes 98308
  0.0 15.0 %copy-start.2 = (bf16[3,3,128,128]{3,2,1,0:T(8,128)(2,1)S(1)}, bf16[3,3,128,128]{3,2,1,0:T(8,128)(2,1)}, u32[]{:S(2)}) copy-start(bf16[3,3,128,128]{3,2,1,0:T(8,128)(2,1)} %two.3) | copy-start | bytes 884740
  0.0 15.0 %copy-start.1 = (bf16[3,3,128,128]{3,2,1,0:T(8,128)(2,1)S(1)}, bf16[3,3,128,128]{3,2,1,0:T(8,128)(2,1)}, u32[]{:S(2)}) copy-start(bf16[3,3,128,128]{3,2,1,0:T(8,128)(2,1)} %one.3) | copy-start | bytes 884740
  0.0 15.0 %copy-start.9 = (f32[128]{0:T(128)S(1)}, f32[128]{0:T(128)}, u32[]{:S(2)}) copy-start(f32[128]{0:T(128)} %param.20) | copy-start | bytes 1540
  5.8 7.2 %collective-permute-start = (bf16[2,512,128]{2,1,0:T(8,128)(2,1)}, bf16[2,512,128]{2,1,0:T(8,128)(2,1)S(1)}, u32[]{:S(2)}, u32[]{:S(2)}) collective-permute-start(bf16[2,512,128]{2,1,0:T(8,128)(2,1)} %get-tuple-element.36), channel_id=1, source_target_pairs={{0,1},{1,0},{2,3},{3,2},{4,5},{5,4},{6,7},{7,6},{8,9},{9,8},{10,11... | collective-permute-start | bytes 786440 | tf_op jit(solution)/shard_map/ppermute | solution.py:623
  5.9 9.1 %collective-permute-start.1 = (bf16[2,512,128]{2,1,0:T(8,128)(2,1)}, bf16[2,512,128]{2,1,0:T(8,128)(2,1)S(1)}, u32[]{:S(2)}, u32[]{:S(2)}) collective-permute-start(bf16[2,512,128]{2,1,0:T(8,128)(2,1)} %get-tuple-element.37), channel_id=1, source_target_pairs={{1,2},{3,4},{5,6},{2,1},{4,3},{6,5},{9,10},{11,12},{13,14},{10,9},... | collective-permute-start | bytes 786440 | tf_op jit(solution)/shard_map/ppermute | solution.py:623
  10.5 13.8 %collective-permute-start.5 = (bf16[4,512,128]{2,1,0:T(8,128)(2,1)}, bf16[4,512,128]{2,1,0:T(8,128)(2,1)S(1)}, u32[]{:S(2)}, u32[]{:S(2)}) collective-permute-start(bf16[4,512,128]{2,1,0:T(8,128)(2,1)} %get-tuple-element.40.refs_3_), channel_id=1, source_target_pairs={{0,16},{8,24},{16,0},{24,8},{1,17},{9,25},{17,1},{25,9},{2,18},{10... | collective-permute-start | bytes 1572872 | tf_op jit(solution)/shard_map/ppermute | solution.py:605
  11.8 14.2 %collective-permute-start.4 = (bf16[4,512,128]{2,1,0:T(8,128)(2,1)}, bf16[4,512,128]{2,1,0:T(8,128)(2,1)S(1)}, u32[]{:S(2)}, u32[]{:S(2)}) collective-permute-start(bf16[4,512,128]{2,1,0:T(8,128)(2,1)} %get-tuple-element.40.refs_3_), channel_id=1, source_target_pairs={{0,8},{8,0},{16,24},{24,16},{1,9},{9,1},{17,25},{25,17},{2,10},{10... | collective-permute-start | bytes 1572872 | tf_op jit(solution)/shard_map/ppermute | solution.py:605
  15.0 1.2 %copy-start.3 = (f32[4,512,128]{2,1,0:T(8,128)S(1)}, f32[4,512,128]{2,1,0:T(8,128)}, u32[]{:S(2)}) copy-start(f32[4,512,128]{2,1,0:T(8,128)} %get-tuple-element.38.state_one) | copy-start | bytes 3145732
  16.2 7.8 %copy-start.12 = (s32[4,2]{0,1:T(2,128)S(1)}, s32[4,2]{0,1:T(2,128)}, u32[]{:S(2)}) copy-start(s32[4,2]{0,1:T(2,128)} %param.13) | copy-start | bytes 100
  16.2 7.9 %copy-start.11 = (bf16[128,128]{1,0:T(8,128)(2,1)S(1)}, bf16[128,128]{1,0:T(8,128)(2,1)}, u32[]{:S(2)}) copy-start(bf16[128,128]{1,0:T(8,128)(2,1)} %param.19) | copy-start | bytes 98308
  16.2 9.7 %copy-start.6 = (bf16[128,128]{1,0:T(8,128)(2,1)S(1)}, bf16[128,128]{1,0:T(8,128)(2,1)}, u32[]{:S(2)}) copy-start(bf16[128,128]{1,0:T(8,128)(2,1)} %refs_4_.1) | copy-start | bytes 98308
  16.2 9.7 %copy-start.7 = (bf16[128,128]{1,0:T(8,128)(2,1)S(1)}, bf16[128,128]{1,0:T(8,128)(2,1)}, u32[]{:S(2)}) copy-start(bf16[128,128]{1,0:T(8,128)(2,1)} %refs_5_.1) | copy-start | bytes 98308
  16.2 9.7 %copy-start.8 = (f32[1,8,512]{2,1,0:T(8,128)S(1)}, f32[1,8,512]{2,1,0:T(8,128)}, u32[]{:S(2)}) copy-start(f32[1,8,512]{2,1,0:T(8,128)} %param.12) | copy-start | bytes 49156
  21.0 12.5 %collective-permute-start.3 = (bf16[4,512,128]{2,1,0:T(8,128)(2,1)}, bf16[4,512,128]{2,1,0:T(8,128)(2,1)S(1)}, u32[]{:S(2)}, u32[]{:S(2)}) collective-permute-start(bf16[4,512,128]{2,1,0:T(8,128)(2,1)} %get-tuple-element.39.refs_2_), channel_id=1, source_target_pairs={{0,16},{8,24},{16,0},{24,8},{1,17},{9,25},{17,1},{25,9},{2,18},{10... | collective-permute-start | bytes 1572872 | tf_op jit(solution)/shard_map/ppermute | solution.py:605
  22.8 12.4 %collective-permute-start.2 = (bf16[4,512,128]{2,1,0:T(8,128)(2,1)}, bf16[4,512,128]{2,1,0:T(8,128)(2,1)S(1)}, u32[]{:S(2)}, u32[]{:S(2)}) collective-permute-start(bf16[4,512,128]{2,1,0:T(8,128)(2,1)} %get-tuple-element.39.refs_2_), channel_id=1, source_target_pairs={{0,8},{8,0},{16,24},{24,16},{1,9},{9,1},{17,25},{25,17},{2,10},{10... | collective-permute-start | bytes 1572872 | tf_op jit(solution)/shard_map/ppermute | solution.py:605
  26.0 1.0 %copy-start.5 = (bf16[4,512,128]{2,1,0:T(8,128)(2,1)S(1)}, bf16[4,512,128]{2,1,0:T(8,128)(2,1)}, u32[]{:S(2)}) copy-start(bf16[4,512,128]{2,1,0:T(8,128)(2,1)} %get-tuple-element.40.refs_3_) | copy-start | bytes 1572868
  35.2 17.2 %collective-permute-start.11 = (bf16[4,512,128]{2,1,0:T(8,128)(2,1)S(1)}, bf16[4,512,128]{2,1,0:T(8,128)(2,1)S(1)}, u32[]{:S(2)}, u32[]{:S(2)}) collective-permute-start(bf16[4,512,128]{2,1,0:T(8,128)(2,1)S(1)} %collective-permute-done.5.refs_1_.refs_3_.refs_2_), channel_id=1, source_target_pairs={{0,8},{8,0},{16,24},{24,16},{1,9},{9,1},{17,25},{25,17},{2,10},{10... | collective-permute-start | bytes 1572872 | tf_op jit(solution)/shard_map/ppermute | solution.py:605
  36.4 16.0 %collective-permute-start.6 = (bf16[4,512,128]{2,1,0:T(8,128)(2,1)S(1)}, bf16[4,512,128]{2,1,0:T(8,128)(2,1)S(1)}, u32[]{:S(2)}, u32[]{:S(2)}) collective-permute-start(bf16[4,512,128]{2,1,0:T(8,128)(2,1)S(1)} %collective-permute-done.2.refs_0_), channel_id=1, source_target_pairs={{0,16},{8,24},{16,0},{24,8},{1,17},{9,25},{17,1},{25,9},{2,18},{10... | collective-permute-start | bytes 1572872 | tf_op jit(solution)/shard_map/ppermute | solution.py:605
  36.7 11.1 %collective-permute-start.7 = (bf16[2,512,128]{2,1,0:T(8,128)(2,1)S(1)}, bf16[2,512,128]{2,1,0:T(8,128)(2,1)S(1)}, u32[]{:S(2)}, u32[]{:S(2)}) collective-permute-start(bf16[2,512,128]{2,1,0:T(8,128)(2,1)S(1)} %get-tuple-element.46), channel_id=1, source_target_pairs={{0,1},{1,0},{2,3},{3,2},{4,5},{5,4},{6,7},{7,6},{8,9},{9,8},{10,11... | collective-permute-start | bytes 786440 | tf_op jit(solution)/shard_map/ppermute | solution.py:623
  36.8 15.6 %copy-start.4 = (f32[4,512,128]{2,1,0:T(8,128)S(1)}, f32[4,512,128]{2,1,0:T(8,128)}, u32[]{:S(2)}) copy-start(f32[4,512,128]{2,1,0:T(8,128)} %get-tuple-element.66.refs_9_) | copy-start | bytes 3145732
  36.8 15.6 %copy-start.10 = (f32[128]{0:T(128)S(1)}, f32[128]{0:T(128)}, u32[]{:S(2)}) copy-start(f32[128]{0:T(128)} %param.21) | copy-start | bytes 1540
  36.8 11.0 %collective-permute-start.8 = (bf16[2,512,128]{2,1,0:T(8,128)(2,1)S(1)}, bf16[2,512,128]{2,1,0:T(8,128)(2,1)S(1)}, u32[]{:S(2)}, u32[]{:S(2)}) collective-permute-start(bf16[2,512,128]{2,1,0:T(8,128)(2,1)S(1)} %get-tuple-element.47), channel_id=1, source_target_pairs={{1,2},{3,4},{5,6},{2,1},{4,3},{6,5},{9,10},{11,12},{13,14},{10,9},... | collective-permute-start | bytes 786440 | tf_op jit(solution)/shard_map/ppermute | solution.py:623
  50.9 8.3 %collective-permute-start.10 = (bf16[1,512,128]{2,1,0:T(8,128)(2,1)S(1)}, bf16[1,512,128]{2,1,0:T(8,128)(2,1)S(1)}, u32[]{:S(2)}, u32[]{:S(2)}) collective-permute-start(bf16[1,512,128]{2,1,0:T(8,128)(2,1)S(1)} %get-tuple-element.60), channel_id=1, source_target_pairs={{0,16},{8,24},{16,0},{24,8},{1,17},{9,25},{17,1},{25,9},{2,18},{10... | collective-permute-start | bytes 393224 | tf_op jit(solution)/shard_map/ppermute | solution.py:605
  52.2 7.1 %collective-permute-start.9 = (bf16[1,512,128]{2,1,0:T(8,128)(2,1)S(1)}, bf16[1,512,128]{2,1,0:T(8,128)(2,1)S(1)}, u32[]{:S(2)}, u32[]{:S(2)}) collective-permute-start(bf16[1,512,128]{2,1,0:T(8,128)(2,1)S(1)} %get-tuple-element.58.refs_2_), channel_id=1, source_target_pairs={{0,8},{8,0},{16,24},{24,16},{1,9},{9,1},{17,25},{25,17},{2,10},{10... | collective-permute-start | bytes 393224 | tf_op jit(solution)/shard_map/ppermute | solution.py:605

commit v8 on v7

--- a/solution.py
+++ b/solution.py
@@ -10,7 +10,7 @@
 
 epsilon = 1e-06
 vmem_bytes = 28 * 1024 * 1024
-edge_vmem_bytes = 50 * 1024 * 1024
+edge_vmem_bytes = 40 * 1024 * 1024
 whole_vmem_bytes = 56 * 1024 * 1024
 in_vmem = pl.BlockSpec(memory_space=pltpu.VMEM)
 in_smem = pl.BlockSpec(memory_space=pltpu.SMEM)
@@ -658,7 +658,7 @@
     mate, cross, near = lax.optimization_barrier((mate, cross, near))
     near_edges = candidates((edges,), *near_ends)[0]
     ends, *halos = attend_ends(partners, near_ends[0], near_edges, mate, cross, queries[0])
-    halos, ends = lax.optimization_barrier((halos, ends))
+    edges, middles, halos, ends = lax.optimization_barrier((edges, middles, halos, ends))
     above = dict(zip(direct, halos[0::2]))
     below = dict(zip(direct, halos[1::2]))
     relay(above, views, True)

time: 63.6 us -> 63.7 us (level)
  waiting for transfers between devices: 7.99 us -> 8.97 us
  Pallas kernels: 32.8 us -> 31.9 us
    ppermute x8, waiting for transfers between devices: 5.96 us -> 6.94 us  [swap(): return lax.ppermute(cells, 'view', [(i, i ^ offset) for i in range(views)])]
    pallas_call x1, Pallas kernels: 4.7 us -> 3.75 us  [edge_rows(): pl.pallas_call(edge_body, in_specs=[anywhere] + [in_vmem] * 2 + [anywhere...]
    unnamed x27 -> x29, local copies, waits for them, and re-layouts: 2.39 us -> 2.4 us
  transfers between devices with their start and end apart: 12 -> 12, of which waited for: 4 -> 5; matrix products, arithmetic and copies ran while one was open for 0% -> 0% of each run, Pallas kernels for 37% -> 35%
where the time goes in v8:
time: 63.7 us; the launch traced here: 63.4 us
  Pallas kernels  31.9 us (50%)
  starting transfers between devices  19.6 us (31%)
  waiting for transfers between devices  8.97 us (14%)
  local copies, waits for them, and re-layouts  2.4 us (4%)
    ppermute x2, starting transfers between devices, swap_bands(): lax.ppermute(cross, 'band', crosses)  10.9 us
    ppermute x8, starting transfers between devices, swap(): return lax.ppermute(cells, 'view', [(i, i ^ offset) for i in range(views)])  8.54 us
    ppermute x8, waiting for transfers between devices, swap(): return lax.ppermute(cells, 'view', [(i, i ^ offset) for i in range(views)])  6.94 us
    pallas_call x1, Pallas kernels, attend_far(): pl.pallas_call(functools.partial(attend_far_body, low, len(candidates[0])...  6.75 us
    pallas_call x1, Pallas kernels, middle_rows(): pl.pallas_call(middle_body, in_specs=[anywhere] * 4, out_specs=[anywhere]...  5.82 us
    pallas_call x1, Pallas kernels, attend_near(): pl.pallas_call(functools.partial(attend_near_body, low, len(candidates[0]...  4.64 us
    pallas_call x1, Pallas kernels, attend_outer(): pl.pallas_call(functools.partial(attend_outer_body, low, len(sides[0])),...  3.92 us
    pallas_call x1, Pallas kernels, attend_first(): pl.pallas_call(functools.partial(attend_first_body, low, len(middles)), i...  3.91 us
  transfers between devices with their start and end apart: 12, of which 5 were waited for; matrix products, arithmetic and copies ran while one was open for 0% of the time, Pallas kernels for 35%

profile of v8, /device:TPU:1, one launch (start us, length us, event | category | flops | bytes accessed | tf_op | source)
XLA Modules:
  0.0 63.4 jit_solution(15520640841430162569)
XLA Ops:
  0.0 0.0 copy-start
  0.0 0.0 copy-start.10
  0.0 0.0 copy-start.1
  0.0 5.8 %residual_middle.1 = (bf16[2,512,128]{2,1,0:T(8,128)(2,1)}, bf16[2,512,128]{2,1,0:T(8,128)(2,1)}, f32[4,512,128]{2,1,0:T(8,128)}, f32[4,512,128]{2,1,0:T(8,128)}, bf16[4,512,128]{2,1,0:T(8,128)(2,1)}) custom-call(f32[8,512,128]{2,1,0:T(8,128)} %bitcast.7, bf16[3,3,128,128]{3,2,1,0:T(8,128)(2,1)} %one.3, bf16[3,3,128,128]{3,2,1,0:T(8,128)(2,1)} %two.3, ...), custom_call_target="tpu_custom_call" | custom-call | tf_op jit(solution)/shard_map/residual_middle/pallas_call | solution.py:185
  5.9 0.1 collective-permute-start
  6.0 4.5 %collective-permute-start.1 = (bf16[2,512,128]{2,1,0:T(8,128)(2,1)}, bf16[2,512,128]{2,1,0:T(8,128)(2,1)S(1)}, u32[]{:S(2)}, u32[]{:S(2)}) collective-permute-start(bf16[2,512,128]{2,1,0:T(8,128)(2,1)} %get-tuple-element.41), channel_id=1, source_target_pairs={{1,2},{3,4},{5,6},{2,1},{4,3},{6,5},{9,10},{11,12},{13,14},{10,9},... | collective-permute-start | bytes 786440 | tf_op jit(solution)/shard_map/ppermute | solution.py:623
  10.5 1.3 %collective-permute-start.5 = (bf16[4,512,128]{2,1,0:T(8,128)(2,1)}, bf16[4,512,128]{2,1,0:T(8,128)(2,1)S(1)}, u32[]{:S(2)}, u32[]{:S(2)}) collective-permute-start(bf16[4,512,128]{2,1,0:T(8,128)(2,1)} %get-tuple-element.44.refs_3_), channel_id=1, source_target_pairs={{0,16},{8,24},{16,0},{24,8},{1,17},{9,25},{17,1},{25,9},{2,18},{10... | collective-permute-start | bytes 1572872 | tf_op jit(solution)/shard_map/ppermute | solution.py:605
  11.8 1.2 %collective-permute-start.4 = (bf16[4,512,128]{2,1,0:T(8,128)(2,1)}, bf16[4,512,128]{2,1,0:T(8,128)(2,1)S(1)}, u32[]{:S(2)}, u32[]{:S(2)}) collective-permute-start(bf16[4,512,128]{2,1,0:T(8,128)(2,1)} %get-tuple-element.44.refs_3_), channel_id=1, source_target_pairs={{0,8},{8,0},{16,24},{24,16},{1,9},{9,1},{17,25},{25,17},{2,10},{10... | collective-permute-start | bytes 1572872 | tf_op jit(solution)/shard_map/ppermute | solution.py:605
  13.1 0.0 collective-permute-done.mate
  13.1 2.0 %collective-permute-done.1.cross = bf16[2,512,128]{2,1,0:T(8,128)(2,1)S(1)} collective-permute-done((bf16[2,512,128]{2,1,0:T(8,128)(2,1)}, bf16[2,512,128]{2,1,0:T(8,128)(2,1)S(1)}, u32[]{:S(2)}, u32[]{:S(2)}) %collective-permute-start.1) | collective-permute-done | bytes 262176 | tf_op jit(solution)/shard_map/ppermute | solution.py:623
  15.1 0.0 copy-done.3
  15.1 0.0 copy-done.10
  15.1 0.0 copy-done.1
  15.1 0.0 copy-start.4
  15.1 1.2 %copy-done.4 = f32[4,512,128]{2,1,0:T(8,128)S(1)} copy-done((f32[4,512,128]{2,1,0:T(8,128)S(1)}, f32[4,512,128]{2,1,0:T(8,128)}, u32[]{:S(2)}) %copy-start.4) | copy-done | bytes 1048600
  16.4 0.0 copy-start.9
  16.4 3.7 %residual_edge.1 = (f32[4,512,128]{2,1,0:T(8,128)S(1)}, bf16[4,512,128]{2,1,0:T(8,128)(2,1)}) custom-call(f32[8,512,128]{2,1,0:T(8,128)S(1)} %bitcast.8, bf16[2,512,128]{2,1,0:T(8,128)(2,1)S(1)} %collective-permute-done.mate, bf16[2,512,128]{2,1,0:T(8,128)(2,1)S(1)} %collective-permute-done.1.cross, bf16[3,3,128,128]{3,2,1,0:T(8,128)(2,1)S(1)} %copy-done.2, ...), custom_call_target="tpu_custom_call" | custom-call | tf_op jit(solution)/shard_map/residual_edge/pallas_call | solution.py:286
  20.1 1.8 %collective-permute-start.3 = (bf16[4,512,128]{2,1,0:T(8,128)(2,1)}, bf16[4,512,128]{2,1,0:T(8,128)(2,1)S(1)}, u32[]{:S(2)}, u32[]{:S(2)}) collective-permute-start(bf16[4,512,128]{2,1,0:T(8,128)(2,1)} %get-tuple-element.43.refs_2_), channel_id=1, source_target_pairs={{0,16},{8,24},{16,0},{24,8},{1,17},{9,25},{17,1},{25,9},{2,18},{10... | collective-permute-start | bytes 1572872 | tf_op jit(solution)/shard_map/ppermute | solution.py:605
  22.0 1.2 %collective-permute-start.2 = (bf16[4,512,128]{2,1,0:T(8,128)(2,1)}, bf16[4,512,128]{2,1,0:T(8,128)(2,1)S(1)}, u32[]{:S(2)}, u32[]{:S(2)}) collective-permute-start(bf16[4,512,128]{2,1,0:T(8,128)(2,1)} %get-tuple-element.43.refs_2_), channel_id=1, source_target_pairs={{0,8},{8,0},{16,24},{24,16},{1,9},{9,1},{17,25},{25,17},{2,10},{10... | collective-permute-start | bytes 1572872 | tf_op jit(solution)/shard_map/ppermute | solution.py:605
  23.2 0.1 copy.16.partners
  23.3 0.0 copy-done
  23.3 0.1 convolution_convert_fusion.refs_10_.refs_9_
  23.4 1.4 %collective-permute-done.5.refs_1_.refs_3_.refs_2_ = bf16[4,512,128]{2,1,0:T(8,128)(2,1)S(1)} collective-permute-done((bf16[4,512,128]{2,1,0:T(8,128)(2,1)}, bf16[4,512,128]{2,1,0:T(8,128)(2,1)S(1)}, u32[]{:S(2)}, u32[]{:S(2)}) %collective-permute-start.5) | collective-permute-done | bytes 524320 | tf_op jit(solution)/shard_map/ppermute | solution.py:605
  24.8 1.2 %collective-permute-done.4.refs_0_.refs_2_ = bf16[4,512,128]{2,1,0:T(8,128)(2,1)S(1)} collective-permute-done((bf16[4,512,128]{2,1,0:T(8,128)(2,1)}, bf16[4,512,128]{2,1,0:T(8,128)(2,1)S(1)}, u32[]{:S(2)}, u32[]{:S(2)}) %collective-permute-start.4) | collective-permute-done | bytes 524320 | tf_op jit(solution)/shard_map/ppermute | solution.py:605
  26.1 0.0 copy-done.7
  26.1 0.0 copy-done.9
  26.1 1.0 %copy-done.6 = bf16[4,512,128]{2,1,0:T(8,128)(2,1)S(1)} copy-done((bf16[4,512,128]{2,1,0:T(8,128)(2,1)S(1)}, bf16[4,512,128]{2,1,0:T(8,128)(2,1)}, u32[]{:S(2)}) %copy-start.6) | copy-done | bytes 524312
  27.1 3.9 %attend_first.1 = (bf16[4,512,128]{2,1,0:T(8,128)(2,1)S(1)}, bf16[4,512,128]{2,1,0:T(8,128)(2,1)S(1)}, bf16[2,512,128]{2,1,0:T(8,128)(2,1)S(1)}) custom-call(s32[4,2]{1,0:T(4,128)S(1)} %copy.16.partners, bf16[4,512,128]{2,1,0:T(8,128)(2,1)S(1)} %collective-permute-done.4.refs_0_.refs_2_, ...), custom_call_target="tpu_custom_call" | custom-call | tf_op jit(solution)/shard_map/attend_first/pallas_call | solution.py:493
  31.0 2.5 %collective-permute-done.3.refs_1_.refs_0_ = bf16[4,512,128]{2,1,0:T(8,128)(2,1)S(1)} collective-permute-done((bf16[4,512,128]{2,1,0:T(8,128)(2,1)}, bf16[4,512,128]{2,1,0:T(8,128)(2,1)S(1)}, u32[]{:S(2)}, u32[]{:S(2)}) %collective-permute-start.3) | collective-permute-done | bytes 524320 | tf_op jit(solution)/shard_map/ppermute | solution.py:605
  33.6 1.7 %collective-permute-done.2.refs_0_ = bf16[4,512,128]{2,1,0:T(8,128)(2,1)S(1)} collective-permute-done((bf16[4,512,128]{2,1,0:T(8,128)(2,1)}, bf16[4,512,128]{2,1,0:T(8,128)(2,1)S(1)}, u32[]{:S(2)}, u32[]{:S(2)}) %collective-permute-start.2) | collective-permute-done | bytes 524320 | tf_op jit(solution)/shard_map/ppermute | solution.py:605
  35.3 1.2 %collective-permute-start.7 = (bf16[4,512,128]{2,1,0:T(8,128)(2,1)S(1)}, bf16[4,512,128]{2,1,0:T(8,128)(2,1)S(1)}, u32[]{:S(2)}, u32[]{:S(2)}) collective-permute-start(bf16[4,512,128]{2,1,0:T(8,128)(2,1)S(1)} %collective-permute-done.5.refs_1_.refs_3_.refs_2_), channel_id=1, source_target_pairs={{0,8},{8,0},{16,24},{24,16},{1,9},{9,1},{17,25},{25,17},{2,10},{10... | collective-permute-start | bytes 1572872 | tf_op jit(solution)/shard_map/ppermute | solution.py:605
  36.5 0.2 collective-permute-start.6
  36.7 0.1 edge_halos.1
  36.8 0.1 collective-permute-start.8
  36.9 0.0 copy-start.11
  36.9 6.3 %collective-permute-start.9 = (bf16[2,512,128]{2,1,0:T(8,128)(2,1)S(1)}, bf16[2,512,128]{2,1,0:T(8,128)(2,1)S(1)}, u32[]{:S(2)}, u32[]{:S(2)}) collective-permute-start(bf16[2,512,128]{2,1,0:T(8,128)(2,1)S(1)} %get-tuple-element.53), channel_id=1, source_target_pairs={{1,2},{3,4},{5,6},{2,1},{4,3},{6,5},{9,10},{11,12},{13,14},{10,9},... | collective-permute-start | bytes 786440 | tf_op jit(solution)/shard_map/ppermute | solution.py:623
  43.3 4.6 %attend_near.1.refs_6_ = bf16[4,512,128]{2,1,0:T(8,128)(2,1)S(1)} custom-call(s32[4,2]{1,0:T(4,128)S(1)} %copy.16.partners, bf16[4,512,128]{2,1,0:T(8,128)(2,1)S(1)} %collective-permute-done.2.refs_0_, bf16[4,512,128]{2,1,0:T(8,128)(2,1)S(1)} %collective-permute-done.3.refs_1_.refs_0_, bf16[4,512,128]{2,1,0:T(8,128)(2,1)S(1)} %collective-permute-done.4.refs_0_.refs_2_, ...), custom_call_target="tpu_custom_call" | custom-call | tf_op jit(solution)/shard_map/attend_near/pallas_call | solution.py:513
  47.9 0.0 collective-permute-done.8.refs_2_
  47.9 0.0 collective-permute-done.9.refs_3_
  47.9 3.0 %attend_ends.1 = (bf16[2,512,128]{2,1,0:T(8,128)(2,1)S(1)}, bf16[1,512,128]{2,1,0:T(8,128)(2,1)}, bf16[1,512,128]{2,1,0:T(8,128)(2,1)S(1)}, bf16[1,512,128]{2,1,0:T(8,128)(2,1)S(1)}, bf16[1,512,128]{2,1,0:T(8,128)(2,1)S(1)}) custom-call(s32[4,2]{1,0:T(4,128)S(1)} %copy.16.partners, bf16[4,512,128]{2,1,0:T(8,128)(2,1)S(1)} %collective-permute-done.2.refs_0_, ...), custom_call_target="tpu_custom_call" | custom-call | tf_op jit(solution)/shard_map/attend_ends/pallas_call | solution.py:549
  50.9 0.0 collective-permute-done.7.refs_3_
  51.0 0.0 collective-permute-done.6.refs_1_
  51.0 1.3 %collective-permute-start.11 = (bf16[1,512,128]{2,1,0:T(8,128)(2,1)S(1)}, bf16[1,512,128]{2,1,0:T(8,128)(2,1)S(1)}, u32[]{:S(2)}, u32[]{:S(2)}) collective-permute-start(bf16[1,512,128]{2,1,0:T(8,128)(2,1)S(1)} %get-tuple-element.66), channel_id=1, source_target_pairs={{0,16},{8,24},{16,0},{24,8},{1,17},{9,25},{17,1},{25,9},{2,18},{10... | collective-permute-start | bytes 393224 | tf_op jit(solution)/shard_map/ppermute | solution.py:605
  52.3 0.2 collective-permute-start.10
  52.5 6.8 %attend_far.1.refs_11_ = f32[6,512,128]{2,1,0:T(8,128)S(1)} custom-call(s32[4,2]{1,0:T(4,128)S(1)} %copy.16.partners, bf16[4,512,128]{2,1,0:T(8,128)(2,1)S(1)} %collective-permute-done.3.refs_1_.refs_0_, bf16[4,512,128]{2,1,0:T(8,128)(2,1)S(1)} %collective-permute-done.6.refs_1_, bf16[4,512,128]{2,1,0:T(8,128)(2,1)S(1)} %collective-permute-done.5.refs_1_.refs_3_.refs_2_, ...), custom_call_target="tpu_custom_call" | custom-call | tf_op jit(solution)/shard_map/attend_far/pallas_call | solution.py:530
  59.3 0.0 collective-permute-done.11.refs_5_
  59.3 0.0 collective-permute-done.10.refs_3_
  59.3 3.9 %attend_outer.1 = f32[8,512,128]{2,1,0:T(8,128)} custom-call(s32[4,2]{1,0:T(4,128)S(1)} %copy.16.partners, bf16[4,512,128]{2,1,0:T(8,128)(2,1)S(1)} %collective-permute-done.3.refs_1_.refs_0_, bf16[4,512,128]{2,1,0:T(8,128)(2,1)S(1)} %collective-permute-done.6.refs_1_, bf16[1,512,128]{2,1,0:T(8,128)(2,1)S(1)} %get-tuple-element.64.refs_2_, ...), custom_call_target="tpu_custom_call" | custom-call | tf_op jit(solution)/shard_map/attend_outer/pallas_call | solution.py:566
  (14 shorter events, 0.0 us)
Async XLA Ops:
  0.0 23.3 %copy-start = (bf16[128,128]{1,0:T(8,128)(2,1)S(1)}, bf16[128,128]{1,0:T(8,128)(2,1)}, u32[]{:S(2)}) copy-start(bf16[128,128]{1,0:T(8,128)(2,1)} %param.18) | copy-start | bytes 98308
  0.0 15.1 %copy-start.3 = (bf16[3,3,128,128]{3,2,1,0:T(8,128)(2,1)S(1)}, bf16[3,3,128,128]{3,2,1,0:T(8,128)(2,1)}, u32[]{:S(2)}) copy-start(bf16[3,3,128,128]{3,2,1,0:T(8,128)(2,1)} %two.3) | copy-start | bytes 884740
  0.0 15.1 %copy-start.2 = (bf16[3,3,128,128]{3,2,1,0:T(8,128)(2,1)S(1)}, bf16[3,3,128,128]{3,2,1,0:T(8,128)(2,1)}, u32[]{:S(2)}) copy-start(bf16[3,3,128,128]{3,2,1,0:T(8,128)(2,1)} %one.3) | copy-start | bytes 884740
  0.0 15.1 %copy-start.10 = (f32[128]{0:T(128)S(1)}, f32[128]{0:T(128)}, u32[]{:S(2)}) copy-start(f32[128]{0:T(128)} %param.20) | copy-start | bytes 1540
  0.0 15.1 %copy-start.1 = (f32[1,8,512,128]{3,2,1,0:T(8,128)S(1)}, f32[1,8,512,128]{3,2,1,0:T(8,128)}, u32[]{:S(2)}) copy-start(f32[1,8,512,128]{3,2,1,0:T(8,128)} %param.11) | copy-start | bytes 6291460
  5.9 7.2 %collective-permute-start = (bf16[2,512,128]{2,1,0:T(8,128)(2,1)}, bf16[2,512,128]{2,1,0:T(8,128)(2,1)S(1)}, u32[]{:S(2)}, u32[]{:S(2)}) collective-permute-start(bf16[2,512,128]{2,1,0:T(8,128)(2,1)} %get-tuple-element.40), channel_id=1, source_target_pairs={{0,1},{1,0},{2,3},{3,2},{4,5},{5,4},{6,7},{7,6},{8,9},{9,8},{10,11... | collective-permute-start | bytes 786440 | tf_op jit(solution)/shard_map/ppermute | solution.py:623
  6.0 9.1 %collective-permute-start.1 = (bf16[2,512,128]{2,1,0:T(8,128)(2,1)}, bf16[2,512,128]{2,1,0:T(8,128)(2,1)S(1)}, u32[]{:S(2)}, u32[]{:S(2)}) collective-permute-start(bf16[2,512,128]{2,1,0:T(8,128)(2,1)} %get-tuple-element.41), channel_id=1, source_target_pairs={{1,2},{3,4},{5,6},{2,1},{4,3},{6,5},{9,10},{11,12},{13,14},{10,9},... | collective-permute-start | bytes 786440 | tf_op jit(solution)/shard_map/ppermute | solution.py:623
  10.5 14.3 %collective-permute-start.5 = (bf16[4,512,128]{2,1,0:T(8,128)(2,1)}, bf16[4,512,128]{2,1,0:T(8,128)(2,1)S(1)}, u32[]{:S(2)}, u32[]{:S(2)}) collective-permute-start(bf16[4,512,128]{2,1,0:T(8,128)(2,1)} %get-tuple-element.44.refs_3_), channel_id=1, source_target_pairs={{0,16},{8,24},{16,0},{24,8},{1,17},{9,25},{17,1},{25,9},{2,18},{10... | collective-permute-start | bytes 1572872 | tf_op jit(solution)/shard_map/ppermute | solution.py:605
  11.8 14.2 %collective-permute-start.4 = (bf16[4,512,128]{2,1,0:T(8,128)(2,1)}, bf16[4,512,128]{2,1,0:T(8,128)(2,1)S(1)}, u32[]{:S(2)}, u32[]{:S(2)}) collective-permute-start(bf16[4,512,128]{2,1,0:T(8,128)(2,1)} %get-tuple-element.44.refs_3_), channel_id=1, source_target_pairs={{0,8},{8,0},{16,24},{24,16},{1,9},{9,1},{17,25},{25,17},{2,10},{10... | collective-permute-start | bytes 1572872 | tf_op jit(solution)/shard_map/ppermute | solution.py:605
  15.1 1.2 %copy-start.4 = (f32[4,512,128]{2,1,0:T(8,128)S(1)}, f32[4,512,128]{2,1,0:T(8,128)}, u32[]{:S(2)}) copy-start(f32[4,512,128]{2,1,0:T(8,128)} %get-tuple-element.42.state_one) | copy-start | bytes 3145732
  16.3 6.8 %copy-start.13 = (s32[4,2]{0,1:T(2,128)S(1)}, s32[4,2]{0,1:T(2,128)}, u32[]{:S(2)}) copy-start(s32[4,2]{0,1:T(2,128)} %param.13) | copy-start | bytes 100
  16.3 6.9 %copy-start.12 = (bf16[128,128]{1,0:T(8,128)(2,1)S(1)}, bf16[128,128]{1,0:T(8,128)(2,1)}, u32[]{:S(2)}) copy-start(bf16[128,128]{1,0:T(8,128)(2,1)} %param.19) | copy-start | bytes 98308
  16.3 9.7 %copy-start.7 = (bf16[128,128]{1,0:T(8,128)(2,1)S(1)}, bf16[128,128]{1,0:T(8,128)(2,1)}, u32[]{:S(2)}) copy-start(bf16[128,128]{1,0:T(8,128)(2,1)} %refs_4_.1) | copy-start | bytes 98308
  16.3 9.7 %copy-start.8 = (bf16[128,128]{1,0:T(8,128)(2,1)S(1)}, bf16[128,128]{1,0:T(8,128)(2,1)}, u32[]{:S(2)}) copy-start(bf16[128,128]{1,0:T(8,128)(2,1)} %refs_5_.1) | copy-start | bytes 98308
  16.4 9.7 %copy-start.9 = (f32[1,8,512]{2,1,0:T(8,128)S(1)}, f32[1,8,512]{2,1,0:T(8,128)}, u32[]{:S(2)}) copy-start(f32[1,8,512]{2,1,0:T(8,128)} %param.12) | copy-start | bytes 49156
  20.1 13.4 %collective-permute-start.3 = (bf16[4,512,128]{2,1,0:T(8,128)(2,1)}, bf16[4,512,128]{2,1,0:T(8,128)(2,1)S(1)}, u32[]{:S(2)}, u32[]{:S(2)}) collective-permute-start(bf16[4,512,128]{2,1,0:T(8,128)(2,1)} %get-tuple-element.43.refs_2_), channel_id=1, source_target_pairs={{0,16},{8,24},{16,0},{24,8},{1,17},{9,25},{17,1},{25,9},{2,18},{10... | collective-permute-start | bytes 1572872 | tf_op jit(solution)/shard_map/ppermute | solution.py:605
  22.0 13.3 %collective-permute-start.2 = (bf16[4,512,128]{2,1,0:T(8,128)(2,1)}, bf16[4,512,128]{2,1,0:T(8,128)(2,1)S(1)}, u32[]{:S(2)}, u32[]{:S(2)}) collective-permute-start(bf16[4,512,128]{2,1,0:T(8,128)(2,1)} %get-tuple-element.43.refs_2_), channel_id=1, source_target_pairs={{0,8},{8,0},{16,24},{24,16},{1,9},{9,1},{17,25},{25,17},{2,10},{10... | collective-permute-start | bytes 1572872 | tf_op jit(solution)/shard_map/ppermute | solution.py:605
  26.1 1.0 %copy-start.6 = (bf16[4,512,128]{2,1,0:T(8,128)(2,1)S(1)}, bf16[4,512,128]{2,1,0:T(8,128)(2,1)}, u32[]{:S(2)}) copy-start(bf16[4,512,128]{2,1,0:T(8,128)(2,1)} %get-tuple-element.44.refs_3_) | copy-start | bytes 1572868
  35.3 15.7 %collective-permute-start.7 = (bf16[4,512,128]{2,1,0:T(8,128)(2,1)S(1)}, bf16[4,512,128]{2,1,0:T(8,128)(2,1)S(1)}, u32[]{:S(2)}, u32[]{:S(2)}) collective-permute-start(bf16[4,512,128]{2,1,0:T(8,128)(2,1)S(1)} %collective-permute-done.5.refs_1_.refs_3_.refs_2_), channel_id=1, source_target_pairs={{0,8},{8,0},{16,24},{24,16},{1,9},{9,1},{17,25},{25,17},{2,10},{10... | collective-permute-start | bytes 1572872 | tf_op jit(solution)/shard_map/ppermute | solution.py:605
  36.5 14.5 %collective-permute-start.6 = (bf16[4,512,128]{2,1,0:T(8,128)(2,1)S(1)}, bf16[4,512,128]{2,1,0:T(8,128)(2,1)S(1)}, u32[]{:S(2)}, u32[]{:S(2)}) collective-permute-start(bf16[4,512,128]{2,1,0:T(8,128)(2,1)S(1)} %collective-permute-done.2.refs_0_), channel_id=1, source_target_pairs={{0,16},{8,24},{16,0},{24,8},{1,17},{9,25},{17,1},{25,9},{2,18},{10... | collective-permute-start | bytes 1572872 | tf_op jit(solution)/shard_map/ppermute | solution.py:605
  36.8 11.1 %collective-permute-start.8 = (bf16[2,512,128]{2,1,0:T(8,128)(2,1)S(1)}, bf16[2,512,128]{2,1,0:T(8,128)(2,1)S(1)}, u32[]{:S(2)}, u32[]{:S(2)}) collective-permute-start(bf16[2,512,128]{2,1,0:T(8,128)(2,1)S(1)} %get-tuple-element.52), channel_id=1, source_target_pairs={{0,1},{1,0},{2,3},{3,2},{4,5},{5,4},{6,7},{7,6},{8,9},{9,8},{10,11... | collective-permute-start | bytes 786440 | tf_op jit(solution)/shard_map/ppermute | solution.py:623
  36.9 15.6 %copy-start.5 = (f32[4,512,128]{2,1,0:T(8,128)S(1)}, f32[4,512,128]{2,1,0:T(8,128)}, u32[]{:S(2)}) copy-start(f32[4,512,128]{2,1,0:T(8,128)} %get-tuple-element.74.refs_9_) | copy-start | bytes 3145732
  36.9 15.6 %copy-start.11 = (f32[128]{0:T(128)S(1)}, f32[128]{0:T(128)}, u32[]{:S(2)}) copy-start(f32[128]{0:T(128)} %param.21) | copy-start | bytes 1540
  36.9 11.0 %collective-permute-start.9 = (bf16[2,512,128]{2,1,0:T(8,128)(2,1)S(1)}, bf16[2,512,128]{2,1,0:T(8,128)(2,1)S(1)}, u32[]{:S(2)}, u32[]{:S(2)}) collective-permute-start(bf16[2,512,128]{2,1,0:T(8,128)(2,1)S(1)} %get-tuple-element.53), channel_id=1, source_target_pairs={{1,2},{3,4},{5,6},{2,1},{4,3},{6,5},{9,10},{11,12},{13,14},{10,9},... | collective-permute-start | bytes 786440 | tf_op jit(solution)/shard_map/ppermute | solution.py:623
  51.0 8.3 %collective-permute-start.11 = (bf16[1,512,128]{2,1,0:T(8,128)(2,1)S(1)}, bf16[1,512,128]{2,1,0:T(8,128)(2,1)S(1)}, u32[]{:S(2)}, u32[]{:S(2)}) collective-permute-start(bf16[1,512,128]{2,1,0:T(8,128)(2,1)S(1)} %get-tuple-element.66), channel_id=1, source_target_pairs={{0,16},{8,24},{16,0},{24,8},{1,17},{9,25},{17,1},{25,9},{2,18},{10... | collective-permute-start | bytes 393224 | tf_op jit(solution)/shard_map/ppermute | solution.py:605
  52.3 7.0 %collective-permute-start.10 = (bf16[1,512,128]{2,1,0:T(8,128)(2,1)S(1)}, bf16[1,512,128]{2,1,0:T(8,128)(2,1)S(1)}, u32[]{:S(2)}, u32[]{:S(2)}) collective-permute-start(bf16[1,512,128]{2,1,0:T(8,128)(2,1)S(1)} %get-tuple-element.64.refs_2_), channel_id=1, source_target_pairs={{0,8},{8,0},{16,24},{24,16},{1,9},{9,1},{17,25},{25,17},{2,10},{10... | collective-permute-start | bytes 393224 | tf_op jit(solution)/shard_map/ppermute | solution.py:605
